TPU v7x, 32 devices: a whole 2x2x4 slice. The times are simulated.
32 devices in a mesh: dp: 4 (over z), seq: 8 (over y, x, core).
Axes of the slice: x: 2, y: 2, z: 4, core: 2. Of those that a mesh axis runs over, the one named last changes fastest.
Arguments:
- hidden_in: bfloat16 [4, 1024, 2048], P('dp', 'seq'), may hold values from -6 to 6
- segments: int32 [4, 1024], P('dp', 'seq'), may hold values from 0 to 254, as said below
- attn_weights: bfloat16 [2048, 8192], P(('dp', 'seq')), may hold values from -0.125 to 0.125
- q_gain: bfloat16 [2048], P(('dp', 'seq')), may hold values from 0.25 to 1.75
- k_gain: bfloat16 [2048], P(('dp', 'seq')), may hold values from 0.25 to 1.75
- attn_gain: bfloat16 [2048], P(('dp', 'seq')), may hold values from 0.25 to 1.75
- ffn_gain: bfloat16 [2048], P(('dp', 'seq')), may hold values from 0.25 to 1.75
- gate_up_weights: bfloat16 [2048, 16384], P(('dp', 'seq')), may hold values from -0.125 to 0.125
- down_weights: bfloat16 [8192, 2048], P(('dp', 'seq')), may hold values from -0.0625 to 0.0625
- cotangent: bfloat16 [4, 1024, 2048], P('dp', 'seq'), may hold values from -6 to 6
Outputs:
- output: bfloat16 [4, 1024, 2048], P('dp', 'seq')
- input_grad: float32 [4, 1024, 2048], P('dp', 'seq')
- grad_attn_weights: float32 [2048, 8192], P(('dp', 'seq'))
- grad_gate_up: float32 [2048, 16384], P(('dp', 'seq'))
- grad_down: float32 [8192, 2048], P(('dp', 'seq'))
- grad_q_gain: float32 [2048], P(('dp', 'seq'))
- grad_k_gain: float32 [2048], P(('dp', 'seq'))
- grad_attn_gain: float32 [2048], P(('dp', 'seq'))
- grad_ffn_gain: float32 [2048], P(('dp', 'seq'))
Inputs may be any that keep to these rules, and one draw needn't show every extreme that they name: `segments`: segment numbers start at 0 in each sequence and never fall. In each sequence one document begins at a position between 1 and 127 and ends at a position between 896 and 1022; every other document is shorter than 128 tokens.
All inputs are finite; a program needn't handle non-finite values.
Results may differ from a plain program's by a relative error of at most 0.03.
Values may be sent and summed in bfloat16 or wider, within the bound.
A program may use at most 512 MiB of HBM per device.

v0:
```python
import jax
import jax.numpy as jnp
from jax import lax
from jax.sharding import PartitionSpec as P

HEAD = 128


epsilon = 1e-06
rope_base = 500000.0


def rms_gain(values, gain):
    return values * lax.rsqrt(jnp.mean(values * values, axis=-1, keepdims=True) + epsilon) * gain


def rotate(values, positions):
    num_rows = values.shape[0]
    heads = values.shape[1] // HEAD
    half_dim = HEAD // 2
    frequency = rope_base ** (-2.0 * jnp.arange(half_dim, dtype=jnp.float32) / HEAD)
    angles = positions[:, None] * frequency[None, :]
    cosine = jnp.cos(angles)[:, None, :]
    sines = jnp.sin(angles)[:, None, :]
    pieces = values.reshape(num_rows, heads, HEAD)
    leading = pieces[..., :half_dim]
    trailing = pieces[..., half_dim:]
    turned = jnp.concatenate(
        [leading * cosine - trailing * sines, trailing * cosine + leading * sines], axis=-1
    )
    return turned.reshape(num_rows, heads * HEAD)


def swiglu(gate_part, up_part):
    return jax.nn.silu(gate_part) * up_part


def contract_last(left, right):
    return lax.dot_general(
        left, right, (((1,), (1,)), ((), ())), preferred_element_type=jnp.float32
    )


def contract_first(left, right):
    return lax.dot_general(
        left, right, (((0,), (0,)), ((), ())), preferred_element_type=jnp.float32
    )


def per_device(
    hidden_in,
    segments,
    attn_weights,
    q_gain,
    k_gain,
    attn_gain,
    ffn_gain,
    gate_up_weights,
    down_weights,
    cotangent,
):
    inputs = hidden_in[0]
    doc_ids = segments[0]
    num_rows = inputs.shape[0]
    width = inputs.shape[1]
    inner = gate_up_weights.shape[1] // 2
    heads = width // HEAD
    inv_root = HEAD ** (-0.5)
    offset = lax.axis_index("seq") * num_rows
    query_index = offset + jnp.arange(num_rows, dtype=jnp.int32)
    positions = query_index.astype(jnp.float32)
    kept_rows = 0
    pieces = (
        lax.all_gather(attn_weights, ("dp", "seq"), axis=0, tiled=True),
        lax.all_gather(q_gain, ("dp", "seq"), axis=0, tiled=True),
        lax.all_gather(k_gain, ("dp", "seq"), axis=0, tiled=True),
        lax.all_gather(attn_gain, ("dp", "seq"), axis=0, tiled=True),
        lax.all_gather(ffn_gain, ("dp", "seq"), axis=0, tiled=True),
    )
    running = jnp.zeros((num_rows, 3 * width), jnp.float32)
    qkv_store = jnp.zeros((kept_rows, 3 * width), jnp.bfloat16)
    w_piece = pieces[0]
    taken = inputs
    running = jnp.dot(taken, w_piece[:, : 3 * width], preferred_element_type=jnp.float32)
    out_store = w_piece[:, 3 * width :]
    gain_store = jnp.stack(pieces[1:], axis=0)
    projected, out_proj, qkv_store, gain_store = (running, out_store, qkv_store, gain_store)
    gains = gain_store.astype(jnp.float32)

    def norm_rotate(values, gain):
        return rotate(rms_gain(values, gain), positions)

    q_rot, q_back = jax.vjp(norm_rotate, projected[:, :width], gains[0])
    k_rot, k_back = jax.vjp(norm_rotate, projected[:, width : 2 * width], gains[1])
    q_low = q_rot.astype(jnp.bfloat16)
    k_low = k_rot.astype(jnp.bfloat16)
    v_low = projected[:, 2 * width :].astype(jnp.bfloat16)
    key_all, value_all = (
        lax.all_gather(k_low, "seq", axis=0, tiled=True),
        lax.all_gather(v_low, "seq", axis=0, tiled=True),
    )
    key_docs = lax.all_gather(doc_ids, "seq", axis=0, tiled=True)
    length = key_all.shape[0]
    key_len = min(512, length)
    num_blocks = (offset + num_rows - 1) // key_len + 1
    query_heads = q_low.reshape(num_rows, heads, HEAD)

    def block_scores(index):
        begin_at = index * key_len
        key_block = lax.dynamic_slice_in_dim(key_all, begin_at, key_len, 0).reshape(
            key_len, heads, HEAD
        )
        value_block = lax.dynamic_slice_in_dim(value_all, begin_at, key_len, 0).reshape(
            key_len, heads, HEAD
        )
        scores = (
            jnp.einsum("qhd,khd->hqk", query_heads, key_block, preferred_element_type=jnp.float32)
            * inv_root
        )
        key_index = begin_at + jnp.arange(key_len, dtype=jnp.int32)
        block_docs = lax.dynamic_slice_in_dim(key_docs, begin_at, key_len)
        allowed = (key_index[None, :] <= query_index[:, None]) & (
            block_docs[None, :] == doc_ids[:, None]
        )
        return (scores, allowed[None], key_block, value_block)

    def forward_step(index, state):
        top_score, total, running = state
        scores, allowed, key_block, value_block = block_scores(index)
        new_top = jnp.maximum(top_score, jnp.max(jnp.where(allowed, scores, -1e30), axis=-1))
        weights = jnp.where(allowed, jnp.exp(scores - new_top[..., None]), 0.0)
        factor = jnp.exp(top_score - new_top)
        total = total * factor + jnp.sum(weights, axis=-1)
        running = running * factor[..., None] + jnp.einsum(
            "hqk,khd->hqd",
            weights.astype(jnp.bfloat16),
            value_block,
            preferred_element_type=jnp.float32,
        )
        return (new_top, total, running)

    first_state = (
        jnp.full((heads, num_rows), -1e30, jnp.float32),
        jnp.zeros((heads, num_rows), jnp.float32),
        jnp.zeros((heads, num_rows, HEAD), jnp.float32),
    )
    top_score, total, running = lax.fori_loop(0, num_blocks, forward_step, first_state)
    log_total = top_score + jnp.log(total)
    mixed = jnp.transpose(running / total[..., None], (1, 0, 2)).reshape(num_rows, width)
    mixed_low = mixed.astype(jnp.bfloat16)
    branch = jnp.dot(mixed_low, out_proj, preferred_element_type=jnp.float32)
    attn_post, attn_back = jax.vjp(rms_gain, branch, gains[2])
    hidden = inputs.astype(jnp.float32) + attn_post
    hidden_low = hidden.astype(jnp.bfloat16)
    taken = hidden_low
    running_sum = jnp.dot(
        taken,
        lax.all_gather(gate_up_weights, ("dp", "seq"), axis=0, tiled=True),
        preferred_element_type=jnp.float32,
    )
    gate_up = running_sum
    activated, swiglu_back = jax.vjp(swiglu, gate_up[:, :inner], gate_up[:, inner:])
    act_low = activated.astype(jnp.bfloat16)
    taken = act_low
    running_sum = jnp.dot(
        taken,
        lax.all_gather(down_weights, ("dp", "seq"), axis=0, tiled=True),
        preferred_element_type=jnp.float32,
    )
    ffn_post, ffn_back = jax.vjp(rms_gain, running_sum, gains[3])
    output = (hidden + ffn_post).astype(jnp.bfloat16)
    grad_out = cotangent[0].astype(jnp.float32)
    grad_down_in, grad_ffn_g = ffn_back(grad_out)
    down_low = grad_down_in.astype(jnp.bfloat16)
    gu_full, down_full = (
        lax.all_gather(gate_up_weights, ("dp", "seq"), axis=0, tiled=True),
        lax.all_gather(down_weights, ("dp", "seq"), axis=0, tiled=True),
    )
    grad_act = contract_last(down_low, down_full)
    grad_gate, grad_up = swiglu_back(grad_act)
    gu_low = jnp.concatenate([grad_gate, grad_up], axis=1).astype(jnp.bfloat16)
    grad_hidden = grad_out + contract_last(gu_low, gu_full)
    grad_down = lax.psum_scatter(
        contract_first(act_low, down_low), ("dp", "seq"), scatter_dimension=0, tiled=True
    )
    grad_gate_up = lax.psum_scatter(
        contract_first(hidden_low, gu_low), ("dp", "seq"), scatter_dimension=0, tiled=True
    )
    grad_branch, grad_attn_g = attn_back(grad_hidden)
    branch_low = grad_branch.astype(jnp.bfloat16)
    attn_full = lax.all_gather(attn_weights, ("dp", "seq"), axis=0, tiled=True)
    qkv_full = attn_full[:, : 3 * width]
    out_full = attn_full[:, 3 * width :]
    grad_mixed = contract_last(branch_low, out_full).astype(jnp.bfloat16)
    grad_heads = grad_mixed.reshape(num_rows, heads, HEAD)
    delta = jnp.einsum(
        "qhd,qhd->hq", grad_heads.astype(jnp.float32), mixed.reshape(num_rows, heads, HEAD)
    )

    def backward_step(index, state):
        grad_query, grad_keys, grad_values = state
        scores, allowed, key_block, value_block = block_scores(index)
        probs = jnp.where(allowed, jnp.exp(scores - log_total[..., None]), 0.0)
        grad_probs = jnp.einsum(
            "qhd,khd->hqk", grad_heads, value_block, preferred_element_type=jnp.float32
        )
        grad_scores = (probs * (grad_probs - delta[..., None])).astype(jnp.bfloat16)
        grad_query = (
            grad_query
            + jnp.einsum("hqk,khd->hqd", grad_scores, key_block, preferred_element_type=jnp.float32)
            * inv_root
        )
        key_part = (
            jnp.einsum(
                "hqk,qhd->khd", grad_scores, query_heads, preferred_element_type=jnp.float32
            ).reshape(key_len, width)
            * inv_root
        )
        value_part = jnp.einsum(
            "hqk,qhd->khd",
            probs.astype(jnp.bfloat16),
            grad_heads,
            preferred_element_type=jnp.float32,
        ).reshape(key_len, width)
        begin_at = index * key_len
        grad_keys = lax.dynamic_update_slice_in_dim(
            grad_keys,
            lax.dynamic_slice_in_dim(grad_keys, begin_at, key_len, 0) + key_part,
            begin_at,
            0,
        )
        grad_values = lax.dynamic_update_slice_in_dim(
            grad_values,
            lax.dynamic_slice_in_dim(grad_values, begin_at, key_len, 0) + value_part,
            begin_at,
            0,
        )
        return (grad_query, grad_keys, grad_values)

    back_state = (
        jnp.zeros((heads, num_rows, HEAD), jnp.float32),
        jnp.zeros((length, width), jnp.float32),
        jnp.zeros((length, width), jnp.float32),
    )
    grad_query, grad_keys, grad_values = lax.fori_loop(0, num_blocks, backward_step, back_state)
    key_mine, value_mine = (
        lax.psum_scatter(
            grad_keys.astype(jnp.bfloat16), "seq", scatter_dimension=0, tiled=True
        ).astype(jnp.float32),
        lax.psum_scatter(
            grad_values.astype(jnp.bfloat16), "seq", scatter_dimension=0, tiled=True
        ).astype(jnp.float32),
    )
    grad_q_in, grad_q_g = q_back(jnp.transpose(grad_query, (1, 0, 2)).reshape(num_rows, width))
    grad_k_in, grad_k_g = k_back(key_mine)
    qkv_low = jnp.concatenate([grad_q_in, grad_k_in, value_mine], axis=1).astype(jnp.bfloat16)
    input_grad = grad_hidden + contract_last(qkv_low, qkv_full)
    in_part = contract_first(inputs, qkv_low)
    out_part = contract_first(mixed_low, branch_low)
    grad_attn = lax.psum_scatter(
        jnp.concatenate([in_part, out_part], axis=1), ("dp", "seq"), scatter_dimension=0, tiled=True
    )
    grad_qg, grad_kg, grad_ag, grad_fg = (
        lax.psum_scatter(grad_q_g, ("dp", "seq"), scatter_dimension=0, tiled=True),
        lax.psum_scatter(grad_k_g, ("dp", "seq"), scatter_dimension=0, tiled=True),
        lax.psum_scatter(grad_attn_g, ("dp", "seq"), scatter_dimension=0, tiled=True),
        lax.psum_scatter(grad_ffn_g, ("dp", "seq"), scatter_dimension=0, tiled=True),
    )
    return (
        output[None],
        input_grad[None],
        grad_attn,
        grad_gate_up,
        grad_down,
        grad_qg,
        grad_kg,
        grad_ag,
        grad_fg,
    )


def solution(mesh):
    in_specs = (
        P("dp", "seq", None),
        P("dp", "seq"),
        P(("dp", "seq"), None),
        P(("dp", "seq")),
        P(("dp", "seq")),
        P(("dp", "seq")),
        P(("dp", "seq")),
        P(("dp", "seq"), None),
        P(("dp", "seq"), None),
        P("dp", "seq", None),
    )
    out_specs = (
        P("dp", "seq", None),
        P("dp", "seq", None),
        P(("dp", "seq"), None),
        P(("dp", "seq"), None),
        P(("dp", "seq"), None),
        P(("dp", "seq")),
        P(("dp", "seq")),
        P(("dp", "seq")),
        P(("dp", "seq")),
    )
    return jax.shard_map(
        per_device, mesh=mesh, in_specs=in_specs, out_specs=out_specs, check_vma=False
    )
```

profile of v0, /device:TPU:15, one launch (start us, length us, event | category | flops | bytes accessed | tf_op | source)
XLA Modules:
  0.0 4013.1 jit_solution(12563810022611201159)
XLA Ops:
  8.0 196.4 %all-gather.7.cloned.1.call-done = bf16[2048,8192]{1,0:T(8,128)(2,1)} async-done(((bf16[64,8192]{1,0:T(8,128)(2,1)}), bf16[2048,8192]{1,0:T(8,128)(2,1)}) %all-gather.7.cloned.1.call-update) | async-done | bytes 33554448 | tf_op jit(solution)/shard_map/all_gather | solution.py:74
  204.4 10.1 fusion.33
  216.7 39.9 all-reduce.14
  267.1 10.0 all-gather
  277.5 6.4 copy.84
  283.9 21.0 all-gather.9.cloned.1.call-done
  305.0 13.1 while.30
  325.8 336.3 %all-gather.13.cloned.1.call-done = bf16[2048,16384]{1,0:T(8,128)(2,1)} async-done(((bf16[64,16384]{1,0:T(8,128)(2,1)}), bf16[2048,16384]{1,0:T(8,128)(2,1)}) %all-gather.13.cloned.1.call-update) | async-done | bytes 67108880 | tf_op jit(solution)/shard_map/all_gather | solution.py:158
  662.0 27.2 fusion.80
  694.0 163.8 %all-gather.15.cloned.1.call-done = bf16[8192,2048]{1,0:T(8,128)(2,1)} async-done(((bf16[256,2048]{1,0:T(8,128)(2,1)}), bf16[8192,2048]{1,0:T(8,128)(2,1)}) %all-gather.15.cloned.1.call-update) | async-done | bytes 33554448 | tf_op jit(solution)/shard_map/all_gather | solution.py:167
  857.7 13.0 multiply_reduce_fusion.7
  872.1 20.2 fusion.41
  892.2 44.8 %multiply_reduce_fusion.1 = (f32[2048]{0:T(1024)}, f32[128]{0:T(128)S(1)}, f32[128,2048]{1,0:T(8,128)}) fusion(f32[128,2048]{1,0:T(8,128)S(1)} %copy-done.8, f32[128]{0:T(128)S(1)} %fusion.72, f32[2048]{0:T(1024)S(1)} %bitcast.191, bf16[2048,16384]{1,0:T(8,128)(2,1)} %all-gather.13.cloned.1.call-done, bf16[128,8192]{1,0:T(8,128)(2,1)} %get-tuple-element.378, ...), kind=kOutput, calls=%fused_computation.92 | convolution fusion | flops 8600418304 | bytes 73942016 | tf_op jit(solution)/shard_map/dot_general | solution.py:39
  939.7 6.5 fusion.57
  958.4 96.1 %while.31 = (s32[]{:T(128)}, f32[16,128,128]{2,1,0:T(8,128)S(1)}, f32[1024,2048]{0,1:T(8,128)}, f32[1024,2048]{1,0:T(8,128)}, s32[]{:T(128)}, /*index=5*/s32[102...) while((s32[]{:T(128)}, f32[16,128,128]{2,1,0:T(8,128)S(1)}, ...), condition=%wide.region_11.12_spmd.clone, body=%wide.region_10.11_spmd.clone.sunk | while | flops 1356530304 | bytes 147033920 | solution.py:245
  973.2 6.6 constant_dynamic-update-slice_fusion.4
  1021.3 6.6 constant_dynamic-update-slice_fusion.4
  1054.5 6.1 convert_element_type.84
  1060.6 6.6 copy.113
  1074.4 26.5 fusion.82
  1102.1 8.1 fusion.81
  1110.2 8.0 reduce-scatter.17.cloned.1.call-done
  1134.2 39.8 reduce-scatter.13.cloned.1.call-done
  1174.0 22.1 convolution_bitcast_fusion
  1196.0 43.9 %pad_maximum_fusion = f32[2048,8192]{0,1:T(8,128)} fusion(f32[2048,2048]{0,1:T(8,128)} %fusion.81, f32[2048,6144]{0,1:T(8,128)} %convolution_bitcast_fusion), kind=kLoop, calls=%fused_computation.48 | loop fusion | flops 16777216 | bytes 134217728 | tf_op jit(solution)/shard_map/concatenate | solution.py:261
  1239.9 62.7 %copy.115 = f32[2048,8192]{1,0:T(8,128)} copy(f32[2048,8192]{0,1:T(8,128)} %pad_maximum_fusion) | data formatting | bytes 134217728
  1304.3 46.2 %fusion.43 = f32[2048,16384]{1,0:T(8,128)} fusion(bf16[128,2048]{1,0:T(8,128)(2,1)S(1)} %copy-done.15, bf16[128,8192]{1,0:T(8,128)(2,1)} %get-tuple-element.378, bf16[128,8192]{1,0:T(8,128)(2,1)S(1)} %copy-done.13), kind=kOutput, calls=%fused_computation.67 | convolution fusion | flops 8598323200 | bytes 138936320 | tf_op jit(solution)/shard_map/dot_general | solution.py:45
  1351.3 43.0 %all-reduce.13 = (f32[2048]{0:T(1024)S(1)}, f32[2048]{0:T(1024)S(1)}, f32[2048]{0:T(1024)S(1)}, f32[2048]{0:T(1024)S(1)}) all-reduce(f32[2048]{0:T(1024)S(1)} %copy-done.40, f32[2048]{0:T(1024)S(1)} %copy-done.39, f32[2048]{0:T(1024)S(1)} %copy-done.38, f32[2048]{0:T(1024)S(1)} %copy-done.37), channel_id=8, replica_groups=mesh['dp'=4,'seq'=8] {'dp','seq'}, use_global_device_ids=true, to_apply=%region_20.21.clone | all-reduce | flops 8192 | bytes 65536
  1396.6 14.0 fusion.48
  1410.6 472.4 %reduce-scatter.15.cloned.1.call-done = f32[256,2048]{1,0:T(8,128)} async-done(((f32[8192,2048]{1,0:T(8,128)}), f32[256,2048]{1,0:T(8,128)}) %reduce-scatter.15.cloned.1.call-update) | async-done | bytes 2097168 | tf_op jit(solution)/shard_map/reduce_scatter | solution.py:183
  1883.0 713.2 %reduce-scatter.19.cloned.1.call-done = f32[64,8192]{1,0:T(8,128)} async-done(((f32[2048,8192]{1,0:T(8,128)}), f32[64,8192]{1,0:T(8,128)}) %reduce-scatter.19.cloned.1.call-update) | async-done | bytes 2097168
  2596.2 1409.7 %reduce-scatter.21.cloned.1.call-done = f32[64,16384]{1,0:T(8,128)} async-done(((f32[2048,16384]{1,0:T(8,128)}), f32[64,16384]{1,0:T(8,128)}) %reduce-scatter.21.cloned.1.call-update) | async-done | bytes 4194320
  (253 shorter events, 166.4 us)
Async XLA Ops:
  7.2 197.3 %all-gather.7.cloned.1.call-start = ((), (), s32[]{:S(2)}) async-start(), calls=%async_computation.5 | async-start | bytes 34603008 | tf_op jit(solution)/shard_map/all_gather | solution.py:74
  7.9 207.7 %copy-start.49 = (bf16[64]{0:T(256)(128)(2,1)S(1)}, bf16[64]{0:T(256)(128)(2,1)}, u32[]{:S(2)}) copy-start(bf16[64]{0:T(256)(128)(2,1)} %param.20) | copy-start | bytes 388
  7.9 208.0 %copy-start.50 = (bf16[64]{0:T(256)(128)(2,1)S(1)}, bf16[64]{0:T(256)(128)(2,1)}, u32[]{:S(2)}) copy-start(bf16[64]{0:T(256)(128)(2,1)} %param.19) | copy-start | bytes 388
  7.9 208.2 %copy-start.51 = (bf16[64]{0:T(256)(128)(2,1)S(1)}, bf16[64]{0:T(256)(128)(2,1)}, u32[]{:S(2)}) copy-start(bf16[64]{0:T(256)(128)(2,1)} %param.18) | copy-start | bytes 388
  7.9 208.5 %copy-start.52 = (bf16[64]{0:T(256)(128)(2,1)S(1)}, bf16[64]{0:T(256)(128)(2,1)}, u32[]{:S(2)}) copy-start(bf16[64]{0:T(256)(128)(2,1)} %param.17) | copy-start | bytes 388
  8.0 269.5 %all-gather.11.cloned.1.call-start = ((), (), s32[]{:S(2)}) async-start(), calls=%async_computation.7 | async-start | bytes 4718592 | tf_op jit(solution)/shard_map/all_gather | solution.py:100
  214.6 47.4 %copy-start.2 = (f32[128,6144]{1,0:T(8,128)}, f32[128,6144]{1,0:T(8,128)S(1)}, u32[]{:S(2)}) copy-start(f32[128,6144]{1,0:T(8,128)S(1)} %fusion.33) | copy-start | bytes 9437188
  215.6 89.3 %all-gather.9.cloned.1.call-start = ((), (), s32[]{:S(2)}) async-start(), calls=%async_computation.6 | async-start | bytes 4718592 | tf_op jit(solution)/shard_map/all_gather | solution.py:99
  265.9 396.1 %all-gather.13.cloned.1.call-start = ((), (), s32[]{:S(2)}) async-start(), calls=%async_computation.8 | async-start | bytes 69206016 | tf_op jit(solution)/shard_map/all_gather | solution.py:158
  266.5 591.3 %all-gather.15.cloned.1.call-start = ((), (), s32[]{:S(2)}) async-start(), calls=%async_computation.9 | async-start | bytes 34603008 | tf_op jit(solution)/shard_map/all_gather | solution.py:167
  267.1 851.2 %reduce-scatter.17.cloned.1.call-start = ((), (), s32[]{:S(2)}) async-start(), calls=%async_computation.12 | async-start | bytes 4718592
  325.8 336.3 %copy-start.14 = (bf16[128,2048]{1,0:T(8,128)(2,1)}, bf16[128,2048]{1,0:T(8,128)(2,1)S(1)}, u32[]{:S(2)}) copy-start(bf16[128,2048]{1,0:T(8,128)(2,1)S(1)} %fusion.66) | copy-start | bytes 1572868
  694.0 176.8 %copy-start.4 = (bf16[128,8192]{1,0:T(8,128)(2,1)}, bf16[128,8192]{1,0:T(8,128)(2,1)S(1)}, u32[]{:S(2)}) copy-start(bf16[128,8192]{1,0:T(8,128)(2,1)S(1)} %multiply_convert_fusion.1) | copy-start | bytes 6291460
  694.0 176.8 %copy-start.16 = (bf16[1,128,2048]{2,1,0:T(8,128)(2,1)S(1)}, bf16[1,128,2048]{2,1,0:T(8,128)(2,1)}, u32[]{:S(2)}) copy-start(bf16[1,128,2048]{2,1,0:T(8,128)(2,1)} %param.23) | copy-start | bytes 1572868
  872.0 20.2 copy-start.21
  872.0 20.2 copy-start.8
  892.2 44.8 %copy-start.6 = (f32[128,2048]{1,0:T(8,128)S(1)}, f32[128,2048]{1,0:T(8,128)}, u32[]{:S(2)}) copy-start(f32[128,2048]{1,0:T(8,128)} %copy-done.5) | copy-start | bytes 3145732
  1067.2 106.8 %reduce-scatter.13.cloned.1.call-start = ((), (), s32[]{:S(2)}) async-start(), calls=%async_computation.10 | async-start | bytes 4718592 | tf_op jit(solution)/shard_map/reduce_scatter | solution.py:250
  1073.3 809.7 %reduce-scatter.15.cloned.1.call-start = ((), (), s32[]{:S(2)}) async-start(), calls=%async_computation.11 | async-start | bytes 69206016 | tf_op jit(solution)/shard_map/reduce_scatter | solution.py:183
  1100.9 1495.2 %reduce-scatter.19.cloned.1.call-start = ((), (), s32[]{:S(2)}) async-start(), calls=%async_computation.13 | async-start | bytes 69206016
  1102.1 17.6 copy-start.29
  1102.1 17.6 copy-start.31
  1121.0 8.8 copy-start.3
  1121.0 8.8 copy-start.33
  1121.0 8.8 copy-start.35
  1121.0 8.8 copy-start.42
  1121.0 8.8 copy-start.44
  1302.6 2703.2 %reduce-scatter.21.cloned.1.call-start = ((), (), s32[]{:S(2)}) async-start(), calls=%async_computation.14 | async-start | bytes 138412032
  1350.5 46.1 %copy-start.18 = (f32[128,2048]{1,0:T(8,128)S(1)}, f32[128,2048]{1,0:T(8,128)}, u32[]{:S(2)}) copy-start(f32[128,2048]{1,0:T(8,128)} %get-tuple-element.407) | copy-start | bytes 3145732
  1350.5 46.1 %copy-start.19 = (bf16[128,2048]{1,0:T(8,128)(2,1)S(1)}, bf16[128,2048]{1,0:T(8,128)(2,1)}, u32[]{:S(2)}) copy-start(bf16[128,2048]{1,0:T(8,128)(2,1)} %get-tuple-element.379) | copy-start | bytes 1572868
  1350.5 46.1 %copy-start.20 = (bf16[128,2048]{1,0:T(8,128)(2,1)S(1)}, bf16[128,2048]{1,0:T(8,128)(2,1)}, u32[]{:S(2)}) copy-start(bf16[128,2048]{1,0:T(8,128)(2,1)} %get-tuple-element.380) | copy-start | bytes 1572868
  1350.6 46.1 %copy-start.27 = (bf16[128,2048]{1,0:T(8,128)(2,1)S(1)}, bf16[128,2048]{1,0:T(8,128)(2,1)}, u32[]{:S(2)}) copy-start(bf16[128,2048]{1,0:T(8,128)(2,1)} %reduce-scatter.13.cloned.1.call-done) | copy-start | bytes 1572868
  (33 other events, 97.3 us)
Sparse Core Ops, SparseCore 0:
  10.9 193.5 all-gather.6
  215.7 37.0 all-gather.10
  266.0 38.8 all-gather.8
  307.6 354.4 all-gather.12
  664.7 192.9 all-gather.14
  1067.3 50.9 reduce-scatter.16
  1122.6 51.3 reduce-scatter.12
  1176.9 706.0 reduce-scatter.14
  1885.9 710.1 reduce-scatter.18
  2599.0 1406.8 reduce-scatter.20
where the time goes:
time: 4030 us; the launch traced here: 4010 us
  waiting for transfers between devices  3360 us (83%)
  matrix products  269 us (7%)
  local copies, waits for them, and re-layouts  170 us (4%)
  other arithmetic  102 us (3%)
  blocking collectives  93 us (2%)
    unnamed x13, waiting for transfers between devices  2130 us
    reduce_scatter x1, waiting for transfers between devices, per_device(): lax.psum_scatter(contract_first(act_low, down_low), ('dp', 'seq'), scatte...  472 us
    all_gather x1, waiting for transfers between devices, per_device(): lax.all_gather(gate_up_weights, ('dp', 'seq'), axis=0, tiled=True)  336 us
    all_gather x1, waiting for transfers between devices, per_device(): lax.all_gather(attn_weights, ('dp', 'seq'), axis=0, tiled=True)  196 us
    all_gather x1, waiting for transfers between devices, per_device(): lax.all_gather(down_weights, ('dp', 'seq'), axis=0, tiled=True)  164 us
    dot_general x4, matrix products, contract_first(): lax.dot_general(left, right, (((0,), (0,)), ((), ())), preferred_element_...  103 us
    unnamed x122, local copies, waits for them, and re-layouts  88.3 us
    dot_general x4, matrix products, contract_last(): lax.dot_general(left, right, (((1,), (1,)), ((), ())), preferred_element_...  85.4 us
  transfers between devices with their start and end apart: 10, of which 9 were waited for; matrix products, arithmetic and copies ran while one was open for 8% of the time, Pallas kernels for 0%

commit v1 on v0

v1 whole, which is shorter than its diff:
```python
import functools

import jax
import jax.numpy as jnp
from jax import lax
from jax.experimental import pallas as pl
from jax.experimental.pallas import tpu as pltpu
from jax.sharding import PartitionSpec as P

HEAD = 128
epsilon = 1e-06
rope_base = 500000.0
MESH = pl.DeviceIdType.MESH
BF = jnp.bfloat16
F32 = jnp.float32
ANY = pl.BlockSpec(memory_space=pl.ANY)
VM = pl.BlockSpec(memory_space=pltpu.VMEM)
DMA = pltpu.SemaphoreType.DMA


class Plan:
    def __init__(self, mesh, heads):
        self.dp = mesh.shape["dp"]
        self.seq = mesh.shape["seq"]
        self.size = heads
        self.low = heads // self.seq
        self.groups = self.dp // self.low
        self.devices = self.dp * self.seq

    def here(self):
        dp = lax.axis_index("dp")
        seq = lax.axis_index("seq")
        return dp, seq, (dp % self.low) * self.seq + seq

    def member(self, dp, index):
        return (dp // self.low) * self.low + index // self.seq, index % self.seq

    def across(self, dp, seq, bit):
        if bit < self.seq:
            return dp, flip(seq, bit)
        return flip(dp, bit // self.seq), seq


def flip(value, bit):
    return value + bit * (1 - 2 * ((value // bit) % 2))


def flips(value, mask):
    bit = 1
    while bit <= mask:
        if mask & bit:
            value = flip(value, bit)
        bit *= 2
    return value


def greet(devices):
    barrier = pltpu.get_barrier_semaphore()
    for device in devices:
        pl.semaphore_signal(barrier, inc=1, device_id=device, device_id_type=MESH)
    pl.semaphore_wait(barrier, len(devices))


def greet_all(plan, dp, seq):
    barrier = pltpu.get_barrier_semaphore()
    me = dp * plan.seq + seq

    def hello(step, carry):
        other = (me + step) % plan.devices
        pl.semaphore_signal(
            barrier, inc=1, device_id=(other // plan.seq, other % plan.seq), device_id_type=MESH
        )
        return carry

    lax.fori_loop(1, plan.devices, hello, 0)
    pl.semaphore_wait(barrier, plan.devices - 1)


def greet_group(plan, dp, index):
    barrier = pltpu.get_barrier_semaphore()

    def hello(step, carry):
        other = plan.member(dp, (index + step) % plan.size)
        pl.semaphore_signal(barrier, inc=1, device_id=other, device_id_type=MESH)
        return carry

    lax.fori_loop(1, plan.size, hello, 0)
    pl.semaphore_wait(barrier, plan.size - 1)


def send(src, dst, send_sem, recv_sem, device):
    copy = pltpu.make_async_remote_copy(
        src_ref=src,
        dst_ref=dst,
        send_sem=send_sem,
        recv_sem=recv_sem,
        device_id=device,
        device_id_type=MESH,
    )
    copy.start()
    return copy


def wait_bytes(ref, sem):
    pltpu.make_async_copy(ref, ref, sem).wait()


def rows_of(rows):
    third = rows // 3 // 16 * 16
    first = (rows - third) // 2 // 16 * 16
    return ((0, first), (first, rows - third - first), (rows - third, third))


ORDERS = ((2, 4, 8), (4, 8, 2), (8, 2, 4))


def subsets(bits):
    masks = [0]
    for bit in bits:
        masks = masks + [mask | bit for mask in masks]
    return masks


def gather_steps(plan, x, out, dp, seq, index, sems):
    ici_send, ici_recv, core_send, core_recv, local = sems
    rows = x.shape[0]
    parts = rows_of(rows)
    copies = []

    def place(mask, part):
        start, count = parts[part]
        return out.at[pl.ds(flips(index, mask) * rows + start, count)]

    def source(mask, part):
        if mask == 0:
            start, count = parts[part]
            return x.at[pl.ds(start, count)]
        return place(mask, part)

    def slot(part, stage, mask):
        done = subsets(ORDERS[part][:stage])
        return part * 7 + 2**stage - 1 + done.index(mask)

    def forward(mask, part, stages):
        for stage in stages:
            bit = ORDERS[part][stage]
            number = slot(part, stage, mask)
            copies.append(
                send(
                    source(mask, part),
                    place(mask, part),
                    ici_send.at[number],
                    ici_recv.at[number],
                    plan.across(dp, seq, bit),
                )
            )

    def to_core(mask, part, number):
        copies.append(
            send(
                source(mask, part),
                place(mask, part),
                core_send.at[number],
                core_recv.at[number],
                plan.across(dp, seq, 1),
            )
        )

    def begin():
        pltpu.make_async_copy(x, out.at[pl.ds(index * rows, rows)], local).start()
        for stage in range(3):
            for part in range(3):
                forward(0, part, (stage,))
        for part in range(3):
            to_core(0, part, part)

    def finish():
        for stage in range(3):
            for part in range(3):
                bit = ORDERS[part][stage]
                for mask in subsets(ORDERS[part][:stage]):
                    number = slot(part, stage, mask)
                    arrived = place(mask | bit, part)
                    wait_bytes(arrived, ici_recv.at[number])
                    forward(mask | bit, part, range(stage + 1, 3))
                    to_core(mask | bit, part, 3 + number)
        for part in range(3):
            wait_bytes(place(1, part), core_recv.at[part])
            for stage in range(3):
                bit = ORDERS[part][stage]
                for mask in subsets(ORDERS[part][:stage]):
                    wait_bytes(place(1 | mask | bit, part), core_recv.at[3 + slot(part, stage, mask)])
        for copy in copies:
            copy.wait_send()
        pltpu.make_async_copy(x, out.at[pl.ds(index * rows, rows)], local).wait()

    return begin, finish


GATHER_SEMS = (DMA((21,)), DMA((21,)), DMA((24,)), DMA((24,)), DMA)


def gather_group(plan, x):
    rows, width = x.shape

    def kernel(x_ref, out_ref, *sems):
        dp, seq, index = plan.here()
        greet([plan.across(dp, seq, bit) for bit in (1, 2, 4, 8)])
        begin, finish = gather_steps(plan, x_ref, out_ref, dp, seq, index, sems)
        begin()
        finish()

    return pl.pallas_call(
        kernel,
        out_shape=jax.ShapeDtypeStruct((plan.size * rows, width), x.dtype),
        in_specs=[ANY],
        out_specs=ANY,
        scratch_shapes=list(GATHER_SEMS),
        compiler_params=pltpu.CompilerParams(collective_id=1, has_side_effects=True),
        name="gather_group",
    )(x)


def scatter_sum(plan, partial):
    rows = partial.shape[0] // plan.size
    width = partial.shape[1]
    parts = rows_of(rows)

    def kernel(p_ref, out_ref, total, got, *rest):
        stage_bufs = rest[:9]
        core_send, core_recv, ici_send, ici_recv, local = rest[9:]
        dp, seq, index = plan.here()
        greet([plan.across(dp, seq, bit) for bit in (1, 2, 4, 8)])
        copies = []
        loads = []
        order = sorted(range(8), key=lambda m: -bin(m).count("1"))
        for m in order:
            block = flips(index, 1 | (2 * m))
            copies.append(
                send(
                    p_ref.at[pl.ds(block * rows, rows)],
                    got.at[m],
                    core_send.at[m],
                    core_recv.at[m],
                    plan.across(dp, seq, 1),
                )
            )
            mine = pltpu.make_async_copy(
                p_ref.at[pl.ds(flips(index, 2 * m) * rows, rows)], total.at[m], local.at[m]
            )
            mine.start()
            loads.append((m, mine, copies[-1]))

        def add(dst, src, count):
            @pl.loop(0, count // 16)
            def _(i):
                here = pl.ds(i * 16, 16)
                dst[here, :] = (dst[here, :].astype(F32) + src[here, :].astype(F32)).astype(BF)

        for m, mine, copy in loads:
            mine.wait()
            copy.wait_recv()
            add(total.at[m], got.at[m], rows)
        for stage in (2, 1, 0):
            landed = []
            for part in range(3):
                start, count = parts[part]
                bit = ORDERS[part][stage]
                for k, mask in enumerate(subsets(ORDERS[part][:stage])):
                    number = part * 7 + 2**stage - 1 + k
                    buffer = stage_bufs[part * 3 + stage].at[k]
                    copy = send(
                        total.at[(mask | bit) // 2, pl.ds(start, count)],
                        buffer,
                        ici_send.at[number],
                        ici_recv.at[number],
                        plan.across(dp, seq, bit),
                    )
                    copies.append(copy)
                    landed.append((copy, mask, start, count, buffer))
            for copy, mask, start, count, buffer in landed:
                copy.wait_recv()
                if stage > 0:
                    add(total.at[mask // 2, pl.ds(start, count)], buffer, count)
                else:

                    @pl.loop(0, count // 16)
                    def _(i, start=start, buffer=buffer):
                        here = pl.ds(start + i * 16, 16)
                        out_ref[here, :] = total[0, here, :].astype(F32) + buffer[
                            pl.ds(i * 16, 16), :
                        ].astype(F32)

        for copy in copies:
            copy.wait_send()

    scratch = [pltpu.VMEM((8, rows, width), BF), pltpu.VMEM((8, rows, width), BF)]
    for part in range(3):
        for stage in range(3):
            scratch.append(pltpu.VMEM((2**stage, parts[part][1], width), BF))
    scratch += [DMA((8,)), DMA((8,)), DMA((21,)), DMA((21,)), DMA((8,))]
    return pl.pallas_call(
        kernel,
        out_shape=jax.ShapeDtypeStruct((rows, width), F32),
        in_specs=[ANY],
        out_specs=VM,
        scratch_shapes=scratch,
        compiler_params=pltpu.CompilerParams(
            collective_id=2, has_side_effects=True, vmem_limit_bytes=40 * 2**20
        ),
        name="scatter_sum",
    )(partial)


def start_gather(plan, x, attn_w, gains, docs):
    rows, width = x.shape
    own = attn_w.shape[0]
    per_head = HEAD // own

    def kernel(x_ref, w_ref, g_ref, d_ref, xo, wo, oo, go, do, *sems):
        gather_sems, (w_send, w_recv, o_send, o_recv, g_send, g_recv, d_send, d_recv, local) = (
            sems[:5],
            sems[5:],
        )
        dp, seq, index = plan.here()
        me = dp * plan.seq + seq
        greet_all(plan, dp, seq)
        begin, finish = gather_steps(plan, x_ref, xo, dp, seq, index, gather_sems)
        begin()
        group = dp // plan.low
        feature = me * own
        head = feature // HEAD
        o_dst = oo.at[pl.ds(pl.multiple_of(feature % HEAD, own), own)]
        o_src = w_ref.at[:, pl.ds(3 * width, width)]

        def columns(part, other):
            return pl.ds(pl.multiple_of(part * width + other * HEAD, HEAD), HEAD)

        mine = pl.ds(me * own, own)

        def w_to(away, step, carry):
            other = (index + step) % plan.size
            to_group = (group + away) % plan.groups
            device = (to_group * plan.low + other // plan.seq, other % plan.seq)
            for part in range(3):
                send(
                    w_ref.at[:, columns(part, other)],
                    wo.at[mine, pl.ds(part * HEAD, HEAD)],
                    w_send,
                    w_recv,
                    device,
                )
            return carry

        for away in range(1, plan.groups):
            lax.fori_loop(0, plan.size, functools.partial(w_to, away), 0)
        lax.fori_loop(1, plan.size, functools.partial(w_to, 0), 0)
        for part in range(3):
            pltpu.make_async_copy(
                w_ref.at[:, columns(part, index)], wo.at[mine, pl.ds(part * HEAD, HEAD)], w_recv
            ).start()

        def o_to(away, carry):
            to_group = (group + away) % plan.groups
            to_dp, to_seq = to_group * plan.low + head // plan.seq, head % plan.seq
            same = to_dp * plan.seq + to_seq == me

            @pl.when(same)
            def _():
                pltpu.make_async_copy(o_src, o_dst, o_recv).start()

            @pl.when(jnp.logical_not(same))
            def _():
                send(o_src, o_dst, o_send, o_recv, (to_dp, to_seq))

            return carry

        lax.fori_loop(0, plan.groups, o_to, 0)

        def g_to(step, carry):
            other = (me + step) % plan.devices
            send(g_ref, go.at[me], g_send, g_recv, (other // plan.seq, other % plan.seq))
            return carry

        lax.fori_loop(1, plan.devices, g_to, 0)
        pltpu.make_async_copy(g_ref, go.at[me], g_recv).start()

        def d_to(step, carry):
            send(d_ref, do.at[index], d_send, d_recv, plan.member(dp, (index + step) % plan.size))
            return carry

        lax.fori_loop(1, plan.size, d_to, 0)
        pltpu.make_async_copy(d_ref, do.at[index], d_recv).start()
        finish()
        wait_bytes(go, g_recv)
        wait_bytes(do, d_recv)
        wait_bytes(oo, o_recv)
        wait_bytes(wo, w_recv)

        def sent(step, carry):
            wait_bytes(w_ref.at[:, pl.ds(0, 3 * HEAD)], w_send)
            wait_bytes(g_ref, g_send)
            return carry

        lax.fori_loop(1, plan.devices, sent, 0)

        def sent_docs(step, carry):
            wait_bytes(d_ref, d_send)
            return carry

        lax.fori_loop(1, plan.size, sent_docs, 0)

        def sent_o(away, carry):
            to_group = (group + away) % plan.groups
            to_dp, to_seq = to_group * plan.low + head // plan.seq, head % plan.seq

            @pl.when(to_dp * plan.seq + to_seq != me)
            def _():
                wait_bytes(o_src, o_send)

            return carry

        lax.fori_loop(0, plan.groups, sent_o, 0)

    shapes = (
        ((plan.size * rows, width), BF),
        ((plan.devices * own, 3 * HEAD), BF),
        ((HEAD, width), BF),
        ((plan.devices,) + gains.shape, gains.dtype),
        ((plan.size,) + docs.shape, docs.dtype),
    )
    return pl.pallas_call(
        kernel,
        out_shape=[jax.ShapeDtypeStruct(*shape) for shape in shapes],
        in_specs=[ANY] * 4,
        out_specs=[ANY] * 5,
        scratch_shapes=list(GATHER_SEMS) + [DMA] * 9,
        compiler_params=pltpu.CompilerParams(collective_id=0, has_side_effects=True),
        name="start_gather",
    )(x, attn_w, gains, docs)


def column_blocks(plan, inner, blocks):
    wide = inner // blocks
    each = wide // plan.size
    table = []
    for half in range(2):
        for block in range(blocks):
            table.append((half * inner + block * wide, each, (half * blocks + block) * each))
    return table


def gate_up_columns(plan, weights, blocks):
    own, both = weights.shape
    table = column_blocks(plan, both // 2, blocks)
    each = table[0][1]
    mine_wide = both // plan.size

    def kernel(w_ref, out_ref, w_send, w_recv):
        dp, seq, index = plan.here()
        greet_group(plan, dp, index)
        rows = pl.ds(index * own, own)

        def to(step, carry):
            other = (index + step) % plan.size
            device = plan.member(dp, other)
            for base, each, place in table:
                send(
                    w_ref.at[:, pl.ds(pl.multiple_of(base + other * each, 128), each)],
                    out_ref.at[rows, pl.ds(place, each)],
                    w_send,
                    w_recv,
                    device,
                )
            return carry

        lax.fori_loop(1, plan.size, to, 0)
        for base, each, place in table:
            pltpu.make_async_copy(
                w_ref.at[:, pl.ds(pl.multiple_of(base + index * each, 128), each)],
                out_ref.at[rows, pl.ds(place, each)],
                w_recv,
            ).start()
        wait_bytes(out_ref, w_recv)

        def sent(step, carry):
            wait_bytes(w_ref.at[:, pl.ds(0, mine_wide)], w_send)
            return carry

        lax.fori_loop(1, plan.size, sent, 0)

    return pl.pallas_call(
        kernel,
        out_shape=jax.ShapeDtypeStruct((plan.size * own, mine_wide), BF),
        in_specs=[ANY],
        out_specs=ANY,
        scratch_shapes=[DMA, DMA],
        compiler_params=pltpu.CompilerParams(collective_id=3, has_side_effects=True),
        name="gate_up_columns",
    )(weights)


def give_back(plan, gate_up, qkv, out_rows, gains, blocks):
    own = gate_up.shape[0] // plan.size
    both = gate_up.shape[1] * plan.size
    width = out_rows.shape[1]
    table = column_blocks(plan, both // 2, blocks)

    def kernel(gu, qk, ow, ga, gu_out, qk_out, ow_out, ga_out, *sems):
        gu_s, gu_r, qk_s, qk_r, ow_s, ow_r, ga_s, ga_r = sems
        dp, seq, index = plan.here()
        me = dp * plan.seq + seq
        group = dp // plan.low
        greet_all(plan, dp, seq)

        def g_to(step, carry):
            other = (me + step) % plan.devices
            send(ga.at[other], ga_out.at[me], ga_s, ga_r, (other // plan.seq, other % plan.seq))
            return carry

        lax.fori_loop(1, plan.devices, g_to, 0)
        pltpu.make_async_copy(ga.at[me], ga_out.at[me], ga_r).start()
        pieces = HEAD // own

        def o_to(piece, carry):
            other = index * pieces + piece
            src = ow.at[pl.ds(pl.multiple_of(piece * own, own), own)]

            @pl.when(other == me)
            def _():
                pltpu.make_async_copy(src, ow_out.at[group], ow_r).start()

            @pl.when(other != me)
            def _():
                send(src, ow_out.at[group], ow_s, ow_r, (other // plan.seq, other % plan.seq))

            return carry

        lax.fori_loop(0, pieces, o_to, 0)

        def moves(other, rows):
            for base, each, place in table:
                yield (
                    gu.at[rows, pl.ds(place, each)],
                    gu_out.at[:, pl.ds(pl.multiple_of(base + index * each, 128), each)],
                    gu_s,
                    gu_r,
                )
            for part in range(3):
                yield (
                    qk.at[rows, pl.ds(part * HEAD, HEAD)],
                    qk_out.at[:, pl.ds(pl.multiple_of(part * width + index * HEAD, 128), HEAD)],
                    qk_s,
                    qk_r,
                )

        def to(step, carry):
            other = (index + step) % plan.size
            device = plan.member(dp, other)
            for src, dst, s, r in moves(other, pl.ds(pl.multiple_of(other * own, own), own)):
                send(src, dst, s, r, device)
            return carry

        lax.fori_loop(1, plan.size, to, 0)
        for src, dst, s, r in moves(index, pl.ds(pl.multiple_of(index * own, own), own)):
            pltpu.make_async_copy(src, dst, r).start()
        wait_bytes(gu_out, gu_r)
        wait_bytes(qk_out, qk_r)
        wait_bytes(ow_out, ow_r)
        wait_bytes(ga_out, ga_r)

        def sent(step, carry):
            wait_bytes(gu.at[pl.ds(0, own)], gu_s)
            wait_bytes(qk.at[pl.ds(0, own)], qk_s)
            return carry

        lax.fori_loop(1, plan.size, sent, 0)

        def sent_gains(step, carry):
            wait_bytes(ga.at[0], ga_s)
            return carry

        lax.fori_loop(1, plan.devices, sent_gains, 0)

        def sent_o(piece, carry):
            @pl.when(index * pieces + piece != me)
            def _():
                wait_bytes(ow.at[pl.ds(0, own)], ow_s)

            return carry

        lax.fori_loop(0, pieces, sent_o, 0)

    shapes = (
        ((own, both), BF),
        ((own, 3 * width), BF),
        ((plan.groups, own, width), BF),
        (gains.shape, F32),
    )
    return pl.pallas_call(
        kernel,
        out_shape=[jax.ShapeDtypeStruct(*shape) for shape in shapes],
        in_specs=[ANY] * 4,
        out_specs=[ANY] * 4,
        scratch_shapes=[DMA] * 8,
        compiler_params=pltpu.CompilerParams(collective_id=4, has_side_effects=True),
        name="give_back",
    )(gate_up, qkv, out_rows, gains)


def sum_group(plan, values):
    def kernel(v_ref, out_ref, held, s_sem, r_sem):
        dp, seq, index = plan.here()
        greet_group(plan, dp, index)

        def to(step, carry):
            send(v_ref, held.at[step - 1], s_sem, r_sem, plan.member(dp, (index + step) % plan.size))
            return carry

        lax.fori_loop(1, plan.size, to, 0)
        wait_bytes(held, r_sem)
        wait_bytes(held, s_sem)
        total = v_ref[...]
        for i in range(plan.size - 1):
            total = total + held[i]
        out_ref[...] = total

    return pl.pallas_call(
        kernel,
        out_shape=jax.ShapeDtypeStruct(values.shape, F32),
        in_specs=[VM],
        out_specs=VM,
        scratch_shapes=[pltpu.VMEM((plan.size - 1,) + values.shape, F32), DMA, DMA],
        compiler_params=pltpu.CompilerParams(collective_id=5, has_side_effects=True),
        name="sum_group",
    )(values)


def dot(left, right):
    return jnp.dot(left, right, preferred_element_type=F32)


def contract_last(left, right):
    return lax.dot_general(left, right, (((1,), (1,)), ((), ())), preferred_element_type=F32)


def contract_first(left, right):
    return lax.dot_general(left, right, (((0,), (0,)), ((), ())), preferred_element_type=F32)


Q_BLOCK = 256


def scores_of(q, k, q_docs, k_docs):
    start = pl.program_id(1) * Q_BLOCK
    scores = contract_last(q, k) * HEAD ** (-0.5)
    row = start + lax.broadcasted_iota(jnp.int32, scores.shape, 0)
    column = lax.broadcasted_iota(jnp.int32, scores.shape, 1)
    allowed = (column <= row) & (q_docs == k_docs)
    scores = jnp.where(allowed, scores, -1e30)
    top = jnp.max(scores, axis=1, keepdims=True)
    weights = jnp.exp(scores - top)
    return weights / jnp.sum(weights, axis=1, keepdims=True)


def attend(q, k, v, docs_column, docs_row, length):
    def kernel(q_ref, k_ref, v_ref, qd_ref, kd_ref, o_ref):
        probs = scores_of(q_ref[...], k_ref[...], qd_ref[...], kd_ref[0])
        o_ref[...] = dot(probs.astype(BF), v_ref[...]).astype(BF)

    total = q.shape[0]
    steps = length // Q_BLOCK
    by_query = pl.BlockSpec((Q_BLOCK, HEAD), lambda i, j: (i * steps + j, 0))
    by_key = pl.BlockSpec((length, HEAD), lambda i, j: (i, 0))
    return pl.pallas_call(
        kernel,
        grid=(total // length, steps),
        out_shape=jax.ShapeDtypeStruct((total, HEAD), BF),
        in_specs=[
            by_query,
            by_key,
            by_key,
            pl.BlockSpec((Q_BLOCK, 1), lambda i, j: (i * steps + j, 0)),
            pl.BlockSpec((1, 1, length), lambda i, j: (i, 0, 0)),
        ],
        out_specs=by_query,
        compiler_params=pltpu.CompilerParams(vmem_limit_bytes=40 * 2**20),
        name="attend",
    )(q, k, v, docs_column, docs_row)


def attend_back(q, k, v, grad, docs_column, docs_row, length):
    def kernel(q_ref, k_ref, v_ref, g_ref, qd_ref, kd_ref, dq_ref, dk_ref, dv_ref):
        @pl.when(pl.program_id(1) == 0)
        def _():
            dk_ref[...] = jnp.zeros_like(dk_ref)
            dv_ref[...] = jnp.zeros_like(dv_ref)

        probs = scores_of(q_ref[...], k_ref[...], qd_ref[...], kd_ref[0])
        grad_probs = contract_last(g_ref[...], v_ref[...])
        delta = jnp.sum(probs * grad_probs, axis=1, keepdims=True)
        grad_scores = (probs * (grad_probs - delta)).astype(BF)
        scale = HEAD ** (-0.5)
        dq_ref[...] = dot(grad_scores, k_ref[...]) * scale
        dk_ref[...] += contract_first(grad_scores, q_ref[...]) * scale
        dv_ref[...] += contract_first(probs.astype(BF), g_ref[...])

    total = q.shape[0]
    steps = length // Q_BLOCK
    by_query = pl.BlockSpec((Q_BLOCK, HEAD), lambda i, j: (i * steps + j, 0))
    by_key = pl.BlockSpec((length, HEAD), lambda i, j: (i, 0))
    return pl.pallas_call(
        kernel,
        grid=(total // length, steps),
        out_shape=[jax.ShapeDtypeStruct((total, HEAD), F32)] * 3,
        in_specs=[
            by_query,
            by_key,
            by_key,
            by_query,
            pl.BlockSpec((Q_BLOCK, 1), lambda i, j: (i * steps + j, 0)),
            pl.BlockSpec((1, 1, length), lambda i, j: (i, 0, 0)),
        ],
        out_specs=[by_query, by_key, by_key],
        compiler_params=pltpu.CompilerParams(vmem_limit_bytes=40 * 2**20),
        name="attend_back",
    )(q, k, v, grad, docs_column, docs_row)


def per_device(
    plan,
    hidden_in,
    segments,
    attn_weights,
    q_gain,
    k_gain,
    attn_gain,
    ffn_gain,
    gate_up_weights,
    down_weights,
    cotangent,
):
    x = hidden_in[0]
    rows, width = x.shape
    own = attn_weights.shape[0]
    inner = gate_up_weights.shape[1] // 2
    length = rows * plan.seq
    tokens = rows * plan.size
    groups = plan.groups
    dp, seq, index = plan.here()
    me = dp * plan.seq + seq
    group = dp // plan.low
    direct = (inner // (groups * plan.size)) % 128 == 0
    blocks = groups if direct else 1

    def from_group(value, away):
        step = away * plan.low
        return lax.ppermute(value, "dp", [(i, (i + step) % plan.dp) for i in range(plan.dp)])

    def join_groups(value):
        whole = jnp.zeros((groups,) + value.shape, value.dtype)
        whole = lax.dynamic_update_index_in_dim(whole, value, group, 0)
        for away in range(1, groups):
            other = from_group(value, away)
            whole = lax.dynamic_update_index_in_dim(whole, other, (group - away) % groups, 0)
        return whole

    def sum_groups(value):
        total = lax.dynamic_index_in_dim(value, group, 0, keepdims=False)
        for away in range(1, groups):
            theirs = lax.dynamic_index_in_dim(value, (group + away) % groups, 0, keepdims=False)
            total = total + from_group(theirs.astype(BF), away).astype(F32)
        return total

    gains_mine = jnp.stack([q_gain, k_gain, attn_gain, ffn_gain]).astype(F32)
    gains_mine = jnp.pad(gains_mine, ((0, 4), (0, 128 - own)))
    docs_mine = jnp.broadcast_to(segments, (8, rows))
    x_all, w_qkv, w_out, gains_all, docs_all = start_gather(
        plan, x, attn_weights, gains_mine, docs_mine
    )
    gains = jnp.transpose(gains_all[:, :4, :own], (1, 0, 2)).reshape(4, width)
    docs = docs_all[:, 0, :].reshape(tokens)
    docs_column = docs.reshape(tokens, 1)
    docs_row = docs.reshape(tokens // length, 1, length)
    w_gu_part = gate_up_columns(plan, gate_up_weights, blocks)
    if direct:
        w_down = join_groups(down_weights).reshape(inner // plan.size, width)
    else:
        w_all = lax.all_gather(down_weights, ("dp", "seq"), axis=0, tiled=True)
        each = inner // plan.size
        w_down = lax.dynamic_slice_in_dim(w_all, index * each, each, 0)
    w_gu = join_groups(w_gu_part).reshape(width, 2 * inner // plan.size)

    qkv = dot(x_all, w_qkv)
    q, k, v = qkv[:, :HEAD], qkv[:, HEAD : 2 * HEAD], qkv[:, 2 * HEAD :]
    my_gains = lax.dynamic_slice_in_dim(gains[:2], index * HEAD, HEAD, 1)
    q_g, k_g = my_gains[0], my_gains[1]

    def over_group(first, second):
        both = jnp.stack([first, second]).reshape(2 * tokens // 128, 128)
        both = sum_group(plan, both).reshape(2, tokens, 1)
        return both[0], both[1]

    q_sum, k_sum = over_group(jnp.sum(q * q, axis=1), jnp.sum(k * k, axis=1))
    q_r = lax.rsqrt(q_sum / width + epsilon)
    k_r = lax.rsqrt(k_sum / width + epsilon)
    positions = (jnp.arange(tokens, dtype=jnp.int32) % length).astype(F32)
    half = HEAD // 2
    frequency = rope_base ** (-2.0 * jnp.arange(half, dtype=F32) / HEAD)
    angles = positions[:, None] * frequency[None, :]
    cosine = jnp.concatenate([jnp.cos(angles)] * 2, axis=1)
    sine = jnp.concatenate([-jnp.sin(angles), jnp.sin(angles)], axis=1)

    def turn(values, sine):
        swapped = jnp.concatenate([values[:, half:], values[:, :half]], axis=1)
        return values * cosine + swapped * sine

    q_low = turn(q * q_r * q_g, sine).astype(BF)
    k_low = turn(k * k_r * k_g, sine).astype(BF)
    v_low = v.astype(BF)
    mixed = attend(q_low, k_low, v_low, docs_column, docs_row, length)
    branch = scatter_sum(plan, dot(mixed, w_out).astype(BF))

    def rms(values):
        return lax.rsqrt(jnp.mean(values * values, axis=1, keepdims=True) + epsilon)

    def rms_back(values, r, gain, grad):
        scaled = gain * grad
        inner_sum = jnp.mean(scaled * values, axis=1, keepdims=True)
        return r * scaled - values * (r * r * r * inner_sum), jnp.sum(grad * values * r, axis=0)

    branch_r = rms(branch)
    hidden = x.astype(F32) + branch * branch_r * gains[2]
    hidden_low = hidden.astype(BF)

    h_all = gather_group(plan, hidden_low)
    gate_up = dot(h_all, w_gu)
    mine = inner // plan.size
    gate, up = gate_up[:, :mine], gate_up[:, mine:]
    act = (jax.nn.silu(gate) * up).astype(BF)
    down = scatter_sum(plan, dot(act, w_down).astype(BF))
    down_r = rms(down)
    output = (hidden + down * down_r * gains[3]).astype(BF)

    grad_out = cotangent[0].astype(F32)
    grad_down_in, grad_fg = rms_back(down, down_r, gains[3], grad_out)
    d_all = gather_group(plan, grad_down_in.astype(BF))
    grad_act = contract_last(d_all, w_down)
    sigma = jax.nn.sigmoid(gate)
    grad_gate = grad_act * up * sigma * (1.0 + gate * (1.0 - sigma))
    grad_up = grad_act * (gate * sigma)
    gu_low = jnp.concatenate([grad_gate, grad_up], axis=1).astype(BF)
    g_down = contract_first(act, d_all)
    if direct:
        grad_down = sum_groups(g_down.reshape(groups, mine // groups, width))
    else:
        spread = jnp.zeros((inner, width), BF)
        spread = lax.dynamic_update_slice_in_dim(spread, g_down.astype(BF), index * mine, 0)
        grad_down = lax.psum_scatter(
            spread, ("dp", "seq"), scatter_dimension=0, tiled=True
        ).astype(F32)
    grad_hidden = grad_out + scatter_sum(plan, contract_last(gu_low, w_gu).astype(BF))
    g_gu = contract_first(h_all, gu_low)
    g_gu = sum_groups(g_gu.reshape(groups, width // groups, 2 * mine)).astype(BF)

    grad_branch, grad_ag = rms_back(branch, branch_r, gains[2], grad_hidden)
    b_all = gather_group(plan, grad_branch.astype(BF))
    grad_mixed = contract_last(b_all, w_out).astype(BF)
    g_out = contract_first(mixed, b_all).astype(BF)
    dqr, dkr, dv = attend_back(q_low, k_low, v_low, grad_mixed, docs_column, docs_row, length)
    dq_n = turn(dqr, -sine)
    dk_n = turn(dkr, -sine)
    q_dot, k_dot = over_group(
        jnp.sum(dq_n * q_g * q, axis=1), jnp.sum(dk_n * k_g * k, axis=1)
    )

    def norm_back(grad, values, r, gain, total):
        return r * (gain * grad) - values * (r * r * r * (total / width))

    dq = norm_back(dq_n, q, q_r, q_g, q_dot)
    dk = norm_back(dk_n, k, k_r, k_g, k_dot)
    grad_qg = jnp.sum(dq_n * q * q_r, axis=0)
    grad_kg = jnp.sum(dk_n * k * k_r, axis=0)
    qkv_low = jnp.concatenate([dq, dk, dv], axis=1).astype(BF)
    input_grad = grad_hidden + scatter_sum(plan, contract_last(qkv_low, w_qkv).astype(BF))
    g_qkv = contract_first(x_all, qkv_low)
    g_qkv = sum_groups(g_qkv.reshape(groups, width // groups, 3 * HEAD)).astype(BF)

    def for_head(values):
        whole = jnp.zeros((width,), F32)
        return lax.dynamic_update_slice_in_dim(whole, values, index * HEAD, 0)

    gain_parts = jnp.stack([for_head(grad_qg), for_head(grad_kg), grad_ag, grad_fg])
    gain_parts = jnp.transpose(gain_parts.reshape(4, plan.devices, own), (1, 0, 2))
    gain_parts = jnp.pad(gain_parts, ((0, 0), (0, 4), (0, 128 - own)))
    gu_rows, qkv_rows, out_rows, gain_rows = give_back(
        plan, g_gu, g_qkv, g_out, gain_parts, blocks
    )
    grad_gate_up = gu_rows.astype(F32)
    grad_attn = jnp.concatenate(
        [qkv_rows.astype(F32), jnp.sum(out_rows.astype(F32), axis=0)], axis=1
    )
    gain_grads = jnp.sum(gain_rows, axis=0)[:4, :own]
    return (
        output[None],
        input_grad[None],
        grad_attn,
        grad_gate_up,
        grad_down,
        gain_grads[0],
        gain_grads[1],
        gain_grads[2],
        gain_grads[3],
    )


def solution(mesh):
    by_token = P("dp", "seq", None)
    by_row = P(("dp", "seq"), None)
    by_gain = P(("dp", "seq"))

    def run(hidden_in, segments, attn_weights, *rest):
        plan = Plan(mesh, hidden_in.shape[2] // HEAD)
        return jax.shard_map(
            functools.partial(per_device, plan),
            mesh=mesh,
            in_specs=(by_token, P("dp", "seq"), by_row)
            + (by_gain,) * 4
            + (by_row, by_row, by_token),
            out_specs=(by_token, by_token, by_row, by_row, by_row) + (by_gain,) * 4,
            check_vma=False,
        )(hidden_in, segments, attn_weights, *rest)

    return run
```

time: 4030 us -> 937 us (0.23)
  waiting for transfers between devices: 3360 us -> 149 us
  Pallas kernels: 0 us -> 604 us
  matrix products: 269 us -> 98.2 us
  local copies, waits for them, and re-layouts: 170 us -> 28.4 us
  blocking collectives: 93 us -> 0 us
  other arithmetic: 102 us -> 41.3 us
    unnamed x13 -> x0, waiting for transfers between devices: 2130 us -> none
    all_gather x5 -> x0, waiting for transfers between devices: 717 us -> none  [the longest x1 336 us: per_device(): lax.all_gather(gate_up_weights, ('dp', 'seq'), axis=0, tiled=True)]
    pallas_call x0 -> x14, Pallas kernels: none -> 604 us  [the longest x1 186 us: start_gather(): pl.pallas_call(kernel, out_shape=[jax.ShapeDtypeStruct(*shape) for shape...]
    reduce_scatter x2 -> x0, waiting for transfers between devices: 512 us -> none  [the longest x1 472 us: per_device(): lax.psum_scatter(contract_first(act_low, down_low), ('dp', 'seq'), scatte...]
    ppermute x0 -> x5, waiting for transfers between devices: none -> 149 us  [from_group(): lax.ppermute(value, 'dp', [(i, (i + step) % plan.dp) for i in range(plan....]
    unnamed x2 -> x0, blocking collectives: 83 us -> none
    unnamed x122 -> x94, local copies, waits for them, and re-layouts: 88.3 us -> 6.23 us
    dot_general x4, matrix products: 103 us -> 35.2 us  [contract_first(): lax.dot_general(left, right, (((0,), (0,)), ((), ())), preferred_element_...]
  transfers between devices with their start and end apart: 10 -> 5, of which waited for: 9 -> 2; matrix products, arithmetic and copies ran while one was open for 8% -> 5% of each run, Pallas kernels for 0% -> 30%
where the time goes in v1:
time: 937 us; the launch traced here: 928 us
  Pallas kernels  604 us (64%)
  waiting for transfers between devices  149 us (16%)
  matrix products  98.2 us (10%)
  other arithmetic  41.3 us (4%)
  local copies, waits for them, and re-layouts  28.4 us (3%)
    pallas_call x1, Pallas kernels, start_gather(): pl.pallas_call(kernel, out_shape=[jax.ShapeDtypeStruct(*shape) for shape...  186 us
    pallas_call x4, Pallas kernels, scatter_sum(): pl.pallas_call(kernel, out_shape=jax.ShapeDtypeStruct((rows, width), F32)...  171 us
    ppermute x5, waiting for transfers between devices, from_group(): lax.ppermute(value, 'dp', [(i, (i + step) % plan.dp) for i in range(plan....  149 us
    pallas_call x3, Pallas kernels, gather_group(): pl.pallas_call(kernel, out_shape=jax.ShapeDtypeStruct((plan.size * rows,...  110 us
    pallas_call x1, Pallas kernels, give_back(): pl.pallas_call(kernel, out_shape=[jax.ShapeDtypeStruct(*shape) for shape...  65.9 us
    pallas_call x1, Pallas kernels, gate_up_columns(): pl.pallas_call(kernel, out_shape=jax.ShapeDtypeStruct((plan.size * own, m...  35.3 us
    dot_general x4, matrix products, contract_first(): lax.dot_general(left, right, (((0,), (0,)), ((), ())), preferred_element_...  35.2 us
    dot_general x4, matrix products, contract_last(): lax.dot_general(left, right, (((1,), (1,)), ((), ())), preferred_element_...  34.7 us
  transfers between devices with their start and end apart: 5, of which 2 were waited for; matrix products, arithmetic and copies ran while one was open for 5% of the time, Pallas kernels for 30%

profile of v1, /device:TPU:15, one launch (start us, length us, event | category | flops | bytes accessed | tf_op | source)
XLA Modules:
  0.0 928.2 jit_solution(16087761841603975057)
XLA Ops:
  0.7 35.3 %gate_up_columns.1 = bf16[1024,1024]{1,0:T(8,128)(2,1)} custom-call(bf16[64,16384]{1,0:T(8,128)(2,1)} %w_ref.3), custom_call_target="tpu_custom_call" | custom-call | tf_op jit(solution)/shard_map/gate_up_columns/pallas_call | solution.py:492
  39.7 186.2 %start_gather.1 = (bf16[2048,2048]{1,0:T(8,128)(2,1)}, bf16[2048,384]{1,0:T(8,128)(2,1)}, bf16[128,2048]{1,0:T(8,128)(2,1)}, f32[32,8,128]{2,1,0:T(8,128)}, s32[16,8,128]{2,1,0:T(8,128)}) custom-call(bf16[128,2048]{1,0:T(8,128)(2,1)} %bitcast.118, bf16[64,8192]{1,0:T(8,128)(2,1)} %w_ref.2, f32[8,128]{1,0:T(8,128)} %fusion.39.g_ref, ...), custom_call_target="tpu_custom_call" | custom-call | tf_op jit(solution)/shard_map/start_gather/pallas_call | solution.py:432
  226.0 7.4 fusion.56
  235.9 9.0 sum_group.2
  249.8 3.7 fusion.23
  255.4 7.4 attend.1
  265.3 43.5 %scatter_sum.4 = f32[128,2048]{1,0:T(8,128)S(1)} custom-call(bf16[2048,2048]{1,0:T(8,128)(2,1)S(1)} %convolution_convert_fusion.3.p_ref), custom_call_target="tpu_custom_call" | custom-call | tf_op jit(solution)/shard_map/scatter_sum/pallas_call | solution.py:302
  310.1 36.4 %gather_group.3 = bf16[2048,2048]{1,0:T(8,128)(2,1)} custom-call(bf16[128,2048]{1,0:T(8,128)(2,1)} %fusion.21.x_ref), custom_call_target="tpu_custom_call" | custom-call | tf_op jit(solution)/shard_map/gather_group/pallas_call | solution.py:213
  354.0 13.3 %fusion.57 = f32[2048,1024]{0,1:T(8,128)S(1)} fusion(bf16[2048,2048]{1,0:T(8,128)(2,1)} %gather_group.3, bf16[2048,1024]{1,0:T(8,128)(2,1)S(1)} %bitcast.123), kind=kOutput, calls=%fused_computation.138 | convolution fusion | flops 8589934592 | bytes 20971520 | tf_op jit(solution)/shard_map/dot_general | solution.py:640
  370.5 5.2 convolution_convert_fusion.2.p_ref
  375.8 42.1 %scatter_sum.5 = f32[128,2048]{1,0:T(8,128)S(1)} custom-call(bf16[2048,2048]{1,0:T(8,128)(2,1)S(1)} %convolution_convert_fusion.2.p_ref), custom_call_target="tpu_custom_call" | custom-call | tf_op jit(solution)/shard_map/scatter_sum/pallas_call | solution.py:302
  419.4 36.7 %gather_group.4 = bf16[2048,2048]{1,0:T(8,128)(2,1)} custom-call(bf16[128,2048]{1,0:T(8,128)(2,1)} %fusion.8.x_ref), custom_call_target="tpu_custom_call" | custom-call | tf_op jit(solution)/shard_map/gather_group/pallas_call | solution.py:213
  456.1 13.4 %multiply_convert_fusion.1 = (bf16[2048,512]{0,1:T(8,128)(2,1)S(1)}, bf16[2048,512]{0,1:T(8,128)(2,1)}) fusion(f32[2048,1024]{0,1:T(8,128)} %copy-done.19, bf16[2048,2048]{1,0:T(8,128)(2,1)} %gather_group.4, bf16[512,2048]{1,0:T(8,128)(2,1)} %bitcast.128), kind=kOutput, calls=%fused_computation.9 | convolution fusion | flops 4308598784 | bytes 23068672 | tf_op jit(solution)/shard_map/dot_general | solution.py:644
  469.5 10.6 %convolution_convert_fusion.1.p_ref = bf16[2048,2048]{1,0:T(8,128)(2,1)S(1)} fusion(bf16[2048,1024]{1,0:T(8,128)(2,1)S(1)} %bitcast.124, bf16[2048,512]{0,1:T(8,128)(2,1)} %get-tuple-element.52, bf16[2048,512]{0,1:T(8,128)(2,1)S(1)} %get-tuple-element.51), kind=kOutput, calls=%fused_computation.1 | convolution fusion | flops 8602517504 | bytes 16777216 | tf_op jit(solution)/shard_map/dot_general | solution.py:644
  480.1 14.0 %fusion.2 = f32[2048,1024]{1,0:T(8,128)} fusion(bf16[2048,2048]{1,0:T(8,128)(2,1)} %gather_group.3, bf16[2048,512]{0,1:T(8,128)(2,1)} %get-tuple-element.52, bf16[2048,512]{0,1:T(8,128)(2,1)S(1)} %get-tuple-element.51), kind=kOutput, calls=%fused_computation.13 | convolution fusion | flops 8598323200 | bytes 20971520 | tf_op jit(solution)/shard_map/dot_general | solution.py:648
  494.1 42.2 %scatter_sum.6 = f32[128,2048]{1,0:T(8,128)S(1)} custom-call(bf16[2048,2048]{1,0:T(8,128)(2,1)S(1)} %convolution_convert_fusion.1.p_ref), custom_call_target="tpu_custom_call" | custom-call | tf_op jit(solution)/shard_map/scatter_sum/pallas_call | solution.py:302
  538.3 36.9 %gather_group.5 = bf16[2048,2048]{1,0:T(8,128)(2,1)} custom-call(bf16[128,2048]{1,0:T(8,128)(2,1)} %get-tuple-element.57.x_ref), custom_call_target="tpu_custom_call" | custom-call | tf_op jit(solution)/shard_map/gather_group/pallas_call | solution.py:213
  575.2 5.9 convolution_convert_fusion.5.g_ref
  581.2 10.9 %attend_back.1 = (f32[2048,128]{1,0:T(8,128)S(1)}, f32[2048,128]{1,0:T(8,128)S(1)}, f32[2048,128]{1,0:T(8,128)S(1)}) custom-call(bf16[2048,128]{1,0:T(8,128)(2,1)S(1)} %copy-done.7, bf16[2048,128]{1,0:T(8,128)(2,1)S(1)} %copy-done.9, bf16[2048,128]{1,0:T(8,128)(2,1)S(1)} %copy-done.5, bf16[2048,128]{1,0:T(8,128)(2,1)S(1)} %convolution_convert_fusion.5.g_ref, ...), custom_call_target="tpu_custom_call" | custom-call | tf_op jit(solution)/shard_map/attend_back/pallas_call | solution.py:712
  595.4 2.9 multiply_reduce_fusion.2
  598.9 8.5 sum_group.3
  608.3 3.4 subtract_convert_fusion.1
  611.8 4.8 convolution_convert_fusion.p_ref
  616.6 8.8 fusion.20
  625.5 6.3 fusion.58
  631.8 43.4 %scatter_sum.7 = f32[128,2048]{1,0:T(8,128)S(1)} custom-call(bf16[2048,2048]{1,0:T(8,128)(2,1)S(1)} %convolution_convert_fusion.p_ref), custom_call_target="tpu_custom_call" | custom-call | tf_op jit(solution)/shard_map/scatter_sum/pallas_call | solution.py:302
  675.2 3.9 fusion.3
  691.3 6.1 convolution_convert_fusion.4.ow
  697.3 128.4 %collective-permute-done.3 = bf16[1024,384]{1,0:T(8,128)(2,1)} collective-permute-done((bf16[1024,384]{1,0:T(8,128)(2,1)}, bf16[1024,384]{1,0:T(8,128)(2,1)}, u32[]{:S(2)}, u32[]{:S(2)}) %collective-permute-start.3) | collective-permute-done | bytes 786464 | tf_op jit(solution)/shard_map/ppermute | solution.py:758
  828.0 20.2 %collective-permute-done.4 = bf16[256,2048]{1,0:T(8,128)(2,1)} collective-permute-done((bf16[256,2048]{1,0:T(8,128)(2,1)}, bf16[256,2048]{1,0:T(8,128)(2,1)}, u32[]{:S(2)}, u32[]{:S(2)}) %collective-permute-start.4) | collective-permute-done | bytes 1048608 | tf_op jit(solution)/shard_map/ppermute | solution.py:758
  851.1 3.8 fusion.gu
  854.9 65.9 %give_back.1 = (bf16[64,16384]{1,0:T(8,128)(2,1)}, bf16[64,6144]{1,0:T(8,128)(2,1)}, bf16[2,64,2048]{2,1,0:T(8,128)(2,1)}, f32[32,8,128]{2,1,0:T(8,128)}) custom-call(bf16[1024,1024]{1,0:T(8,128)(2,1)} %fusion.gu, bf16[1024,384]{1,0:T(8,128)(2,1)} %fusion.4.qk, bf16[128,2048]{1,0:T(8,128)(2,1)} %convolution_convert_fusion.4.ow, f32[32,8,128]{2,1,0:T(8,128)} %pad.12.ga), custom_call_target="tpu_custom_call" | custom-call | tf_op jit(solution)/shard_map/give_back/pallas_call | solution.py:600
  (177 shorter events, 59.6 us)
Async XLA Ops:
  0.6 37.8 %copy-start.37 = (bf16[64]{0:T(256)(128)(2,1)S(1)}, bf16[64]{0:T(256)(128)(2,1)}, u32[]{:S(2)}) copy-start(bf16[64]{0:T(256)(128)(2,1)} %param.16) | copy-start | bytes 388
  0.7 37.8 %copy-start.38 = (bf16[64]{0:T(256)(128)(2,1)S(1)}, bf16[64]{0:T(256)(128)(2,1)}, u32[]{:S(2)}) copy-start(bf16[64]{0:T(256)(128)(2,1)} %param.15) | copy-start | bytes 388
  0.7 37.8 %copy-start.39 = (bf16[64]{0:T(256)(128)(2,1)S(1)}, bf16[64]{0:T(256)(128)(2,1)}, u32[]{:S(2)}) copy-start(bf16[64]{0:T(256)(128)(2,1)} %param.14) | copy-start | bytes 388
  0.7 37.8 %copy-start.40 = (bf16[64]{0:T(256)(128)(2,1)S(1)}, bf16[64]{0:T(256)(128)(2,1)}, u32[]{:S(2)}) copy-start(bf16[64]{0:T(256)(128)(2,1)} %param.13) | copy-start | bytes 388
  0.7 38.4 %copy-start.41 = (s32[1,128]{1,0:T(1,128)S(1)}, s32[1,128]{1,0:T(1,128)}, u32[]{:S(2)}) copy-start(s32[1,128]{1,0:T(1,128)} %param.11) | copy-start | bytes 1540
  36.0 315.3 %collective-permute-start = (bf16[1024,1024]{1,0:T(8,128)(2,1)}, bf16[1024,1024]{1,0:T(8,128)(2,1)}, u32[]{:S(2)}, u32[]{:S(2)}) collective-permute-start(bf16[1024,1024]{1,0:T(8,128)(2,1)} %gate_up_columns.1), channel_id=1, source_target_pairs={{0,16},{8,24},{16,0},{24,8},{1,17},{9,25},{17,1},{25,9},{2,18},{10... | collective-permute-start | bytes 6291464 | tf_op jit(solution)/shard_map/ppermute | solution.py:758
  38.4 311.6 %collective-permute-start.1 = (bf16[256,2048]{1,0:T(8,128)(2,1)}, bf16[256,2048]{1,0:T(8,128)(2,1)}, u32[]{:S(2)}, u32[]{:S(2)}) collective-permute-start(bf16[256,2048]{1,0:T(8,128)(2,1)} %param.18), channel_id=1, source_target_pairs={{0,16},{8,24},{16,0},{24,8},{1,17},{9,25},{17,1},{25,9},{2,18},{10... | collective-permute-start | bytes 3145736 | tf_op jit(solution)/shard_map/ppermute | solution.py:758
  226.0 9.1 copy-start.36
  235.1 20.4 %copy-start.4 = (bf16[2048,128]{1,0:T(8,128)(2,1)}, bf16[2048,128]{1,0:T(8,128)(2,1)S(1)}, u32[]{:S(2)}) copy-start(bf16[2048,128]{1,0:T(8,128)(2,1)S(1)} %slice.179.v_ref) | copy-start | bytes 1572868
  246.8 8.6 copy-start.2
  265.2 43.8 %copy-start.21 = (bf16[1,128,2048]{2,1,0:T(8,128)(2,1)S(1)}, bf16[1,128,2048]{2,1,0:T(8,128)(2,1)}, u32[]{:S(2)}) copy-start(bf16[1,128,2048]{2,1,0:T(8,128)(2,1)} %param.10) | copy-start | bytes 1572868
  351.3 19.2 %copy-start.29 = (bf16[2,256,2048]{2,1,0:T(8,128)(2,1)}, bf16[2,256,2048]{2,1,0:T(8,128)(2,1)S(1)}, u32[]{:S(2)}) copy-start(bf16[2,256,2048]{2,1,0:T(8,128)(2,1)S(1)} %bitcast_dynamic-update-slice_fusion.2) | copy-start | bytes 6291460
  353.9 13.4 %copy-start.23 = (bf16[2,1024,1024]{2,1,0:T(8,128)(2,1)}, bf16[2,1024,1024]{2,1,0:T(8,128)(2,1)S(1)}, u32[]{:S(2)}) copy-start(bf16[2,1024,1024]{2,1,0:T(8,128)(2,1)S(1)} %bitcast_dynamic-update-slice_fusion) | copy-start | bytes 12582916
  375.8 42.3 %copy-start.14 = (bf16[1,128,2048]{2,1,0:T(8,128)(2,1)S(1)}, bf16[1,128,2048]{2,1,0:T(8,128)(2,1)}, u32[]{:S(2)}) copy-start(bf16[1,128,2048]{2,1,0:T(8,128)(2,1)} %param.19) | copy-start | bytes 1572868
  456.1 13.4 %copy-start.24 = (bf16[2,1024,1024]{2,1,0:T(8,128)(2,1)S(1)}, bf16[2,1024,1024]{2,1,0:T(8,128)(2,1)}, u32[]{:S(2)}) copy-start(bf16[2,1024,1024]{2,1,0:T(8,128)(2,1)} %copy-done.23) | copy-start | bytes 12582916
  494.1 42.2 %copy-start.15 = (bf16[1,128,2048]{2,1,0:T(8,128)(2,1)S(1)}, bf16[1,128,2048]{2,1,0:T(8,128)(2,1)}, u32[]{:S(2)}) copy-start(bf16[1,128,2048]{2,1,0:T(8,128)(2,1)} %param.19) | copy-start | bytes 1572868
  494.1 42.6 %copy-start.22 = (bf16[1,128,2048]{2,1,0:T(8,128)(2,1)S(1)}, bf16[1,128,2048]{2,1,0:T(8,128)(2,1)}, u32[]{:S(2)}) copy-start(bf16[1,128,2048]{2,1,0:T(8,128)(2,1)} %param.10) | copy-start | bytes 1572868
  538.3 36.9 %copy-start.33 = (bf16[128,2048]{1,0:T(8,128)(2,1)S(1)}, bf16[128,2048]{1,0:T(8,128)(2,1)}, u32[]{:S(2)}) copy-start(bf16[128,2048]{1,0:T(8,128)(2,1)} %get-tuple-element.25) | copy-start | bytes 1572868
  595.4 12.1 %copy-start.34 = (f32[32,128]{1,0:T(8,128)S(1)}, f32[32,128]{1,0:T(8,128)}, u32[]{:S(2)}) copy-start(f32[32,128]{1,0:T(8,128)} %sum_group.2) | copy-start | bytes 49156
  598.3 13.5 %copy-start.31 = (bf16[2048,128]{1,0:T(8,128)(2,1)S(1)}, bf16[2048,128]{1,0:T(8,128)(2,1)}, u32[]{:S(2)}) copy-start(bf16[2048,128]{1,0:T(8,128)(2,1)} %convert.26) | copy-start | bytes 1572868
  611.8 13.6 %slice-start = ((s8[8388608]{0:T(1024)(128)(4,1)}), s8[4194304]{0:T(1024)(128)(4,1)S(1)}, s32[]{:S(2)}) async-start(s8[8388608]{0:T(1024)(128)(4,1)} %bitcast.116), calls=%async_computation | async-start | bytes 8388608
  616.6 8.8 slice-start.1
  616.6 8.8 copy-start.27
  675.2 13.4 %copy-start.16 = (bf16[1,128,2048]{2,1,0:T(8,128)(2,1)S(1)}, bf16[1,128,2048]{2,1,0:T(8,128)(2,1)}, u32[]{:S(2)}) copy-start(bf16[1,128,2048]{2,1,0:T(8,128)(2,1)} %param.19) | copy-start | bytes 1572868
  679.1 12.1 %copy-start.1 = (bf16[2048,128]{1,0:T(8,128)(2,1)S(1)}, bf16[2048,128]{1,0:T(8,128)(2,1)}, u32[]{:S(2)}) copy-start(bf16[2048,128]{1,0:T(8,128)(2,1)} %copy-done) | copy-start | bytes 1572868
  679.1 172.0 %collective-permute-start.2 = (bf16[1024,1024]{1,0:T(8,128)(2,1)}, bf16[1024,1024]{1,0:T(8,128)(2,1)}, u32[]{:S(2)}, u32[]{:S(2)}) collective-permute-start(bf16[1024,1024]{1,0:T(8,128)(2,1)} %fusion.3), channel_id=1, source_target_pairs={{0,16},{8,24},{16,0},{24,8},{1,17},{9,25},{17,1},{25,9},{2,18},{10... | collective-permute-start | bytes 6291464 | tf_op jit(solution)/shard_map/ppermute | solution.py:758
  682.0 143.8 %collective-permute-start.3 = (bf16[1024,384]{1,0:T(8,128)(2,1)}, bf16[1024,384]{1,0:T(8,128)(2,1)}, u32[]{:S(2)}, u32[]{:S(2)}) collective-permute-start(bf16[1024,384]{1,0:T(8,128)(2,1)} %fusion.19), channel_id=1, source_target_pairs={{0,16},{8,24},{16,0},{24,8},{1,17},{9,25},{17,1},{25,9},{2,18},{10... | collective-permute-start | bytes 2359304 | tf_op jit(solution)/shard_map/ppermute | solution.py:758
  688.0 160.2 %collective-permute-start.4 = (bf16[256,2048]{1,0:T(8,128)(2,1)}, bf16[256,2048]{1,0:T(8,128)(2,1)}, u32[]{:S(2)}, u32[]{:S(2)}) collective-permute-start(bf16[256,2048]{1,0:T(8,128)(2,1)} %fusion.12), channel_id=1, source_target_pairs={{0,16},{8,24},{16,0},{24,8},{1,17},{9,25},{17,1},{25,9},{2,18},{10... | collective-permute-start | bytes 3145736 | tf_op jit(solution)/shard_map/ppermute | solution.py:758
  690.6 160.5 %slice-start.2 = ((s8[8388608]{0:T(1024)(128)(4,1)}), s8[4194304]{0:T(1024)(128)(4,1)S(1)}, s32[]{:S(2)}) async-start(s8[8388608]{0:T(1024)(128)(4,1)} %bitcast.120), calls=%async_computation.2 | async-start | bytes 8388608
  691.3 134.5 %copy-start.30 = (f32[2048,384]{1,0:T(8,128)S(1)}, f32[2048,384]{1,0:T(8,128)}, u32[]{:S(2)}) copy-start(f32[2048,384]{1,0:T(8,128)} %fusion.20) | copy-start | bytes 9437188
  691.3 157.0 %copy-start.25 = (f32[512,2048]{1,0:T(8,128)S(1)}, f32[512,2048]{1,0:T(8,128)}, u32[]{:S(2)}) copy-start(f32[512,2048]{1,0:T(8,128)} %fusion.58) | copy-start | bytes 12582916
  691.3 159.8 %slice-start.3 = ((s8[8388608]{0:T(1024)(128)(4,1)}), s8[4194304]{0:T(1024)(128)(4,1)S(1)}, s32[]{:S(2)}) async-start(s8[8388608]{0:T(1024)(128)(4,1)} %bitcast.120), calls=%async_computation.3 | async-start | bytes 8388608
  (20 other events, 82.0 us)

commit v2 on v1

v2 whole, which is shorter than its diff:
```python
import functools

import jax
import jax.numpy as jnp
from jax import lax
from jax.experimental import pallas as pl
from jax.experimental.pallas import tpu as pltpu
from jax.sharding import PartitionSpec as P

HEAD = 128
epsilon = 1e-06
rope_base = 500000.0
MESH = pl.DeviceIdType.MESH
BF = jnp.bfloat16
F32 = jnp.float32
ANY = pl.BlockSpec(memory_space=pl.ANY)
VM = pl.BlockSpec(memory_space=pltpu.VMEM)
DMA = pltpu.SemaphoreType.DMA
LIGHT = pl.CostEstimate(flops=0, bytes_accessed=0, transcendentals=0)


class Plan:
    def __init__(self, mesh, heads):
        self.dp = mesh.shape["dp"]
        self.seq = mesh.shape["seq"]
        self.size = heads
        self.low = heads // self.seq
        self.groups = self.dp // self.low
        self.devices = self.dp * self.seq

    def here(self):
        dp = lax.axis_index("dp")
        seq = lax.axis_index("seq")
        return dp, seq, (dp % self.low) * self.seq + seq

    def member(self, dp, index):
        return (dp // self.low) * self.low + index // self.seq, index % self.seq

    def across(self, dp, seq, bit):
        if bit < self.seq:
            return dp, flip(seq, bit)
        return flip(dp, bit // self.seq), seq


def flip(value, bit):
    return value + bit * (1 - 2 * ((value // bit) % 2))


def flips(value, mask):
    bit = 1
    while bit <= mask:
        if mask & bit:
            value = flip(value, bit)
        bit *= 2
    return value


def greet(devices):
    barrier = pltpu.get_barrier_semaphore()
    for device in devices:
        pl.semaphore_signal(barrier, inc=1, device_id=device, device_id_type=MESH)
    pl.semaphore_wait(barrier, len(devices))


def greet_all(plan, dp, seq):
    barrier = pltpu.get_barrier_semaphore()
    me = dp * plan.seq + seq

    def hello(step, carry):
        other = (me + step) % plan.devices
        pl.semaphore_signal(
            barrier, inc=1, device_id=(other // plan.seq, other % plan.seq), device_id_type=MESH
        )
        return carry

    lax.fori_loop(1, plan.devices, hello, 0)
    pl.semaphore_wait(barrier, plan.devices - 1)


def greet_group(plan, dp, index):
    barrier = pltpu.get_barrier_semaphore()

    def hello(step, carry):
        other = plan.member(dp, (index + step) % plan.size)
        pl.semaphore_signal(barrier, inc=1, device_id=other, device_id_type=MESH)
        return carry

    lax.fori_loop(1, plan.size, hello, 0)
    pl.semaphore_wait(barrier, plan.size - 1)


def send(src, dst, send_sem, recv_sem, device):
    copy = pltpu.make_async_remote_copy(
        src_ref=src,
        dst_ref=dst,
        send_sem=send_sem,
        recv_sem=recv_sem,
        device_id=device,
        device_id_type=MESH,
    )
    copy.start()
    return copy


def wait_bytes(ref, sem):
    pltpu.make_async_copy(ref, ref, sem).wait()


def halves(rows):
    return ((0, rows // 2), (rows // 2, rows - rows // 2))


ORDERS = ((2, 4), (4, 2))


def gather_steps(plan, x, out, dp, seq, index, sems):
    far_send, far_recv, near_send, near_recv, core_send, core_recv, local = sems
    rows = x.shape[0]
    parts = halves(rows)
    copies = []

    def place(mask, part=None):
        start, count = (0, rows) if part is None else parts[part]
        return out.at[pl.ds(pl.multiple_of(flips(index, mask) * rows + start, 16), count)]

    def push(src, dst, send_sem, recv_sem, bit):
        copies.append(send(src, dst, send_sem, recv_sem, plan.across(dp, seq, bit)))

    def spread(src, mask):
        plane = mask // 8
        for bit in (2, 4):
            number = plane * 2 + bit // 4
            push(src, place(mask), near_send.at[number], near_recv.at[number], bit)
        push(src, place(mask), core_send.at[plane], core_recv.at[plane], 1)

    def begin():
        pltpu.make_async_copy(x, out.at[pl.ds(index * rows, rows)], local).start()
        push(x, place(0), far_send, far_recv, 8)
        spread(x, 0)

    def onward(plane):
        base = plane * 8
        for bit, other in ORDERS:
            number = plane * 2 + bit // 4
            wait_bytes(place(base | bit), near_recv.at[number])
            part = bit // 4
            push(
                place(base | bit, part),
                place(base | bit, part),
                near_send.at[4 + number],
                near_recv.at[4 + number],
                other,
            )
            push(
                place(base | bit),
                place(base | bit),
                core_send.at[2 + number],
                core_recv.at[2 + number],
                1,
            )

    def corner(plane):
        base = plane * 8
        for bit, _ in ORDERS:
            part = bit // 4
            number = plane * 2 + part
            wait_bytes(place(base | 6, part), near_recv.at[4 + number])
            push(
                place(base | 6, part),
                place(base | 6, part),
                core_send.at[6 + number],
                core_recv.at[6 + number],
                1,
            )

    def finish():
        onward(0)
        wait_bytes(place(8), far_recv)
        spread(place(8), 8)
        corner(0)
        onward(1)
        corner(1)
        for plane in range(2):
            base = plane * 8 + 1
            wait_bytes(place(base), core_recv.at[plane])
            for bit, _ in ORDERS:
                number = plane * 2 + bit // 4
                wait_bytes(place(base | bit), core_recv.at[2 + number])
                wait_bytes(place(base | 6, bit // 4), core_recv.at[6 + number])
        for copy in copies:
            copy.wait_send()
        pltpu.make_async_copy(x, out.at[pl.ds(index * rows, rows)], local).wait()

    return begin, finish


GATHER_SEMS = (DMA, DMA, DMA((8,)), DMA((8,)), DMA((10,)), DMA((10,)), DMA)


def gather_group(plan, x):
    rows, width = x.shape

    def kernel(x_ref, out_ref, *sems):
        dp, seq, index = plan.here()
        greet([plan.across(dp, seq, bit) for bit in (1, 2, 4, 8)])
        begin, finish = gather_steps(plan, x_ref, out_ref, dp, seq, index, sems)
        begin()
        finish()

    return pl.pallas_call(
        kernel,
        out_shape=jax.ShapeDtypeStruct((plan.size * rows, width), x.dtype),
        in_specs=[ANY],
        out_specs=ANY,
        scratch_shapes=list(GATHER_SEMS),
        compiler_params=pltpu.CompilerParams(collective_id=1, has_side_effects=True),
        cost_estimate=LIGHT,
        name="gather_group",
    )(x)


def scatter_steps(plan, dp, seq, index, pairs, turned, write, bufs, sems, meanwhile=None):
    theirs, mine, got_core, got_first, got_second, got_far = bufs
    core_send, core_recv, send_sems, recv_sems, far_send, far_recv = sems
    rows, width = got_far.shape
    tile = 512
    parts = halves(rows)
    copies = []

    def compute(dst, plane, core):
        starts = [flips(index, core | 2 * m | 8 * plane) * rows for m in range(4)]

        @pl.loop(0, width // tile)
        def _(j):
            columns = pl.ds(pl.multiple_of(j * tile, tile), tile)
            block = None
            for l_ref, r_ref in pairs:
                some = jnp.concatenate(
                    [l_ref[pl.ds(pl.multiple_of(start, rows), rows), :] for start in starts], axis=0
                )
                if turned:
                    part = contract_last(some, r_ref[columns, :])
                else:
                    part = dot(some, r_ref[:, columns])
                block = part if block is None else block + part
            dst[plane, :, :, columns] = block.astype(BF).reshape(4, rows, tile)

    def push(src, dst, send_sem, recv_sem, bit):
        copy = send(src, dst, send_sem, recv_sem, plan.across(dp, seq, bit))
        copies.append(copy)
        return copy

    def add(dst, src, count):
        @pl.loop(0, count // 16)
        def _(i):
            here = pl.ds(pl.multiple_of(i * 16, 16), 16)
            dst[here, :] = dst[here, :] + src[here, :]

    def to_core(plane):
        return push(
            theirs.at[plane], got_core.at[plane], core_send.at[plane], core_recv.at[plane], 1
        )

    def add_core(plane, copy):
        copy.wait_recv()
        for m in range(4):
            add(mine.at[plane, m], got_core.at[plane, m], rows)

    def first(plane):
        started = []
        for part, (bit, other) in enumerate(ORDERS):
            start, count = parts[part]
            for k, keep in enumerate((0, other)):
                number = plane * 6 + part * 2 + k
                buffer = got_first.at[plane, part * 2 + k]
                copy = push(
                    mine.at[plane, (keep | bit) // 2, pl.ds(start, count)],
                    buffer,
                    send_sems.at[number],
                    recv_sems.at[number],
                    bit,
                )
                started.append((copy, keep // 2, start, count, buffer))
        return started

    def second(plane):
        started = []
        for part, (bit, other) in enumerate(ORDERS):
            start, count = parts[part]
            number = plane * 6 + 4 + part
            buffer = got_second.at[plane, part]
            copy = push(
                mine.at[plane, other // 2, pl.ds(start, count)],
                buffer,
                send_sems.at[number],
                recv_sems.at[number],
                other,
            )
            started.append((copy, 0, start, count, buffer))
        return started

    def settle(plane, started):
        for copy, m, start, count, buffer in started:
            copy.wait_recv()
            add(mine.at[plane, m, pl.ds(start, count)], buffer, count)

    compute(theirs, 1, 1)
    core = to_core(1)
    compute(mine, 1, 0)
    add_core(1, core)
    far_first = first(1)
    compute(theirs, 0, 1)
    core = to_core(0)
    compute(mine, 0, 0)
    settle(1, far_first)
    far_second = second(1)
    add_core(0, core)
    near_first = first(0)
    if meanwhile is not None:
        meanwhile()
    settle(1, far_second)
    far = push(mine.at[1, 0], got_far, far_send, far_recv, 8)
    settle(0, near_first)
    near_second = second(0)
    settle(0, near_second)
    far.wait_recv()

    @pl.loop(0, rows // 16)
    def _(i):
        here = pl.ds(pl.multiple_of(i * 16, 16), 16)
        write(here, mine[0, 0, here, :].astype(F32) + got_far[here, :].astype(F32))

    for copy in copies:
        copy.wait_send()


def scatter_scratch(rows, width):
    block = (rows, width)
    half = (rows // 2, width)
    return [
        pltpu.VMEM((2, 4) + block, BF),
        pltpu.VMEM((2, 4) + block, BF),
        pltpu.VMEM((2, 4) + block, BF),
        pltpu.VMEM((2, 4) + half, BF),
        pltpu.VMEM((2, 2) + half, BF),
        pltpu.VMEM(block, BF),
        DMA((2,)),
        DMA((2,)),
        DMA((12,)),
        DMA((12,)),
        DMA,
        DMA,
    ]


def scatter_dot(plan, lefts, rights, turned, collective_id):
    rows = lefts[0].shape[0] // plan.size
    width = rights[0].shape[0] if turned else rights[0].shape[1]
    count = len(lefts)

    def kernel(*refs):
        pairs = list(zip(refs[:count], refs[count : 2 * count]))
        out_ref = refs[2 * count]
        rest = refs[2 * count + 1 :]
        dp, seq, index = plan.here()
        greet([plan.across(dp, seq, bit) for bit in (1, 2, 4, 8)])

        def write(here, value):
            out_ref[here, :] = value

        scatter_steps(plan, dp, seq, index, pairs, turned, write, rest[:6], rest[6:])

    return pl.pallas_call(
        kernel,
        out_shape=jax.ShapeDtypeStruct((rows, width), F32),
        in_specs=[VM] * (2 * count),
        out_specs=VM,
        scratch_shapes=scatter_scratch(rows, width),
        compiler_params=pltpu.CompilerParams(
            collective_id=collective_id, has_side_effects=True, vmem_limit_bytes=48 * 2**20
        ),
        cost_estimate=LIGHT,
        name="scatter_dot",
    )(*lefts, *rights)


def half_columns(plan, inner, blocks, half):
    wide = inner // blocks
    each = wide // plan.size
    return [(half * inner + block * wide, each, block * each) for block in range(blocks)]


def columns_out(plan, dp, index, w_ref, out_ref, table, send_sem, recv_sem):
    own = w_ref.shape[0]
    wide = out_ref.shape[1]
    rows = pl.ds(pl.multiple_of(index * own, own), own)

    def moves(other):
        for base, each, place in table:
            yield (
                w_ref.at[:, pl.ds(pl.multiple_of(base + other * each, 128), each)],
                out_ref.at[rows, pl.ds(place, each)],
            )

    def begin():
        def to(step, carry):
            other = (index + step) % plan.size
            for src, dst in moves(other):
                send(src, dst, send_sem, recv_sem, plan.member(dp, other))
            return carry

        lax.fori_loop(1, plan.size, to, 0)
        for src, dst in moves(index):
            pltpu.make_async_copy(src, dst, recv_sem).start()

    def finish():
        wait_bytes(out_ref, recv_sem)

        def sent(step, carry):
            wait_bytes(w_ref.at[:, pl.ds(0, wide)], send_sem)
            return carry

        lax.fori_loop(1, plan.size, sent, 0)

    return begin, finish


def columns_back(plan, dp, index, g_ref, out_ref, table, send_sem, recv_sem):
    own = g_ref.shape[0] // plan.size

    def moves(other):
        rows = pl.ds(pl.multiple_of(other * own, own), own)
        for base, each, place in table:
            yield (
                g_ref.at[rows, pl.ds(place, each)],
                out_ref.at[:, pl.ds(pl.multiple_of(base + index * each, 128), each)],
            )

    def begin():
        def to(step, carry):
            other = (index + step) % plan.size
            for src, dst in moves(other):
                send(src, dst, send_sem, recv_sem, plan.member(dp, other))
            return carry

        lax.fori_loop(1, plan.size, to, 0)
        for src, dst in moves(index):
            pltpu.make_async_copy(src, dst, recv_sem).start()

    def finish():
        wait_bytes(g_ref, recv_sem)

        def sent(step, carry):
            wait_bytes(g_ref.at[pl.ds(0, own)], send_sem)
            return carry

        lax.fori_loop(1, plan.size, sent, 0)

    return begin, finish


def start_gather(plan, x, attn_w, gate_up_w, gains, docs, blocks):
    rows, width = x.shape
    own, both = gate_up_w.shape
    table = half_columns(plan, both // 2, blocks, 0)

    def kernel(x_ref, w_ref, u_ref, g_ref, d_ref, xo, wo, uo, go, do, *sems):
        gather_sems = sems[:7]
        w_send, w_recv, u_send, u_recv, g_send, g_recv, d_send, d_recv = sems[7:]
        dp, seq, index = plan.here()
        me = dp * plan.seq + seq
        greet_all(plan, dp, seq)
        begin, finish = gather_steps(plan, x_ref, xo, dp, seq, index, gather_sems)
        begin()
        group = dp // plan.low
        def columns(part, other):
            return pl.ds(pl.multiple_of(part * width + other * HEAD, HEAD), HEAD)

        mine = pl.ds(me * own, own)

        def w_to(away, step, carry):
            other = (index + step) % plan.size
            to_group = (group + away) % plan.groups
            device = (to_group * plan.low + other // plan.seq, other % plan.seq)
            for part in range(3):
                send(
                    w_ref.at[:, columns(part, other)],
                    wo.at[mine, pl.ds(part * HEAD, HEAD)],
                    w_send,
                    w_recv,
                    device,
                )
            return carry

        for away in range(1, plan.groups):
            lax.fori_loop(0, plan.size, functools.partial(w_to, away), 0)
        lax.fori_loop(1, plan.size, functools.partial(w_to, 0), 0)
        for part in range(3):
            pltpu.make_async_copy(
                w_ref.at[:, columns(part, index)], wo.at[mine, pl.ds(part * HEAD, HEAD)], w_recv
            ).start()

        def g_to(step, carry):
            other = (me + step) % plan.devices
            send(g_ref, go.at[me], g_send, g_recv, (other // plan.seq, other % plan.seq))
            return carry

        lax.fori_loop(1, plan.devices, g_to, 0)
        pltpu.make_async_copy(g_ref, go.at[me], g_recv).start()

        def d_to(step, carry):
            send(d_ref, do.at[index], d_send, d_recv, plan.member(dp, (index + step) % plan.size))
            return carry

        lax.fori_loop(1, plan.size, d_to, 0)
        pltpu.make_async_copy(d_ref, do.at[index], d_recv).start()
        begin_u, finish_u = columns_out(plan, dp, index, u_ref, uo, table, u_send, u_recv)
        begin_u()
        finish()
        finish_u()
        wait_bytes(go, g_recv)
        wait_bytes(do, d_recv)
        wait_bytes(wo, w_recv)

        def sent(step, carry):
            wait_bytes(w_ref.at[:, pl.ds(0, 3 * HEAD)], w_send)
            wait_bytes(g_ref, g_send)
            return carry

        lax.fori_loop(1, plan.devices, sent, 0)

        def sent_docs(step, carry):
            wait_bytes(d_ref, d_send)
            return carry

        lax.fori_loop(1, plan.size, sent_docs, 0)

    shapes = (
        ((plan.size * rows, width), BF),
        ((plan.devices * own, 3 * HEAD), BF),
        ((plan.size * own, both // 2 // plan.size), BF),
        ((plan.devices,) + gains.shape, gains.dtype),
        ((plan.size,) + docs.shape, docs.dtype),
    )
    return pl.pallas_call(
        kernel,
        out_shape=[jax.ShapeDtypeStruct(*shape) for shape in shapes],
        in_specs=[ANY] * 5,
        out_specs=[ANY] * 5,
        scratch_shapes=list(GATHER_SEMS) + [DMA] * 8,
        compiler_params=pltpu.CompilerParams(collective_id=0, has_side_effects=True),
        cost_estimate=LIGHT,
        name="start_gather",
    )(x, attn_w, gate_up_w, gains, docs)


def dot(left, right):
    return jnp.dot(left, right, preferred_element_type=F32)


def contract_last(left, right):
    return lax.dot_general(left, right, (((1,), (1,)), ((), ())), preferred_element_type=F32)


def contract_first(left, right):
    return lax.dot_general(left, right, (((0,), (0,)), ((), ())), preferred_element_type=F32)


def row_sums(values):
    ones = jnp.ones((8, values.shape[1]), F32)
    sums = lax.dot_general(
        ones,
        values,
        (((1,), (1,)), ((), ())),
        precision=lax.Precision.HIGHEST,
        preferred_element_type=F32,
    )
    return sums[:1]


def spread_sums(rows):
    ones = jnp.ones((rows.shape[0], HEAD), F32)
    return lax.dot_general(
        rows,
        ones,
        (((0,), (0,)), ((), ())),
        precision=lax.Precision.HIGHEST,
        preferred_element_type=F32,
    )


STEP = 256


def scores_of(q, k, q_docs, k_docs, start):
    scores = contract_last(q, k) * HEAD ** (-0.5)
    row = start + lax.broadcasted_iota(jnp.int32, scores.shape, 0)
    column = lax.broadcasted_iota(jnp.int32, scores.shape, 1)
    allowed = (column <= row) & (q_docs == k_docs)
    scores = jnp.where(allowed, scores, -1e30)
    top = jnp.max(scores, axis=1, keepdims=True)
    weights = jnp.exp(scores - top)
    return weights / jnp.sum(weights, axis=1, keepdims=True)


def swap_sums(plan, dp, index, mine, held, s_sem, r_sem):
    def begin():
        def to(step, carry):
            send(mine, held.at[index], s_sem, r_sem, plan.member(dp, (index + step) % plan.size))
            return carry

        pltpu.make_async_copy(mine, held.at[index], r_sem).start()
        lax.fori_loop(1, plan.size, to, 0)

    def finish():
        wait_bytes(held, r_sem)
        wait_bytes(held.at[pl.ds(0, plan.size - 1)], s_sem)

    return begin, finish


def attend_forward(
    plan, x_all, w_qkv, attn_w, gate_up_w, gains, docs_column, docs_row, cosine, sine, blocks
):
    tokens, width = x_all.shape
    length = cosine.shape[0]
    own, both = gate_up_w.shape
    table = half_columns(plan, both // 2, blocks, 1)

    def kernel(x, wq, aw, up, gn, dc, dr, cs, sn, wo, uo, q, k, rq, rk, ql, kl, vl, mixed, *rest):
        stats, held, t_send, t_recv, o_send, o_recv, u_send, u_recv = rest
        dp, seq, index = plan.here()
        me = dp * plan.seq + seq
        group = dp // plan.low
        greet_all(plan, dp, seq)
        @pl.loop(0, tokens // STEP)
        def _(i):
            rows = pl.ds(pl.multiple_of(i * STEP, STEP), STEP)
            block = dot(x[rows, :], wq[...])
            q[rows, :] = block[:, :HEAD]
            k[rows, :] = block[:, HEAD : 2 * HEAD]
            vl[rows, :] = block[:, 2 * HEAD :].astype(BF)
            stats[0, :, rows] = row_sums(block[:, :HEAD] * block[:, :HEAD])
            stats[1, :, rows] = row_sums(block[:, HEAD : 2 * HEAD] * block[:, HEAD : 2 * HEAD])

        begin, finish = swap_sums(plan, dp, index, stats, held, t_send, t_recv)
        begin()
        feature = me * own
        head = feature // HEAD
        o_dst = wo.at[pl.ds(pl.multiple_of(feature % HEAD, own), own)]
        o_src = aw.at[:, pl.ds(3 * width, width)]

        def o_to(away, carry):
            to_group = (group + away) % plan.groups
            to_dp, to_seq = to_group * plan.low + head // plan.seq, head % plan.seq
            same = to_dp * plan.seq + to_seq == me

            @pl.when(same)
            def _():
                pltpu.make_async_copy(o_src, o_dst, o_recv).start()

            @pl.when(jnp.logical_not(same))
            def _():
                send(o_src, o_dst, o_send, o_recv, (to_dp, to_seq))

            return carry

        lax.fori_loop(0, plan.groups, o_to, 0)
        begin_u, finish_u = columns_out(plan, dp, index, up, uo, table, u_send, u_recv)
        begin_u()
        finish()

        @pl.loop(0, tokens // STEP)
        def _(i):
            rows = pl.ds(pl.multiple_of(i * STEP, STEP), STEP)
            places = pl.ds(pl.multiple_of((i % (length // STEP)) * STEP, STEP), STEP)
            for which, raw, factor, low in ((0, q, rq, ql), (1, k, rk, kl)):
                r = lax.rsqrt(spread_sums(held[:, which, 0, rows]) / width + epsilon)
                factor[rows, :] = r
                values = raw[rows, :] * r * gn[which : which + 1, :]
                turned = values * cs[places, :] + pltpu.roll(values, HEAD // 2, 1) * sn[places, :]
                low[rows, :] = turned.astype(BF)

        @pl.loop(0, tokens // length)
        def _(b):
            for j in range(length // STEP):
                start = pl.multiple_of(b * length + j * STEP, STEP)
                rows = pl.ds(start, STEP)
                keys = pl.ds(pl.multiple_of(b * length, length), (j + 1) * STEP)
                probs = scores_of(
                    ql[rows, :], kl[keys, :], dc[rows, :], dr[b, :, : (j + 1) * STEP], j * STEP
                )
                mixed[rows, :] = dot(probs.astype(BF), vl[keys, :]).astype(BF)

        wait_bytes(wo, o_recv)
        finish_u()

        def sent_o(away, carry):
            to_group = (group + away) % plan.groups
            to_dp, to_seq = to_group * plan.low + head // plan.seq, head % plan.seq

            @pl.when(to_dp * plan.seq + to_seq != me)
            def _():
                wait_bytes(o_src, o_send)

            return carry

        lax.fori_loop(0, plan.groups, sent_o, 0)

    per_head = (tokens, HEAD)
    shapes = (
        ((HEAD, width), BF),
        ((plan.size * own, both // 2 // plan.size), BF),
        (per_head, F32),
        (per_head, F32),
        (per_head, F32),
        (per_head, F32),
        (per_head, BF),
        (per_head, BF),
        (per_head, BF),
        (per_head, BF),
    )
    return pl.pallas_call(
        kernel,
        out_shape=[jax.ShapeDtypeStruct(*shape) for shape in shapes],
        in_specs=[VM, VM, ANY, ANY] + [VM] * 5,
        out_specs=[ANY, ANY] + [VM] * 8,
        scratch_shapes=[
            pltpu.VMEM((2, 1, tokens), F32),
            pltpu.VMEM((plan.size, 2, 1, tokens), F32),
        ]
        + [DMA] * 6,
        compiler_params=pltpu.CompilerParams(
            collective_id=3, has_side_effects=True, vmem_limit_bytes=56 * 2**20
        ),
        cost_estimate=LIGHT,
        name="attend_forward",
    )(x_all, w_qkv, attn_w, gate_up_w, gains, docs_column, docs_row, cosine, sine)


def attend_backward(
    plan,
    b_all,
    w_out,
    q,
    k,
    rq,
    rk,
    ql,
    kl,
    vl,
    mixed,
    gains,
    docs_column,
    docs_row,
    cosine,
    sine,
    g_gate,
    g_up,
    blocks,
):
    tokens, width = b_all.shape
    own = g_gate.shape[0] // plan.size
    inner = g_gate.shape[1] * plan.size
    length = cosine.shape[0]
    scale = HEAD ** (-0.5)

    def kernel(*refs):
        ba, wo, q, k, rq, rk, ql, kl, vl, mx, gn, dc, dr, cs, sn, gg, gu = refs[:17]
        dqkv, g_out, g_gain, gu_out = refs[17:21]
        dq, dk, dv, gm, stats, held, t_send, t_recv, gg_send, gg_recv, gu_send, gu_recv = refs[21:]
        dp, seq, index = plan.here()
        greet_group(plan, dp, index)
        begin_g, finish_g = columns_back(
            plan, dp, index, gg, gu_out, half_columns(plan, inner, blocks, 0), gg_send, gg_recv
        )
        begin_u, finish_u = columns_back(
            plan, dp, index, gu, gu_out, half_columns(plan, inner, blocks, 1), gu_send, gu_recv
        )
        begin_g()
        begin_u()
        dk[...] = jnp.zeros_like(dk)
        dv[...] = jnp.zeros_like(dv)

        @pl.loop(0, tokens // STEP)
        def _(i):
            rows = pl.ds(pl.multiple_of(i * STEP, STEP), STEP)
            gm[rows, :] = contract_last(ba[rows, :], wo[...]).astype(BF)

        @pl.loop(0, tokens // length)
        def _(b):
            for j in range(length // STEP):
                rows = pl.ds(pl.multiple_of(b * length + j * STEP, STEP), STEP)
                keys = pl.ds(pl.multiple_of(b * length, length), (j + 1) * STEP)
                probs = scores_of(
                    ql[rows, :], kl[keys, :], dc[rows, :], dr[b, :, : (j + 1) * STEP], j * STEP
                )
                grad = gm[rows, :]
                grad_probs = contract_last(grad, vl[keys, :])
                delta = jnp.sum(probs * grad_probs, axis=1, keepdims=True)
                grad_scores = (probs * (grad_probs - delta)).astype(BF)
                dq[rows, :] = dot(grad_scores, kl[keys, :]) * scale
                dk[keys, :] += contract_first(grad_scores, ql[rows, :]) * scale
                dv[keys, :] += contract_first(probs.astype(BF), grad)

        @pl.loop(0, tokens // STEP)
        def _(i):
            rows = pl.ds(pl.multiple_of(i * STEP, STEP), STEP)
            places = pl.ds(pl.multiple_of((i % (length // STEP)) * STEP, STEP), STEP)
            for which, raw, grad in ((0, q, dq), (1, k, dk)):
                values = grad[rows, :]
                turned = values * cs[places, :] - pltpu.roll(values, HEAD // 2, 1) * sn[places, :]
                grad[rows, :] = turned
                stats[which, :, rows] = row_sums(turned * gn[which : which + 1, :] * raw[rows, :])

        begin, finish = swap_sums(plan, dp, index, stats, held, t_send, t_recv)
        begin()
        turned_mixed = mx[...].T

        @pl.loop(0, width // 512)
        def _(i):
            columns = pl.ds(pl.multiple_of(i * 512, 512), 512)
            g_out[:, columns] = dot(turned_mixed, ba[:, columns]).astype(BF)

        g_gain[...] = jnp.zeros_like(g_gain)
        finish()

        @pl.loop(0, tokens // STEP)
        def _(i):
            rows = pl.ds(pl.multiple_of(i * STEP, STEP), STEP)
            for which, raw, factor, grad in ((0, q, rq, dq), (1, k, rk, dk)):
                total = spread_sums(held[:, which, 0, rows])
                r = factor[rows, :]
                u = raw[rows, :]
                e = grad[rows, :]
                back = r * (gn[which : which + 1, :] * e) - u * (r * r * r * (total / width))
                dqkv[rows, pl.ds(which * HEAD, HEAD)] = back.astype(BF)
                g_gain[which : which + 1, :] += jnp.sum(e * u * r, axis=0, keepdims=True)
            dqkv[rows, pl.ds(2 * HEAD, HEAD)] = dv[rows, :].astype(BF)

        finish_g()
        finish_u()

    per_head = (tokens, HEAD)
    shapes = (
        ((tokens, 3 * HEAD), BF),
        ((HEAD, width), BF),
        ((8, HEAD), F32),
        ((own, 2 * inner), BF),
    )
    return pl.pallas_call(
        kernel,
        out_shape=[jax.ShapeDtypeStruct(*shape) for shape in shapes],
        in_specs=[VM] * 15 + [ANY] * 2,
        out_specs=[VM] * 3 + [ANY],
        scratch_shapes=[
            pltpu.VMEM(per_head, F32),
            pltpu.VMEM(per_head, F32),
            pltpu.VMEM(per_head, F32),
            pltpu.VMEM(per_head, BF),
            pltpu.VMEM((2, 1, tokens), F32),
            pltpu.VMEM((plan.size, 2, 1, tokens), F32),
        ]
        + [DMA] * 6,
        compiler_params=pltpu.CompilerParams(
            collective_id=4, has_side_effects=True, vmem_limit_bytes=56 * 2**20
        ),
        cost_estimate=LIGHT,
        name="attend_backward",
    )(
        b_all,
        w_out,
        q,
        k,
        rq,
        rk,
        ql,
        kl,
        vl,
        mixed,
        gains,
        docs_column,
        docs_row,
        cosine,
        sine,
        g_gate,
        g_up,
    )


def finish_backward(plan, dqkv, w_qkv, x_all, g_out, gains, before):
    tokens, width = x_all.shape
    own = width // plan.devices
    rows = tokens // plan.size
    pieces = HEAD // own
    tile = 256

    def kernel(dq, wq, x, go, ga, bf, ig, w_grad, ga_out, *rest):
        bufs, sems = rest[:6], rest[6:12]
        turned, gq, got_q, got_o = rest[12:16]
        q_s, q_r, o_s, o_r, ga_s, ga_r = rest[16:]
        dp, seq, index = plan.here()
        me = dp * plan.seq + seq
        group = dp // plan.low
        greet_all(plan, dp, seq)

        def device_of(flat):
            return flat // plan.seq, flat % plan.seq

        def o_to(piece, carry):
            other = index * pieces + piece
            src = go.at[pl.ds(pl.multiple_of(piece * own, own), own)]

            @pl.when(other == me)
            def _():
                pltpu.make_async_copy(src, got_o.at[group], o_r).start()

            @pl.when(other != me)
            def _():
                send(src, got_o.at[group], o_s, o_r, device_of(other))

            return carry

        def ga_to(step, carry):
            other = (me + step) % plan.devices
            send(ga.at[other], ga_out.at[me], ga_s, ga_r, device_of(other))
            return carry

        def weights():
            turned[...] = dq[...].T

            @pl.loop(0, width // tile)
            def _(i):
                columns = pl.ds(pl.multiple_of(i * tile, tile), tile)
                block = dot(turned[...], x[:, columns])
                gq[columns, :] = block.T.astype(BF)

                def q_to(piece, carry):
                    other = i * (tile // own) + piece
                    src = gq.at[pl.ds(pl.multiple_of(other * own, own), own)]

                    @pl.when(other == me)
                    def _():
                        pltpu.make_async_copy(src, got_q.at[group, index], q_r).start()

                    @pl.when(other != me)
                    def _():
                        send(src, got_q.at[group, index], q_s, q_r, device_of(other))

                    return carry

                lax.fori_loop(0, tile // own, q_to, 0)

            lax.fori_loop(0, pieces, o_to, 0)
            lax.fori_loop(1, plan.devices, ga_to, 0)
            pltpu.make_async_copy(ga.at[me], ga_out.at[me], ga_r).start()

        def write(here, value):
            ig[here, :] = bf[here, :] + value

        scatter_steps(plan, dp, seq, index, [(dq, wq)], True, write, bufs, sems, weights)
        wait_bytes(got_o, o_r)
        wait_bytes(got_q, q_r)
        for part in range(3):
            for member in range(plan.size):
                total = got_q[0, member, :, part * HEAD : (part + 1) * HEAD].astype(F32)
                for other in range(1, plan.groups):
                    total = total + got_q[
                        other, member, :, part * HEAD : (part + 1) * HEAD
                    ].astype(F32)
                w_grad[:, pl.ds(part * width + member * HEAD, HEAD)] = total
        total = got_o[0].astype(F32)
        for other in range(1, plan.groups):
            total = total + got_o[other].astype(F32)
        w_grad[:, pl.ds(3 * width, width)] = total
        wait_bytes(ga_out, ga_r)
        wait_bytes(ga_out.at[pl.ds(0, plan.devices - 1)], ga_s)
        wait_bytes(gq.at[pl.ds(0, width - own)], q_s)

        def sent_o(piece, carry):
            @pl.when(index * pieces + piece != me)
            def _():
                wait_bytes(go.at[pl.ds(0, own)], o_s)

            return carry

        lax.fori_loop(0, pieces, sent_o, 0)

    shapes = (
        ((rows, width), F32),
        ((own, 4 * width), F32),
        (gains.shape, F32),
    )
    return pl.pallas_call(
        kernel,
        out_shape=[jax.ShapeDtypeStruct(*shape) for shape in shapes],
        in_specs=[VM] * 6,
        out_specs=[VM] * 3,
        scratch_shapes=scatter_scratch(rows, width)
        + [
            pltpu.VMEM((3 * HEAD, tokens), BF),
            pltpu.VMEM((width, 3 * HEAD), BF),
            pltpu.VMEM((plan.groups, plan.size, own, 3 * HEAD), BF),
            pltpu.VMEM((plan.groups, own, width), BF),
        ]
        + [DMA] * 6,
        compiler_params=pltpu.CompilerParams(
            collective_id=5, has_side_effects=True, vmem_limit_bytes=60 * 2**20
        ),
        cost_estimate=LIGHT,
        name="finish_backward",
    )(dqkv, w_qkv, x_all, g_out, gains, before)


def per_device(
    plan,
    hidden_in,
    segments,
    attn_weights,
    q_gain,
    k_gain,
    attn_gain,
    ffn_gain,
    gate_up_weights,
    down_weights,
    cotangent,
):
    x = hidden_in[0]
    rows, width = x.shape
    own = attn_weights.shape[0]
    inner = gate_up_weights.shape[1] // 2
    length = rows * plan.seq
    tokens = rows * plan.size
    groups = plan.groups
    dp, seq, index = plan.here()
    me = dp * plan.seq + seq
    group = dp // plan.low
    direct = (inner // (groups * plan.size)) % 128 == 0
    blocks = groups if direct else 1

    across = [[low + high * plan.low for high in range(groups)] for low in range(plan.low)]

    def join_groups(value):
        return lax.all_gather(value, "dp", axis_index_groups=across, axis=0, tiled=True)

    def sum_groups(value):
        return lax.psum_scatter(
            value.astype(BF), "dp", axis_index_groups=across, scatter_dimension=0, tiled=True
        )

    gains_mine = jnp.stack([q_gain, k_gain, attn_gain, ffn_gain]).astype(F32)
    gains_mine = jnp.pad(gains_mine, ((0, 4), (0, 128 - own)))
    docs_mine = jnp.broadcast_to(segments, (8, rows))
    x_all, w_qkv, gate_part, gains_all, docs_all = start_gather(
        plan, x, attn_weights, gate_up_weights, gains_mine, docs_mine, blocks
    )
    w_gate = join_groups(gate_part)
    gains = jnp.transpose(gains_all[:, :4, :own], (1, 0, 2)).reshape(4, width)
    docs = docs_all[:, 0, :].reshape(tokens)
    docs_column = docs.reshape(tokens, 1)
    docs_row = docs.reshape(tokens // length, 1, length)
    my_gains = lax.dynamic_slice_in_dim(gains[:2], index * HEAD, HEAD, 1)
    positions = jnp.arange(length, dtype=jnp.int32).astype(F32)
    half = HEAD // 2
    frequency = rope_base ** (-2.0 * jnp.arange(half, dtype=F32) / HEAD)
    angles = positions[:, None] * frequency[None, :]
    cosine = jnp.concatenate([jnp.cos(angles)] * 2, axis=1)
    sine = jnp.concatenate([-jnp.sin(angles), jnp.sin(angles)], axis=1)

    w_out, up_part, q, k, rq, rk, q_low, k_low, v_low, mixed = attend_forward(
        plan,
        x_all,
        w_qkv,
        attn_weights,
        gate_up_weights,
        my_gains,
        docs_column,
        docs_row,
        cosine,
        sine,
        blocks,
    )
    w_up = join_groups(up_part)
    down_weights, _ = lax.optimization_barrier((down_weights, up_part))
    if direct:
        w_down = join_groups(down_weights)
    else:
        w_all = lax.all_gather(down_weights, ("dp", "seq"), axis=0, tiled=True)
        each = inner // plan.size
        w_down = lax.dynamic_slice_in_dim(w_all, index * each, each, 0)
    branch = scatter_dot(plan, [mixed], [w_out], False, 2)

    def rms(values):
        return lax.rsqrt(jnp.mean(values * values, axis=1, keepdims=True) + epsilon)

    def rms_back(values, r, gain, grad):
        scaled = gain * grad
        inner_sum = jnp.mean(scaled * values, axis=1, keepdims=True)
        return r * scaled - values * (r * r * r * inner_sum), jnp.sum(grad * values * r, axis=0)

    branch_r = rms(branch)
    hidden = x.astype(F32) + branch * branch_r * gains[2]
    hidden_low = hidden.astype(BF)

    h_all = gather_group(plan, hidden_low)
    mine = inner // plan.size
    gate = dot(h_all, w_gate)
    up = dot(h_all, w_up)
    act = (jax.nn.silu(gate) * up).astype(BF)
    down = scatter_dot(plan, [act], [w_down], False, 6)
    down_r = rms(down)
    output = (hidden + down * down_r * gains[3]).astype(BF)

    grad_out = cotangent[0].astype(F32)
    grad_down_in, grad_fg = rms_back(down, down_r, gains[3], grad_out)
    d_all = gather_group(plan, grad_down_in.astype(BF))
    grad_act = contract_last(d_all, w_down)
    sigma = jax.nn.sigmoid(gate)
    grad_gate = (grad_act * up * sigma * (1.0 + gate * (1.0 - sigma))).astype(BF)
    grad_up = (grad_act * (gate * sigma)).astype(BF)
    g_gate = contract_first(h_all, grad_gate).astype(BF)
    g_up = contract_first(h_all, grad_up).astype(BF)
    g_down = contract_first(act, d_all).astype(BF)
    grad_gate, grad_up, g_gate, g_up, g_down = lax.optimization_barrier(
        (grad_gate, grad_up, g_gate, g_up, g_down)
    )
    g_gate = sum_groups(g_gate)
    g_up = sum_groups(g_up)
    if direct:
        grad_down = sum_groups(g_down).astype(F32)
    else:
        spread = jnp.zeros((inner, width), BF)
        spread = lax.dynamic_update_slice_in_dim(spread, g_down, index * mine, 0)
        grad_down = lax.psum_scatter(
            spread, ("dp", "seq"), scatter_dimension=0, tiled=True
        ).astype(F32)
    grad_hidden = grad_out + scatter_dot(
        plan, [grad_gate, grad_up], [w_gate, w_up], True, 7
    )

    grad_branch, grad_ag = rms_back(branch, branch_r, gains[2], grad_hidden)
    b_all = gather_group(plan, grad_branch.astype(BF))
    dqkv, g_out, g_head, gu_rows = attend_backward(
        plan,
        b_all,
        w_out,
        q,
        k,
        rq,
        rk,
        q_low,
        k_low,
        v_low,
        mixed,
        my_gains,
        docs_column,
        docs_row,
        cosine,
        sine,
        g_gate,
        g_up,
        blocks,
    )

    def for_head(values):
        whole = jnp.zeros((width,), F32)
        return lax.dynamic_update_slice_in_dim(whole, values, index * HEAD, 0)

    gain_parts = jnp.stack([for_head(g_head[0]), for_head(g_head[1]), grad_ag, grad_fg])
    gain_parts = jnp.transpose(gain_parts.reshape(4, plan.devices, own), (1, 0, 2))
    gain_parts = jnp.pad(gain_parts, ((0, 0), (0, 4), (0, 128 - own)))
    input_grad, grad_attn, gain_rows = finish_backward(
        plan, dqkv, w_qkv, x_all, g_out, gain_parts, grad_hidden
    )
    grad_gate_up = gu_rows.astype(F32)
    gain_grads = jnp.sum(gain_rows, axis=0)[:4, :own]
    return (
        output[None],
        input_grad[None],
        grad_attn,
        grad_gate_up,
        grad_down,
        gain_grads[0],
        gain_grads[1],
        gain_grads[2],
        gain_grads[3],
    )


def solution(mesh):
    by_token = P("dp", "seq", None)
    by_row = P(("dp", "seq"), None)
    by_gain = P(("dp", "seq"))

    def run(hidden_in, segments, attn_weights, *rest):
        plan = Plan(mesh, hidden_in.shape[2] // HEAD)
        return jax.shard_map(
            functools.partial(per_device, plan),
            mesh=mesh,
            in_specs=(by_token, P("dp", "seq"), by_row)
            + (by_gain,) * 4
            + (by_row, by_row, by_token),
            out_specs=(by_token, by_token, by_row, by_row, by_row) + (by_gain,) * 4,
            check_vma=False,
        )(hidden_in, segments, attn_weights, *rest)

    return run
```

time: 937 us -> 724 us (0.77)
  waiting for transfers between devices: 149 us -> 1.83 us
  matrix products: 98.2 us -> 66.7 us
  other arithmetic: 41.3 us -> 15.7 us
  between operations: 2.01 us -> 14.8 us
    ppermute x5 -> x0, waiting for transfers between devices: 149 us -> none  [from_group(): lax.ppermute(value, 'dp', [(i, (i + step) % plan.dp) for i in range(plan....]
    pallas_call x1, Pallas kernels: 186 us -> 75 us  [start_gather(): pl.pallas_call(kernel, out_shape=[jax.ShapeDtypeStruct(*shape) for shape...]
    pallas_call x10 -> x6, Pallas kernels: 308 us -> 376 us  [the longest x3 175 us: scatter_dot(): pl.pallas_call(kernel, out_shape=jax.ShapeDtypeStruct((rows, width), F32)...]
    pallas_call x3, Pallas kernels: 110 us -> 144 us  [gather_group(): pl.pallas_call(kernel, out_shape=jax.ShapeDtypeStruct((plan.size * rows,...]
    dot_general x4 -> x1, matrix products: 34.7 us -> 13.8 us  [contract_last(): lax.dot_general(left, right, (((1,), (1,)), ((), ())), preferred_element_...]
    dot_general x4 -> x3, matrix products: 35.2 us -> 29.4 us  [contract_first(): lax.dot_general(left, right, (((0,), (0,)), ((), ())), preferred_element_...]
    dot_general x4 -> x2, matrix products: 28.2 us -> 23.5 us  [dot(): return jnp.dot(left, right, preferred_element_type=F32)]
  transfers between devices with their start and end apart: 5 -> 6, of which waited for: 2 -> 0; matrix products, arithmetic and copies ran while one was open for 5% -> 6% of each run, Pallas kernels for 30% -> 60%
where the time goes in v2:
time: 724 us; the launch traced here: 716 us
  Pallas kernels  595 us (82%)
  matrix products  66.7 us (9%)
  local copies, waits for them, and re-layouts  21.4 us (3%)
  other arithmetic  15.7 us (2%)
  between operations  14.8 us (2%)
    pallas_call x3, Pallas kernels, scatter_dot(): pl.pallas_call(kernel, out_shape=jax.ShapeDtypeStruct((rows, width), F32)...  175 us
    pallas_call x3, Pallas kernels, gather_group(): pl.pallas_call(kernel, out_shape=jax.ShapeDtypeStruct((plan.size * rows,...  144 us
    pallas_call x1, Pallas kernels, finish_backward(): pl.pallas_call(kernel, out_shape=[jax.ShapeDtypeStruct(*shape) for shape...  86.7 us
    pallas_call x1, Pallas kernels, start_gather(): pl.pallas_call(kernel, out_shape=[jax.ShapeDtypeStruct(*shape) for shape...  75 us
    pallas_call x1, Pallas kernels, attend_backward(): pl.pallas_call(kernel, out_shape=[jax.ShapeDtypeStruct(*shape) for shape...  61 us
    pallas_call x1, Pallas kernels, attend_forward(): pl.pallas_call(kernel, out_shape=[jax.ShapeDtypeStruct(*shape) for shape...  53.1 us
    dot_general x3, matrix products, contract_first(): lax.dot_general(left, right, (((0,), (0,)), ((), ())), preferred_element_...  29.4 us
    dot_general x2, matrix products, dot(): return jnp.dot(left, right, preferred_element_type=F32)  23.5 us
  transfers between devices with their start and end apart: 6, of which 0 were waited for; matrix products, arithmetic and copies ran while one was open for 6% of the time, Pallas kernels for 60%

profile of v2, /device:TPU:15, one launch (start us, length us, event | category | flops | bytes accessed | tf_op | source)
XLA Modules:
  0.0 716.0 jit_solution(538615045162675018)
XLA Ops:
  7.2 1.3 fusion.20.g_ref
  8.5 1.2 broadcast_in_dim.9.d_ref
  9.8 75.0 %start_gather.1 = (bf16[2048,2048]{1,0:T(8,128)(2,1)}, bf16[2048,384]{1,0:T(8,128)(2,1)}, bf16[1024,512]{1,0:T(8,128)(2,1)}, f32[32,8,128]{2,1,0:T(8,128)}, s32[16,8,128]{2,1,0:T(8,128)}) custom-call(bf16[128,2048]{1,0:T(8,128)(2,1)} %bitcast.45, bf16[64,8192]{1,0:T(8,128)(2,1)} %aw.1, bf16[64,16384]{1,0:T(8,128)(2,1)} %up.1, f32[8,128]{1,0:T(8,128)} %fusion.20.g_ref, ...), custom_call_target="tpu_custom_call" | custom-call | tf_op jit(solution)/shard_map/start_gather/pallas_call | solution.py:545
  85.9 1.4 fusion.26
  87.4 1.3 copy.21.dc.refs_11_
  89.3 1.9 fusion.10
  91.2 1.4 pad_maximum_fusion
  92.6 53.1 %attend_forward.1 = (bf16[128,2048]{1,0:T(8,128)(2,1)}, bf16[1024,512]{1,0:T(8,128)(2,1)}, f32[2048,128]{1,0:T(8,128)}, f32[2048,128]{1,0:T(8,128)}, f32[2048,12...) custom-call(bf16[2048,2048]{1,0:T(8,128)(2,1)} %get-tuple-element.37, ...), custom_call_target="tpu_custom_call" | custom-call | tf_op jit(solution)/shard_map/attend_forward/pallas_call | solution.py:723
  148.1 1.0 copy-done.3
  149.2 69.3 %scatter_dot.3 = f32[128,2048]{1,0:T(8,128)S(1)} custom-call(bf16[2048,128]{1,0:T(8,128)(2,1)S(1)} %copy-done.3, bf16[128,2048]{1,0:T(8,128)(2,1)S(1)} %copy-done.2), custom_call_target="tpu_custom_call" | custom-call | tf_op jit(solution)/shard_map/scatter_dot/pallas_call | solution.py:373
  219.7 52.5 %gather_group.3 = bf16[2048,2048]{1,0:T(8,128)(2,1)} custom-call(bf16[128,2048]{1,0:T(8,128)(2,1)} %fusion.8.x_ref), custom_call_target="tpu_custom_call" | custom-call | tf_op jit(solution)/shard_map/gather_group/pallas_call | solution.py:210
  272.3 10.5 %fusion.27 = f32[2048,512]{1,0:T(8,128)} fusion(bf16[2048,2048]{1,0:T(8,128)(2,1)} %gather_group.3, bf16[2048,512]{1,0:T(8,128)(2,1)} %all-gather.4.cloned.1.call-done.refs_2_), kind=kOutput, calls=%fused_computation.68 | convolution fusion | flops 4294967296 | bytes 14680064 | tf_op jit(solution)/shard_map/dot_general | solution.py:558
  282.9 13.0 %multiply_convert_fusion.2 = (bf16[2048,512]{1,0:T(8,128)(2,1)}, f32[2048,512]{1,0:T(8,128)}) fusion(f32[2048,512]{1,0:T(8,128)} %fusion.27, bf16[2048,2048]{1,0:T(8,128)(2,1)} %gather_group.3, bf16[2048,512]{1,0:T(8,128)(2,1)} %all-gather.6.cloned.1.call-done.refs_3_), kind=kOutput, calls=%fused_computation.2 | convolution fusion | flops 4301258752 | bytes 20971520 | tf_op jit(solution)/shard_map/dot_general | solution.py:558
  295.8 1.6 copy-done
  297.4 1.6 copy-done.1
  299.0 44.7 %scatter_dot.4 = f32[128,2048]{1,0:T(8,128)S(1)} custom-call(bf16[2048,512]{1,0:T(8,128)(2,1)S(1)} %copy-done.1, bf16[512,2048]{1,0:T(8,128)(2,1)S(1)} %copy-done), custom_call_target="tpu_custom_call" | custom-call | tf_op jit(solution)/shard_map/scatter_dot/pallas_call | solution.py:373
  345.2 42.1 %gather_group.4 = bf16[2048,2048]{1,0:T(8,128)(2,1)} custom-call(bf16[128,2048]{1,0:T(8,128)(2,1)} %fusion.4.x_ref), custom_call_target="tpu_custom_call" | custom-call | tf_op jit(solution)/shard_map/gather_group/pallas_call | solution.py:210
  387.4 9.9 %convolution_convert_fusion = bf16[512,2048]{1,0:T(8,128)(2,1)} fusion(bf16[2048,512]{1,0:T(8,128)(2,1)} %get-tuple-element.85.refs_0_, bf16[2048,2048]{1,0:T(8,128)(2,1)} %gather_group.4), kind=kOutput, calls=%fused_computation.5 | convolution fusion | flops 4296015872 | bytes 12582912 | tf_op jit(solution)/shard_map/dot_general | solution.py:566
  397.3 13.8 %multiply_convert_fusion = (bf16[2048,512]{1,0:T(8,128)(2,1)S(1)}, bf16[2048,512]{1,0:T(8,128)(2,1)}) fusion(f32[2048,512]{1,0:T(8,128)} %fusion.27, f32[2048,512]{1,0:T(8,128)} %get-tuple-element.86, bf16[2048,2048]{1,0:T(8,128)(2,1)} %gather_group.4, bf16[512,2048]{1,0:T(8,128)(2,1)} %all-gather.8.cloned.1.call-done.refs_1_), kind=kOutput, calls=%fused_computation | convolution fusion | flops 4308598784 | bytes 23068672 | tf_op jit(solution)/shard_map/dot_general | solution.py:562
  411.2 9.7 %convolution_convert_fusion.1 = bf16[2048,512]{1,0:T(8,128)(2,1)} fusion(bf16[2048,2048]{1,0:T(8,128)(2,1)} %gather_group.3, bf16[2048,512]{1,0:T(8,128)(2,1)S(1)} %get-tuple-element.47.refs_1_), kind=kOutput, calls=%fused_computation.6 | convolution fusion | flops 4296015872 | bytes 12582912 | tf_op jit(solution)/shard_map/dot_general | solution.py:566
  420.8 1.3 copy-done.4
  422.1 9.9 %convolution_convert_fusion.2 = bf16[2048,512]{1,0:T(8,128)(2,1)} fusion(bf16[2048,2048]{1,0:T(8,128)(2,1)} %gather_group.3, bf16[2048,512]{1,0:T(8,128)(2,1)} %get-tuple-element.46.refs_0_), kind=kOutput, calls=%fused_computation.7 | convolution fusion | flops 4296015872 | bytes 12582912 | tf_op jit(solution)/shard_map/dot_general | solution.py:566
  433.2 1.6 copy-done.5
  434.8 1.6 copy-done.6
  436.4 61.5 %scatter_dot.5 = f32[128,2048]{1,0:T(8,128)S(1)} custom-call(bf16[2048,512]{1,0:T(8,128)(2,1)S(1)} %copy-done.6, bf16[2048,512]{1,0:T(8,128)(2,1)S(1)} %copy-done.5, bf16[2048,512]{1,0:T(8,128)(2,1)} %all-gather.4.cloned.1.call-done.refs_2_, bf16[2048,512]{1,0:T(8,128)(2,1)} %all-gather.6.cloned.1.call-done.refs_3_), custom_call_target="tpu_custom_call" | custom-call | tf_op jit(solution)/shard_map/scatter_dot/pallas_call | solution.py:373
  498.3 1.5 subtract_convert_fusion
  499.8 48.8 %gather_group.5.refs_0_ = bf16[2048,2048]{1,0:T(8,128)(2,1)} custom-call(bf16[128,2048]{1,0:T(8,128)(2,1)} %get-tuple-element.74.x_ref), custom_call_target="tpu_custom_call" | custom-call | tf_op jit(solution)/shard_map/gather_group/pallas_call | solution.py:210
  548.8 61.0 %attend_backward.1 = (bf16[2048,384]{1,0:T(8,128)(2,1)}, bf16[128,2048]{1,0:T(8,128)(2,1)}, f32[8,128]{1,0:T(8,128)}, bf16[64,16384]{1,0:T(8,128)(2,1)}) custom-call(bf16[2048,2048]{1,0:T(8,128)(2,1)} %gather_group.5.refs_0_, bf16[128,2048]{1,0:T(8,128)(2,1)} %get-tuple-element.42.refs_1_, f32[2048,128]{1,0:T(8,128)} %get-tuple-element.48.refs_2_, ...), custom_call_target="tpu_custom_call" | custom-call | tf_op jit(solution)/shard_map/attend_backward/pallas_call | solution.py:851
  614.0 86.7 %finish_backward.1 = (f32[128,2048]{1,0:T(8,128)}, f32[64,8192]{1,0:T(8,128)}, f32[32,8,128]{2,1,0:T(8,128)}) custom-call(bf16[2048,384]{1,0:T(8,128)(2,1)} %get-tuple-element.57.dq, bf16[2048,384]{1,0:T(8,128)(2,1)} %get-tuple-element.38.wq, bf16[2048,2048]{1,0:T(8,128)(2,1)} %get-tuple-element.37.x, bf16[128,2048]{1,0:T(8,128)(2,1)} %get-tuple-element.58.go, ...), custom_call_target="tpu_custom_call" | custom-call | tf_op jit(solution)/shard_map/finish_backward/pallas_call | solution.py:994
  700.7 2.3 convert_element_type.77
  703.6 2.8 convert_element_type.78
  707.4 1.3 copy.30
  (80 shorter events, 14.4 us)
Async XLA Ops:
  7.2 265.2 %all-gather.4.cloned.1.call-start = ((), (), s32[]{:S(2)}) async-start(), calls=%async_computation.3 | async-start | bytes 3145728 | tf_op jit(solution)/shard_map/all_gather | solution.py:1044
  84.8 198.0 %all-gather.6.cloned.1.call-start = ((), (), s32[]{:S(2)}) async-start(), calls=%async_computation.4 | async-start | bytes 3145728 | tf_op jit(solution)/shard_map/all_gather | solution.py:1044
  145.7 73.0 %copy-start.8 = (bf16[1,128,2048]{2,1,0:T(8,128)(2,1)S(1)}, bf16[1,128,2048]{2,1,0:T(8,128)(2,1)}, u32[]{:S(2)}) copy-start(bf16[1,128,2048]{2,1,0:T(8,128)(2,1)} %param.10) | copy-start | bytes 1572868
  145.7 150.1 %all-gather.8.cloned.1.call-start = ((), (), s32[]{:S(2)}) async-start(), calls=%async_computation.5 | async-start | bytes 3145728 | tf_op jit(solution)/shard_map/all_gather | solution.py:1044
  146.4 402.3 %reduce-scatter.4.cloned.1.call-start = ((), (), s32[]{:S(2)}) async-start(), calls=%async_computation.6 | async-start | bytes 3145728 | tf_op jit(solution)/shard_map/reduce_scatter | solution.py:1047
  147.1 1.0 copy-start.2
  148.1 1.0 copy-start.3
  282.8 61.0 %copy-start.10 = (bf16[1,128,2048]{2,1,0:T(8,128)(2,1)S(1)}, bf16[1,128,2048]{2,1,0:T(8,128)(2,1)}, u32[]{:S(2)}) copy-start(bf16[1,128,2048]{2,1,0:T(8,128)(2,1)} %param.19) | copy-start | bytes 1572868
  295.8 1.6 copy-start
  297.4 1.6 copy-start.1
  420.8 1.3 copy-start.4
  432.0 116.8 %reduce-scatter.6.cloned.1.call-start = ((), (), s32[]{:S(2)}) async-start(), calls=%async_computation.7 | async-start | bytes 3145728 | tf_op jit(solution)/shard_map/reduce_scatter | solution.py:1047
  432.6 271.0 %reduce-scatter.8.cloned.1.call-start = ((), (), s32[]{:S(2)}) async-start(), calls=%async_computation.8 | async-start | bytes 3145728 | tf_op jit(solution)/shard_map/reduce_scatter | solution.py:1047
  433.2 1.6 copy-start.5
  434.8 1.6 copy-start.6
  436.4 61.5 %copy-start.11 = (bf16[1,128,2048]{2,1,0:T(8,128)(2,1)S(1)}, bf16[1,128,2048]{2,1,0:T(8,128)(2,1)}, u32[]{:S(2)}) copy-start(bf16[1,128,2048]{2,1,0:T(8,128)(2,1)} %param.19) | copy-start | bytes 1572868
  436.4 61.9 %copy-start.9 = (bf16[1,128,2048]{2,1,0:T(8,128)(2,1)S(1)}, bf16[1,128,2048]{2,1,0:T(8,128)(2,1)}, u32[]{:S(2)}) copy-start(bf16[1,128,2048]{2,1,0:T(8,128)(2,1)} %param.10) | copy-start | bytes 1572868
  498.3 50.3 %copy-start.7 = (f32[128,2048]{1,0:T(8,128)}, f32[128,2048]{1,0:T(8,128)S(1)}, u32[]{:S(2)}) copy-start(f32[128,2048]{1,0:T(8,128)S(1)} %get-tuple-element.71.bf) | copy-start | bytes 3145732
  614.0 86.7 %copy-start.12 = (bf16[64,16384]{1,0:T(8,128)(2,1)S(1)}, bf16[64,16384]{1,0:T(8,128)(2,1)}, u32[]{:S(2)}) copy-start(bf16[64,16384]{1,0:T(8,128)(2,1)} %get-tuple-element.62) | copy-start | bytes 6291460
  700.7 2.3 copy-start.15
  700.7 5.7 copy-start.14
  703.0 4.4 copy-start.13
Sparse Core Ops, SparseCore 0:
  84.9 65.3 all-gather.3
  151.9 60.8 all-gather.5
  214.3 55.5 all-gather.7
  432.1 53.4 reduce-scatter.3
  487.9 54.2 reduce-scatter.5
  544.3 54.5 reduce-scatter.7

commit v3 on v2

v3 whole, which is shorter than its diff:
```python
import functools

import jax
import jax.numpy as jnp
import numpy as np
from jax import lax
from jax.experimental import pallas as pl
from jax.experimental.pallas import tpu as pltpu
from jax.sharding import PartitionSpec as P

HEAD = 128
epsilon = 1e-06
rope_base = 500000.0
MESH = pl.DeviceIdType.MESH
BF = jnp.bfloat16
F32 = jnp.float32
ANY = pl.BlockSpec(memory_space=pl.ANY)
VM = pl.BlockSpec(memory_space=pltpu.VMEM)
DMA = pltpu.SemaphoreType.DMA
LIGHT = pl.CostEstimate(flops=0, bytes_accessed=0, transcendentals=0)


class Plan:
    def __init__(self, mesh, heads):
        self.dp = mesh.shape["dp"]
        self.seq = mesh.shape["seq"]
        self.size = heads
        self.low = heads // self.seq
        self.groups = self.dp // self.low
        self.devices = self.dp * self.seq
        self.pieces = self.devices // heads

    def here(self):
        dp = lax.axis_index("dp")
        seq = lax.axis_index("seq")
        return dp, seq, (dp % self.low) * self.seq + seq

    def head(self, index):
        return index // 2 + (self.size // 2) * (index % 2)

    def of_head(self, head):
        return (head % (self.size // 2)) * 2 + head // (self.size // 2)

    def member(self, dp, index):
        return (dp // self.low) * self.low + index // self.seq, index % self.seq

    def across(self, dp, seq, bit):
        if bit < self.seq:
            return dp, flip(seq, bit)
        return flip(dp, bit // self.seq), seq


def flip(value, bit):
    return value + bit * (1 - 2 * ((value // bit) % 2))


def flips(value, mask):
    bit = 1
    while bit <= mask:
        if mask & bit:
            value = flip(value, bit)
        bit *= 2
    return value


def greet(devices):
    barrier = pltpu.get_barrier_semaphore()
    for device in devices:
        pl.semaphore_signal(barrier, inc=1, device_id=device, device_id_type=MESH)
    pl.semaphore_wait(barrier, len(devices))


def greet_all(plan, dp, seq):
    barrier = pltpu.get_barrier_semaphore()
    me = dp * plan.seq + seq

    def hello(step, carry):
        other = (me + step) % plan.devices
        pl.semaphore_signal(
            barrier, inc=1, device_id=(other // plan.seq, other % plan.seq), device_id_type=MESH
        )
        return carry

    lax.fori_loop(1, plan.devices, hello, 0)
    pl.semaphore_wait(barrier, plan.devices - 1)


def greet_group(plan, dp, index):
    barrier = pltpu.get_barrier_semaphore()

    def hello(step, carry):
        other = plan.member(dp, (index + step) % plan.size)
        pl.semaphore_signal(barrier, inc=1, device_id=other, device_id_type=MESH)
        return carry

    lax.fori_loop(1, plan.size, hello, 0)
    pl.semaphore_wait(barrier, plan.size - 1)


def send(src, dst, send_sem, recv_sem, device):
    copy = pltpu.make_async_remote_copy(
        src_ref=src,
        dst_ref=dst,
        send_sem=send_sem,
        recv_sem=recv_sem,
        device_id=device,
        device_id_type=MESH,
    )
    copy.start()
    return copy


def wait_bytes(ref, sem):
    pltpu.make_async_copy(ref, ref, sem).wait()


def halves(rows):
    return ((0, rows // 2), (rows // 2, rows - rows // 2))


ORDERS = ((2, 4), (4, 2))


def gather_steps(plan, x, out, dp, seq, index, sems):
    far_send, far_recv, near_send, near_recv, core_send, core_recv, local = sems
    rows = x.shape[0]
    parts = halves(rows)
    copies = []

    def place(mask, part=None):
        start, count = (0, rows) if part is None else parts[part]
        return out.at[pl.ds(pl.multiple_of(flips(index, mask) * rows + start, 16), count)]

    def push(src, dst, send_sem, recv_sem, bit):
        copies.append(send(src, dst, send_sem, recv_sem, plan.across(dp, seq, bit)))

    def near(mask, part, number, bit):
        push(place(mask, part), place(mask, part), near_send.at[number], near_recv.at[number], bit)

    def to_core(mask, part, number):
        push(place(mask, part), place(mask, part), core_send.at[number], core_recv.at[number], 1)

    def begin():
        pltpu.make_async_copy(x, out.at[pl.ds(index * rows, rows)], local).start()
        for part in range(2):
            start, count = parts[part]
            push(
                x.at[pl.ds(start, count)], place(0, part), far_send.at[part], far_recv.at[part], 8
            )
        for bit in (2, 4):
            push(x, place(0), near_send.at[bit // 4], near_recv.at[bit // 4], bit)
        push(x, place(0), core_send.at[0], core_recv.at[0], 1)

    def own_plane():
        for bit, other in ORDERS:
            part = bit // 4
            wait_bytes(place(bit), near_recv.at[part])
            near(bit, part, 2 + part, other)
            to_core(bit, None, 1 + part)
        for part in range(2):
            wait_bytes(place(8, part), far_recv.at[part])
            for bit in (2, 4):
                near(8, part, 4 + 2 * part + bit // 4, bit)
            to_core(8, part, 5 + part)
        for part in range(2):
            wait_bytes(place(6, part), near_recv.at[2 + part])
            to_core(6, part, 3 + part)
        wait_bytes(place(1), core_recv.at[0])
        for part in range(2):
            wait_bytes(place(1 | (2 + 2 * part)), core_recv.at[1 + part])
            wait_bytes(place(7, part), core_recv.at[3 + part])
        pltpu.make_async_copy(x, out.at[pl.ds(index * rows, rows)], local).wait()

    def other_plane():
        for part in range(2):
            for bit, other in ORDERS:
                wait_bytes(place(8 | bit, part), near_recv.at[4 + 2 * part + bit // 4])
                if part == bit // 4:
                    near(8 | bit, part, 8 + part, other)
                to_core(8 | bit, part, 7 + 2 * part + bit // 4)
        for part in range(2):
            wait_bytes(place(14, part), near_recv.at[8 + part])
            to_core(14, part, 11 + part)
        for part in range(2):
            wait_bytes(place(9, part), core_recv.at[5 + part])
            for bit in (2, 4):
                wait_bytes(place(9 | bit, part), core_recv.at[7 + 2 * part + bit // 4])
            wait_bytes(place(15, part), core_recv.at[11 + part])

    def finish(use=None):
        own_plane()
        if use is not None:
            use(0)
        other_plane()
        if use is not None:
            use(1)
        for copy in copies:
            copy.wait_send()

    return begin, finish


GATHER_SEMS = (DMA((2,)), DMA((2,)), DMA((10,)), DMA((10,)), DMA((13,)), DMA((13,)), DMA)


def scatter_steps(plan, dp, seq, index, pairs, turned, write, bufs, sems, meanwhile=None):
    theirs, mine, got_core, got_first, got_second, got_far = bufs
    core_send, core_recv, send_sems, recv_sems, far_send, far_recv = sems
    rows, width = got_far.shape
    tile = 512
    piece = rows // 4
    copies = []

    def compute(dst, plane, core, blocks):
        starts = [flips(index, core | 2 * m | 8 * plane) * rows for m in blocks]

        @pl.loop(0, width // tile)
        def _(j):
            columns = pl.ds(pl.multiple_of(j * tile, tile), tile)
            block = None
            for l_ref, offset, r_ref in pairs:
                depth = r_ref.shape[1] if turned else r_ref.shape[0]
                some = jnp.concatenate(
                    [
                        l_ref[pl.ds(pl.multiple_of(start, rows), rows), pl.ds(offset, depth)]
                        for start in starts
                    ],
                    axis=0,
                )
                if turned:
                    part = contract_last(some, r_ref[columns, :])
                else:
                    part = dot(some, r_ref[:, columns])
                block = part if block is None else block + part
            block = block.astype(BF)
            for i, m in enumerate(blocks):
                dst[plane, m, :, columns] = block[i * rows : (i + 1) * rows]

    def push(src, dst, send_sem, recv_sem, bit):
        copy = send(src, dst, send_sem, recv_sem, plan.across(dp, seq, bit))
        copies.append(copy)
        return copy

    def add(dst, src, count):
        @pl.loop(0, count // 16)
        def _(i):
            here = pl.ds(pl.multiple_of(i * 16, 16), 16)
            dst[here, :] = dst[here, :] + src[here, :]

    def to_core(plane, blocks):
        started = []
        for m in blocks:
            number = plane * 4 + m
            started.append(
                (
                    push(
                        theirs.at[plane, m],
                        got_core.at[plane, m],
                        core_send.at[number],
                        core_recv.at[number],
                        1,
                    ),
                    m,
                )
            )
        return started

    def add_core(plane, started):
        for copy, m in started:
            copy.wait_recv()
            add(mine.at[plane, m], got_core.at[plane, m], rows)

    def start_of(chunk, part):
        return (chunk * 2 + part) * piece

    def first(plane, chunk):
        started = []
        for part, (bit, other) in enumerate(ORDERS):
            here = pl.ds(start_of(chunk, part), piece)
            for k, keep in enumerate((other, 0)):
                number = (plane * 2 + chunk) * 6 + part * 2 + k
                buffer = got_first.at[plane, chunk, part * 2 + k]
                copy = push(
                    mine.at[plane, (keep | bit) // 2, here],
                    buffer,
                    send_sems.at[number],
                    recv_sems.at[number],
                    bit,
                )
                started.append((copy, keep // 2, here, buffer))
        return started

    def second(plane, chunk):
        started = []
        for part, (bit, other) in enumerate(ORDERS):
            here = pl.ds(start_of(chunk, part), piece)
            number = (plane * 2 + chunk) * 6 + 4 + part
            buffer = got_second.at[plane, chunk, part]
            copy = push(
                mine.at[plane, other // 2, here],
                buffer,
                send_sems.at[number],
                recv_sems.at[number],
                other,
            )
            started.append((copy, 0, here, buffer))
        return started

    def far(chunk):
        here = pl.ds(chunk * 2 * piece, 2 * piece)
        return push(
            mine.at[1, 0, here], got_far.at[here], far_send.at[chunk], far_recv.at[chunk], 8
        )

    def settle(plane, started):
        for copy, m, here, buffer in started:
            copy.wait_recv()
            add(mine.at[plane, m, here], buffer, piece)

    def hook(i):
        if meanwhile is not None:
            meanwhile(i)

    compute(theirs, 1, 1, (3, 1))
    core_a = to_core(1, (3, 1))
    compute(theirs, 1, 1, (2, 0))
    core_b = to_core(1, (2, 0))
    compute(mine, 1, 0, (3, 1, 2, 0))
    hook(0)
    add_core(1, core_a)
    add_core(1, core_b)
    one = [first(1, chunk) for chunk in range(2)]
    compute(theirs, 0, 1, (3, 1, 2, 0))
    core = to_core(0, (3, 1, 2, 0))
    compute(mine, 0, 0, (3, 1, 2, 0))
    hook(1)
    for chunk in range(2):
        settle(1, one[chunk])
        one[chunk] = second(1, chunk)
    add_core(0, core)
    zero = [first(0, chunk) for chunk in range(2)]
    hook(2)
    fars = []
    for chunk in range(2):
        settle(1, one[chunk])
        fars.append(far(chunk))
    hook(3)
    for chunk in range(2):
        settle(0, zero[chunk])
        zero[chunk] = second(0, chunk)
    for chunk in range(2):
        settle(0, zero[chunk])
        fars[chunk].wait_recv()

        @pl.loop(0, 2 * piece // 16)
        def _(i):
            here = pl.ds(pl.multiple_of(chunk * 2 * piece + i * 16, 16), 16)
            write(here, mine[0, 0, here, :].astype(F32) + got_far[here, :].astype(F32))

    for copy in copies:
        copy.wait_send()


def scatter_scratch(rows, width):
    block = (rows, width)
    piece = (rows // 4, width)
    return [
        pltpu.VMEM((2, 4) + block, BF),
        pltpu.VMEM((2, 4) + block, BF),
        pltpu.VMEM((2, 4) + block, BF),
        pltpu.VMEM((2, 2, 4) + piece, BF),
        pltpu.VMEM((2, 2, 2) + piece, BF),
        pltpu.VMEM(block, BF),
        DMA((8,)),
        DMA((8,)),
        DMA((24,)),
        DMA((24,)),
        DMA((2,)),
        DMA((2,)),
    ]


def scatter_dot(plan, left, rights, turned, collective_id):
    rows = left.shape[0] // plan.size
    width = rights[0].shape[0] if turned else rights[0].shape[1]
    count = len(rights)
    depth = left.shape[1] // count

    def kernel(*refs):
        pairs = [(refs[0], i * depth, refs[1 + i]) for i in range(count)]
        out_ref = refs[1 + count]
        rest = refs[2 + count :]
        dp, seq, index = plan.here()
        greet([plan.across(dp, seq, bit) for bit in (1, 2, 4, 8)])

        def write(here, value):
            out_ref[here, :] = value

        scatter_steps(plan, dp, seq, index, pairs, turned, write, rest[:6], rest[6:])

    return pl.pallas_call(
        kernel,
        out_shape=jax.ShapeDtypeStruct((rows, width), F32),
        in_specs=[VM] * (1 + count),
        out_specs=VM,
        scratch_shapes=scatter_scratch(rows, width),
        compiler_params=pltpu.CompilerParams(
            collective_id=collective_id, has_side_effects=True, vmem_limit_bytes=48 * 2**20
        ),
        cost_estimate=LIGHT,
        name="scatter_dot",
    )(left, *rights)


def half_columns(plan, inner, blocks, half):
    wide = inner // blocks
    each = wide // plan.size
    return [(half * inner + block * wide, each, block * each) for block in range(blocks)]


def columns_out(plan, dp, index, w_ref, out_ref, table, send_sem, recv_sem):
    own = w_ref.shape[0]
    wide = out_ref.shape[1]
    rows = pl.ds(pl.multiple_of(index * own, own), own)

    def moves(other):
        for base, each, place in table:
            yield (
                w_ref.at[:, pl.ds(pl.multiple_of(base + other * each, 128), each)],
                out_ref.at[rows, pl.ds(place, each)],
            )

    def begin():
        def to(step, carry):
            other = (index + step) % plan.size
            for src, dst in moves(other):
                send(src, dst, send_sem, recv_sem, plan.member(dp, other))
            return carry

        lax.fori_loop(1, plan.size, to, 0)
        for src, dst in moves(index):
            pltpu.make_async_copy(src, dst, recv_sem).start()

    def finish():
        wait_bytes(out_ref, recv_sem)

        def sent(step, carry):
            wait_bytes(w_ref.at[:, pl.ds(0, wide)], send_sem)
            return carry

        lax.fori_loop(1, plan.size, sent, 0)

    return begin, finish


def columns_back(plan, dp, index, g_ref, out_ref, table, send_sem, recv_sem):
    own = g_ref.shape[0] // plan.size

    def moves(other):
        rows = pl.ds(pl.multiple_of(other * own, own), own)
        for base, each, place in table:
            yield (
                g_ref.at[rows, pl.ds(place, each)],
                out_ref.at[:, pl.ds(pl.multiple_of(base + index * each, 128), each)],
            )

    def begin(plane):
        first = flips(index, 8 * plane) // 8 * 8

        def to(step, carry):
            other = first + (index + step) % 8
            for src, dst in moves(other):
                send(src, dst, send_sem, recv_sem, plan.member(dp, other))
            return carry

        lax.fori_loop(1 - plane, 8, to, 0)
        if plane == 0:
            for src, dst in moves(index):
                pltpu.make_async_copy(src, dst, recv_sem).start()

    def finish():
        wait_bytes(g_ref, recv_sem)

        def sent(step, carry):
            wait_bytes(g_ref.at[pl.ds(0, own)], send_sem)
            return carry

        lax.fori_loop(1, plan.size, sent, 0)

    return begin, finish


def hidden_backward(plan, g_low, rights, grad_out, branch, gain):
    rows, width = branch.shape
    count = len(rights)
    depth = g_low.shape[1] // count

    def kernel(*refs):
        pairs = [(refs[0], i * depth, refs[1 + i]) for i in range(count)]
        dy, u, g, grad, g_gain, low = refs[1 + count : 7 + count]
        rest = refs[7 + count :]
        dp, seq, index = plan.here()
        greet([plan.across(dp, seq, bit) for bit in (1, 2, 4, 8)])
        g_gain[...] = jnp.zeros_like(g_gain)

        def write(here, value):
            e = dy[here, :].astype(F32) + value
            grad[here, :] = e
            values = u[here, :]
            r = lax.rsqrt(jnp.mean(values * values, axis=1, keepdims=True) + epsilon)
            scaled = e * g[...]
            inner = jnp.mean(scaled * values, axis=1, keepdims=True)
            low[here, :] = (r * scaled - values * (r * r * r * inner)).astype(BF)
            g_gain[...] += jnp.sum(e * values * r, axis=0, keepdims=True)

        scatter_steps(plan, dp, seq, index, pairs, True, write, rest[:6], rest[6:])

    return pl.pallas_call(
        kernel,
        out_shape=[
            jax.ShapeDtypeStruct((rows, width), F32),
            jax.ShapeDtypeStruct((1, width), F32),
            jax.ShapeDtypeStruct((rows, width), BF),
        ],
        in_specs=[VM] * (4 + count),
        out_specs=[VM] * 3,
        scratch_shapes=scatter_scratch(rows, width),
        compiler_params=pltpu.CompilerParams(
            collective_id=7, has_side_effects=True, vmem_limit_bytes=48 * 2**20
        ),
        cost_estimate=LIGHT,
        name="hidden_backward",
    )(g_low, *rights, grad_out, branch, gain)


def start_gather(plan, x, attn_w, gate_up_w, gains, segments, blocks):
    rows, width = x.shape
    own, both = gate_up_w.shape
    table = half_columns(plan, both // 2, blocks, 0)

    count = len(gains)

    def kernel(x_ref, w_ref, u_ref, s_ref, *refs):
        gain_refs, (xo, wo, uo, oo, go, do) = refs[:count], refs[count : count + 6]
        g_ref, d_ref = refs[count + 6 : count + 8]
        sems = refs[count + 8 :]
        gather_sems = sems[:7]
        w_send, w_recv, u_send, u_recv, o_send, o_recv, g_send, g_recv, d_send, d_recv = sems[7:]
        g_ref[...] = jnp.zeros_like(g_ref)
        for i, gain in enumerate(gain_refs):
            g_ref[i : i + 1, :own] = gain[...].astype(F32)
        d_ref[...] = jnp.broadcast_to(s_ref[...], d_ref.shape)
        dp, seq, index = plan.here()
        me = dp * plan.seq + seq
        greet_all(plan, dp, seq)
        begin, finish = gather_steps(plan, x_ref, xo, dp, seq, index, gather_sems)
        begin()
        group = dp // plan.low
        def columns(part, other):
            return pl.ds(pl.multiple_of(part * width + plan.head(other) * HEAD, HEAD), HEAD)

        mine = pl.ds(pl.multiple_of(me * own, own), own)

        def w_to(away, step, carry):
            other = (index + step) % plan.size
            to_group = (group + away) % plan.groups
            device = (to_group * plan.low + other // plan.seq, other % plan.seq)
            for part in range(3):
                send(
                    w_ref.at[:, columns(part, other)],
                    wo.at[mine, pl.ds(part * HEAD, HEAD)],
                    w_send,
                    w_recv,
                    device,
                )
            return carry

        for away in range(1, plan.groups):
            lax.fori_loop(0, plan.size, functools.partial(w_to, away), 0)
        lax.fori_loop(1, plan.size, functools.partial(w_to, 0), 0)
        for part in range(3):
            pltpu.make_async_copy(
                w_ref.at[:, columns(part, index)], wo.at[mine, pl.ds(part * HEAD, HEAD)], w_recv
            ).start()

        feature = me * own
        keeper = plan.of_head(feature // HEAD)
        o_dst = oo.at[pl.ds(pl.multiple_of(feature % HEAD, own), own)]
        o_src = w_ref.at[:, pl.ds(3 * width, width)]

        def o_to(away, carry):
            to_group = (group + away) % plan.groups
            to_dp, to_seq = to_group * plan.low + keeper // plan.seq, keeper % plan.seq
            same = to_dp * plan.seq + to_seq == me

            @pl.when(same)
            def _():
                pltpu.make_async_copy(o_src, o_dst, o_recv).start()

            @pl.when(jnp.logical_not(same))
            def _():
                send(o_src, o_dst, o_send, o_recv, (to_dp, to_seq))

            return carry

        lax.fori_loop(0, plan.groups, o_to, 0)

        def g_to(step, carry):
            other = (me + step) % plan.devices
            send(g_ref, go.at[me], g_send, g_recv, (other // plan.seq, other % plan.seq))
            return carry

        lax.fori_loop(1, plan.devices, g_to, 0)
        pltpu.make_async_copy(g_ref, go.at[me], g_recv).start()

        def d_to(step, carry):
            send(d_ref, do.at[index], d_send, d_recv, plan.member(dp, (index + step) % plan.size))
            return carry

        lax.fori_loop(1, plan.size, d_to, 0)
        pltpu.make_async_copy(d_ref, do.at[index], d_recv).start()
        begin_u, finish_u = columns_out(plan, dp, index, u_ref, uo, table, u_send, u_recv)
        begin_u()
        finish()
        finish_u()
        wait_bytes(go, g_recv)
        wait_bytes(do, d_recv)
        wait_bytes(wo, w_recv)

        def sent(step, carry):
            wait_bytes(w_ref.at[:, pl.ds(0, 3 * HEAD)], w_send)
            wait_bytes(g_ref, g_send)
            return carry

        lax.fori_loop(1, plan.devices, sent, 0)

        def sent_docs(step, carry):
            wait_bytes(d_ref, d_send)
            return carry

        lax.fori_loop(1, plan.size, sent_docs, 0)
        wait_bytes(oo, o_recv)

        def sent_o(away, carry):
            to_group = (group + away) % plan.groups
            to_dp, to_seq = to_group * plan.low + keeper // plan.seq, keeper % plan.seq

            @pl.when(to_dp * plan.seq + to_seq != me)
            def _():
                wait_bytes(o_src, o_send)

            return carry

        lax.fori_loop(0, plan.groups, sent_o, 0)


    shapes = (
        ((plan.size * rows, width), BF),
        ((plan.devices * own, 3 * HEAD), BF),
        ((plan.size * own, both // 2 // plan.size), BF),
        ((HEAD, width), BF),
        ((plan.devices, 8, 128), F32),
        ((plan.size, 8, rows), jnp.int32),
    )
    return pl.pallas_call(
        kernel,
        out_shape=[jax.ShapeDtypeStruct(*shape) for shape in shapes],
        in_specs=[ANY] * 3 + [VM] * (1 + count),
        out_specs=[ANY] * 6,
        scratch_shapes=[pltpu.VMEM((8, 128), F32), pltpu.VMEM((8, rows), jnp.int32)]
        + list(GATHER_SEMS)
        + [DMA] * 10,
        compiler_params=pltpu.CompilerParams(collective_id=0, has_side_effects=True),
        cost_estimate=LIGHT,
        name="start_gather",
    )(x, attn_w, gate_up_w, segments, *[gain.reshape(1, own) for gain in gains])


def dot(left, right):
    return jnp.dot(left, right, preferred_element_type=F32)


def contract_last(left, right):
    return lax.dot_general(left, right, (((1,), (1,)), ((), ())), preferred_element_type=F32)


def contract_first(left, right):
    return lax.dot_general(left, right, (((0,), (0,)), ((), ())), preferred_element_type=F32)


def plane_rows(index, plane, rows):
    return pl.multiple_of(flips(index, 8 * plane) // 8 * (8 * rows), 8 * rows)


def ffn_forward(plan, h, w_gate, w_up):
    rows, width = h.shape
    tokens = rows * plan.size
    units = w_gate.shape[1]

    def kernel(h_ref, wg_ref, wu_ref, h_out, gate, up, act, h_all, wg, wu, *sems):
        wg_sem, wu_sem, out_sem = sems[7:]
        dp, seq, index = plan.here()
        loads = [
            pltpu.make_async_copy(wg_ref, wg, wg_sem),
            pltpu.make_async_copy(wu_ref, wu, wu_sem),
        ]
        for load in loads:
            load.start()
        greet([plan.across(dp, seq, bit) for bit in (1, 2, 4, 8)])
        begin, finish = gather_steps(plan, h_ref, h_all, dp, seq, index, sems[:7])
        begin()
        stores = []

        def use(plane):
            if plane == 0:
                for load in loads:
                    load.wait()
            first = plane_rows(index, plane, rows)
            here = pl.ds(first, 8 * rows)
            stores.append(pltpu.make_async_copy(h_all.at[here], h_out.at[here], out_sem.at[plane]))
            stores[-1].start()

            @pl.loop(0, 8 * rows // STEP)
            def _(i):
                some = pl.ds(pl.multiple_of(first + i * STEP, STEP), STEP)
                values = h_all[some, :]
                g = dot(values, wg[...])
                u = dot(values, wu[...])
                gate[some, :] = g.astype(BF)
                up[some, :] = u.astype(BF)
                act[some, :] = (g * jax.nn.sigmoid(g) * u).astype(BF)

        finish(use)
        for store in stores:
            store.wait()

    part = jax.ShapeDtypeStruct((tokens, units), BF)
    return pl.pallas_call(
        kernel,
        out_shape=[jax.ShapeDtypeStruct((tokens, width), BF), part, part, part],
        in_specs=[VM, ANY, ANY],
        out_specs=[ANY, VM, VM, VM],
        scratch_shapes=[
            pltpu.VMEM((tokens, width), BF),
            pltpu.VMEM(w_gate.shape, BF),
            pltpu.VMEM(w_up.shape, BF),
        ]
        + list(GATHER_SEMS)
        + [DMA, DMA, DMA((2,))],
        compiler_params=pltpu.CompilerParams(
            collective_id=9, has_side_effects=True, vmem_limit_bytes=48 * 2**20
        ),
        cost_estimate=LIGHT,
        name="ffn_forward",
    )(h, w_gate, w_up)


def ffn_backward(plan, d, h_all, w_down, gate, up, act):
    rows, width = d.shape
    tokens = rows * plan.size
    half = tokens // 2
    units = w_down.shape[0]
    tile = 256

    def kernel(d_ref, *refs):
        ins, (out, g_gate, g_up, g_down), held = refs[:5], refs[5:9], refs[9:14]
        d_all, gu_turned, act_turned, gu_sum, down_sum = refs[14:19]
        sems, load_sems = refs[19:26], refs[26]
        h_all, wd, gate, up, act = held
        dp, seq, index = plan.here()
        loads = [
            pltpu.make_async_copy(src, dst, load_sems.at[i])
            for i, (src, dst) in enumerate(zip(ins, held))
        ]
        for load in loads[1:] + loads[:1]:
            load.start()
        greet([plan.across(dp, seq, bit) for bit in (1, 2, 4, 8)])
        begin, finish = gather_steps(plan, d_ref, d_all, dp, seq, index, sems)
        begin()

        def use(plane):
            if plane == 0:
                for load in loads:
                    load.wait()
            first = plane_rows(index, plane, rows)
            here = pl.ds(first, half)

            @pl.loop(0, half // STEP)
            def _(i):
                some = pl.ds(pl.multiple_of(first + i * STEP, STEP), STEP)
                columns = pl.ds(pl.multiple_of(i * STEP, STEP), STEP)
                grad = contract_last(d_all[some, :], wd[...])
                g = gate[some, :].astype(F32)
                u = up[some, :].astype(F32)
                sigma = jax.nn.sigmoid(g)
                grad_gate = (grad * u * sigma * (1.0 + g * (1.0 - sigma))).astype(BF)
                grad_up = (grad * (g * sigma)).astype(BF)
                out[some, pl.ds(0, units)] = grad_gate
                out[some, pl.ds(units, units)] = grad_up
                gu_turned[pl.ds(0, units), columns] = grad_gate.T
                gu_turned[pl.ds(units, units), columns] = grad_up.T
                act_turned[:, columns] = act[some, :].T

            @pl.loop(0, width // tile)
            def _(i):
                columns = pl.ds(pl.multiple_of(i * tile, tile), tile)
                block = dot(gu_turned[...], h_all[here, columns])
                if plane == 0:
                    gu_sum[:, columns] = block
                else:
                    block = (gu_sum[:, columns] + block).T.astype(BF)
                    g_gate[columns, :] = block[:, :units]
                    g_up[columns, :] = block[:, units:]

            @pl.loop(0, width // tile)
            def _(i):
                columns = pl.ds(pl.multiple_of(i * tile, tile), tile)
                block = dot(act_turned[...], d_all[here, columns])
                if plane == 0:
                    down_sum[:, columns] = block
                else:
                    g_down[:, columns] = (down_sum[:, columns] + block).astype(BF)

        finish(use)

    return pl.pallas_call(
        kernel,
        out_shape=[
            jax.ShapeDtypeStruct((tokens, 2 * units), BF),
            jax.ShapeDtypeStruct((width, units), BF),
            jax.ShapeDtypeStruct((width, units), BF),
            jax.ShapeDtypeStruct((units, width), BF),
        ],
        in_specs=[VM] + [ANY] * 5,
        out_specs=[VM] * 4,
        scratch_shapes=[
            pltpu.VMEM(value.shape, BF) for value in (h_all, w_down, gate, up, act, h_all)
        ]
        + [
            pltpu.VMEM((2 * units, half), BF),
            pltpu.VMEM((units, half), BF),
            pltpu.VMEM((2 * units, width), F32),
            pltpu.VMEM((units, width), F32),
        ]
        + list(GATHER_SEMS)
        + [DMA((5,))],
        compiler_params=pltpu.CompilerParams(
            collective_id=10, has_side_effects=True, vmem_limit_bytes=62 * 2**20
        ),
        cost_estimate=LIGHT,
        name="ffn_backward",
    )(d, h_all, w_down, gate, up, act)


def row_sums(values):
    ones = jnp.ones((8, values.shape[1]), F32)
    sums = lax.dot_general(
        ones,
        values,
        (((1,), (1,)), ((), ())),
        precision=lax.Precision.HIGHEST,
        preferred_element_type=F32,
    )
    return sums[:1]


def spread_sums(rows):
    ones = jnp.ones((rows.shape[0], HEAD), F32)
    return lax.dot_general(
        rows,
        ones,
        (((0,), (0,)), ((), ())),
        precision=lax.Precision.HIGHEST,
        preferred_element_type=F32,
    )


STEP = 256


def lay_out(docs_ref, row_ref):
    for i in range(docs_ref.shape[0]):
        rows = docs_ref.shape[2]
        row_ref[:, i * rows : (i + 1) * rows] = docs_ref[i, :1, :].astype(F32)


def my_gain(plan, gains_ref, which, head):
    own = HEAD // plan.pieces
    parts = [gains_ref[head * plan.pieces + i, which : which + 1, :own] for i in range(plan.pieces)]
    return jnp.concatenate(parts, axis=1)


def scores_of(q, k, q_docs, k_docs, start):
    scores = contract_last(q, k) * HEAD ** (-0.5)
    row = start + lax.broadcasted_iota(jnp.int32, scores.shape, 0)
    column = lax.broadcasted_iota(jnp.int32, scores.shape, 1)
    allowed = (column <= row) & (spread_sums(q_docs)[:, :1] == k_docs)
    scores = jnp.where(allowed, scores, -1e30)
    top = jnp.max(scores, axis=1, keepdims=True)
    weights = jnp.exp(scores - top)
    return weights / jnp.sum(weights, axis=1, keepdims=True)


def swap_sums(plan, dp, index, mine, held, s_sem, r_sem):
    def begin():
        def to(step, carry):
            send(mine, held.at[index], s_sem, r_sem, plan.member(dp, (index + step) % plan.size))
            return carry

        pltpu.make_async_copy(mine, held.at[index], r_sem).start()
        lax.fori_loop(1, plan.size, to, 0)

    def finish():
        wait_bytes(held, r_sem)
        wait_bytes(held.at[pl.ds(0, plan.size - 1)], s_sem)

    return begin, finish


def attend_forward(
    plan, x_all, w_qkv, gate_up_w, gains, docs, cosine, sine, blocks
):
    tokens, width = x_all.shape
    length = cosine.shape[0]
    own, both = gate_up_w.shape
    table = half_columns(plan, both // 2, blocks, 1)

    def kernel(x, wq, up, ga, do, cs, sn, uo, q, k, sums, ql, kl, vl, mixed, *rest):
        gn, dr, stats, held, t_send, t_recv, u_send, u_recv = rest
        dp, seq, index = plan.here()
        greet_group(plan, dp, index)
        lay_out(do, dr)
        for which in range(2):
            gn[which : which + 1, :] = my_gain(plan, ga, which, plan.head(index))
        @pl.loop(0, tokens // STEP)
        def _(i):
            rows = pl.ds(pl.multiple_of(i * STEP, STEP), STEP)
            block = dot(x[rows, :], wq[...])
            q[rows, :] = block[:, :HEAD]
            k[rows, :] = block[:, HEAD : 2 * HEAD]
            vl[rows, :] = block[:, 2 * HEAD :].astype(BF)
            stats[0, :, rows] = row_sums(block[:, :HEAD] * block[:, :HEAD])
            stats[1, :, rows] = row_sums(block[:, HEAD : 2 * HEAD] * block[:, HEAD : 2 * HEAD])

        begin, finish = swap_sums(plan, dp, index, stats, held, t_send, t_recv)
        begin()
        begin_u, finish_u = columns_out(plan, dp, index, up, uo, table, u_send, u_recv)
        begin_u()
        finish()
        for which in range(2):
            sums[which] = jnp.sum(held[:, which, 0, :], axis=0, keepdims=True)

        @pl.loop(0, tokens // STEP)
        def _(i):
            rows = pl.ds(pl.multiple_of(i * STEP, STEP), STEP)
            places = pl.ds(pl.multiple_of((i % (length // STEP)) * STEP, STEP), STEP)
            for which, raw, low in ((0, q, ql), (1, k, kl)):
                r = lax.rsqrt(spread_sums(sums[which, :, rows]) / width + epsilon)
                values = raw[rows, :] * r * gn[which : which + 1, :]
                turned = values * cs[places, :] + pltpu.roll(values, HEAD // 2, 1) * sn[places, :]
                low[rows, :] = turned.astype(BF)

        @pl.loop(0, tokens // length)
        def _(b):
            for j in range(length // STEP):
                start = pl.multiple_of(b * length + j * STEP, STEP)
                rows = pl.ds(start, STEP)
                keys = pl.ds(pl.multiple_of(b * length, length), (j + 1) * STEP)
                probs = scores_of(
                    ql[rows, :], kl[keys, :], dr[:, rows], dr[:, keys], j * STEP
                )
                mixed[rows, :] = dot(probs.astype(BF), vl[keys, :]).astype(BF)

        finish_u()

    per_head = (tokens, HEAD)
    shapes = (
        ((plan.size * own, both // 2 // plan.size), BF),
        (per_head, F32),
        (per_head, F32),
        ((2, 1, tokens), F32),
        (per_head, BF),
        (per_head, BF),
        (per_head, BF),
        (per_head, BF),
    )
    return pl.pallas_call(
        kernel,
        out_shape=[jax.ShapeDtypeStruct(*shape) for shape in shapes],
        in_specs=[VM, VM, ANY] + [VM] * 4,
        out_specs=[ANY] + [VM] * 7,
        scratch_shapes=[
            pltpu.VMEM((8, HEAD), F32),
            pltpu.VMEM((1, tokens), F32),
            pltpu.VMEM((2, 1, tokens), F32),
            pltpu.VMEM((plan.size, 2, 1, tokens), F32),
        ]
        + [DMA] * 4,
        compiler_params=pltpu.CompilerParams(
            collective_id=3, has_side_effects=True, vmem_limit_bytes=56 * 2**20
        ),
        cost_estimate=LIGHT,
        name="attend_forward",
    )(x_all, w_qkv, gate_up_w, gains, docs, cosine, sine)


def attend_backward(
    plan,
    b,
    w_out,
    q,
    k,
    sums,
    ql,
    kl,
    vl,
    mixed,
    gains,
    docs,
    cosine,
    sine,
    g_gate,
    blocks,
):
    rows_here, width = b.shape
    tokens = rows_here * plan.size
    in_plane = 8 * rows_here
    own = g_gate.shape[0] // plan.size
    inner = g_gate.shape[1] * plan.size
    length = cosine.shape[0]
    scale = HEAD ** (-0.5)

    def kernel(*refs):
        b_ref, wo, q, k, sums, ql, kl, vl, mx, ga, do, cs, sn, gg = refs[:14]
        dqkv, g_out, g_gain, gate_out = refs[14:18]
        ba, dq, dk, dv, gn, dr, stats, held, t_send, t_recv, gg_send, gg_recv = refs[18:30]
        dp, seq, index = plan.here()
        greet_group(plan, dp, index)
        begin_b, finish_b = gather_steps(plan, b_ref, ba, dp, seq, index, refs[30:])
        begin_b()
        lay_out(do, dr)
        for which in range(2):
            gn[which : which + 1, :] = my_gain(plan, ga, which, plan.head(index))
        begin_g, finish_g = columns_back(
            plan, dp, index, gg, gate_out, half_columns(plan, inner, blocks, 0), gg_send, gg_recv
        )
        dk[...] = jnp.zeros_like(dk)
        dv[...] = jnp.zeros_like(dv)

        def use(plane):
            if plane == 1:
                begin_g(0)
            plane_first = plane_rows(index, plane, rows_here)
            for j in range(in_plane // STEP):
                first = pl.multiple_of(plane_first + j * STEP, STEP)
                rows = pl.ds(first, STEP)
                start = first % length
                count = (j + 1) * STEP if length == in_plane else length
                base = pl.multiple_of(first - start, STEP)
                keys = pl.ds(base, count)
                grad = contract_last(ba[rows, :], wo[...]).astype(BF)
                probs = scores_of(
                    ql[rows, :], kl[keys, :], dr[:, rows], dr[:, keys], start
                )
                grad_probs = contract_last(grad, vl[keys, :])
                delta = jnp.sum(probs * grad_probs, axis=1, keepdims=True)
                grad_scores = (probs * (grad_probs - delta)).astype(BF)
                dq[rows, :] = dot(grad_scores, kl[keys, :]) * scale
                dk[keys, :] += contract_first(grad_scores, ql[rows, :]) * scale
                dv[keys, :] += contract_first(probs.astype(BF), grad)

        finish_b(use)

        @pl.loop(0, tokens // STEP)
        def _(i):
            rows = pl.ds(pl.multiple_of(i * STEP, STEP), STEP)
            places = pl.ds(pl.multiple_of((i % (length // STEP)) * STEP, STEP), STEP)
            for which, raw, grad in ((0, q, dq), (1, k, dk)):
                values = grad[rows, :]
                turned = values * cs[places, :] - pltpu.roll(values, HEAD // 2, 1) * sn[places, :]
                grad[rows, :] = turned
                stats[which, :, rows] = row_sums(turned * gn[which : which + 1, :] * raw[rows, :])

        begin, finish = swap_sums(plan, dp, index, stats, held, t_send, t_recv)
        begin()
        begin_g(1)
        turned_mixed = mx[...].T

        @pl.loop(0, width // 512)
        def _(i):
            columns = pl.ds(pl.multiple_of(i * 512, 512), 512)
            g_out[:, columns] = dot(turned_mixed, ba[:, columns]).astype(BF)

        g_gain[...] = jnp.zeros_like(g_gain)
        finish()

        @pl.loop(0, tokens // STEP)
        def _(i):
            rows = pl.ds(pl.multiple_of(i * STEP, STEP), STEP)
            for which, raw, grad in ((0, q, dq), (1, k, dk)):
                total = spread_sums(held[:, which, 0, rows])
                r = lax.rsqrt(spread_sums(sums[which, :, rows]) / width + epsilon)
                u = raw[rows, :]
                e = grad[rows, :]
                back = r * (gn[which : which + 1, :] * e) - u * (r * r * r * (total / width))
                dqkv[rows, pl.ds(which * HEAD, HEAD)] = back.astype(BF)
                g_gain[which : which + 1, :] += jnp.sum(e * u * r, axis=0, keepdims=True)
            dqkv[rows, pl.ds(2 * HEAD, HEAD)] = dv[rows, :].astype(BF)

        finish_g()

    per_head = (tokens, HEAD)
    shapes = (
        ((tokens, 3 * HEAD), BF),
        ((HEAD, width), BF),
        ((8, HEAD), F32),
        ((own, inner), BF),
    )
    return pl.pallas_call(
        kernel,
        out_shape=[jax.ShapeDtypeStruct(*shape) for shape in shapes],
        in_specs=[VM] * 13 + [ANY],
        out_specs=[VM] * 3 + [ANY],
        scratch_shapes=[
            pltpu.VMEM((tokens, width), BF),
            pltpu.VMEM(per_head, F32),
            pltpu.VMEM(per_head, F32),
            pltpu.VMEM(per_head, F32),
            pltpu.VMEM((8, HEAD), F32),
            pltpu.VMEM((1, tokens), F32),
            pltpu.VMEM((2, 1, tokens), F32),
            pltpu.VMEM((plan.size, 2, 1, tokens), F32),
        ]
        + [DMA] * 4
        + list(GATHER_SEMS),
        compiler_params=pltpu.CompilerParams(
            collective_id=4, has_side_effects=True, vmem_limit_bytes=56 * 2**20
        ),
        cost_estimate=LIGHT,
        name="attend_backward",
    )(
        b,
        w_out,
        q,
        k,
        sums,
        ql,
        kl,
        vl,
        mixed,
        gains,
        docs,
        cosine,
        sine,
        g_gate,
    )


def finish_backward(
    plan, dqkv, w_qkv, x_all, g_up, g_out, g_head, g_attn, g_ffn, before, blocks
):
    tokens, width = x_all.shape
    own = width // plan.devices
    rows = tokens // plan.size
    inner = g_up.shape[1] * plan.size
    pieces = HEAD // own
    tile = 256

    def kernel(dq, wq, x, gu, go, gh, gat, gff, bf, ig, w_grad, up_out, ga_out, *rest):
        bufs, sems = rest[:6], rest[6:12]
        turned, gq, got_q, got_o, ga = rest[12:17]
        q_s, q_r, o_s, o_r, ga_s, ga_r, gu_s, gu_r = rest[17:]
        dp, seq, index = plan.here()
        me = dp * plan.seq + seq
        group = dp // plan.low
        greet_all(plan, dp, seq)

        def device_of(flat):
            return flat // plan.seq, flat % plan.seq

        def o_to(piece, carry):
            other = plan.head(index) * pieces + piece
            src = go.at[pl.ds(pl.multiple_of(piece * own, own), own)]

            @pl.when(other == me)
            def _():
                pltpu.make_async_copy(src, got_o.at[group], o_r).start()

            @pl.when(other != me)
            def _():
                send(src, got_o.at[group], o_s, o_r, device_of(other))

            return carry

        def ga_to(step, carry):
            other = (me + step) % plan.devices
            send(ga.at[other], ga_out.at[me], ga_s, ga_r, device_of(other))
            return carry

        tiles = width // tile
        table = half_columns(plan, inner, blocks, 0)
        begin_u, finish_u = columns_back(plan, dp, index, gu, up_out, table, gu_s, gu_r)

        def weights(first, last):
            @pl.loop(first, last)
            def _(i):
                at = (i + (me * own) // tile) % tiles
                columns = pl.ds(pl.multiple_of(at * tile, tile), tile)
                block = dot(turned[...], x[:, columns])
                gq[columns, :] = block.T.astype(BF)

                def q_to(piece, carry):
                    other = at * (tile // own) + piece
                    src = gq.at[pl.ds(pl.multiple_of(other * own, own), own)]

                    @pl.when(other == me)
                    def _():
                        pltpu.make_async_copy(src, got_q.at[group, index], q_r).start()

                    @pl.when(other != me)
                    def _():
                        send(src, got_q.at[group, index], q_s, q_r, device_of(other))

                    return carry

                lax.fori_loop(0, tile // own, q_to, 0)

        def meanwhile(i):
            if i == 0:
                turned[...] = dq[...].T
                weights(0, tiles // 4)
            elif i == 1:
                weights(tiles // 4, 5 * tiles // 8)
            elif i == 2:
                lax.fori_loop(0, pieces, o_to, 0)
                begin_u(1)
            else:
                begin_u(0)
                weights(5 * tiles // 8, tiles)
                ga[...] = jnp.zeros_like(ga)
                for other in range(plan.devices):
                    part = slice(other * own, (other + 1) * own)
                    ga[other, 2:3, :own] = gat[:, part]
                    ga[other, 3:4, :own] = gff[:, part]
                for piece in range(pieces):
                    part = slice(piece * own, (piece + 1) * own)
                    ga[plan.head(index) * pieces + piece, 0:2, :own] = gh[0:2, part]
                lax.fori_loop(1, plan.devices, ga_to, 0)
                pltpu.make_async_copy(ga.at[me], ga_out.at[me], ga_r).start()

        def write(here, value):
            ig[here, :] = bf[here, :] + value

        scatter_steps(plan, dp, seq, index, [(dq, 0, wq)], True, write, bufs, sems, meanwhile)
        wait_bytes(got_o, o_r)
        wait_bytes(got_q, q_r)
        for part in range(3):
            for member in range(plan.size):
                total = got_q[0, member, :, part * HEAD : (part + 1) * HEAD].astype(F32)
                for other in range(1, plan.groups):
                    total = total + got_q[
                        other, member, :, part * HEAD : (part + 1) * HEAD
                    ].astype(F32)
                w_grad[:, pl.ds(part * width + plan.head(member) * HEAD, HEAD)] = total
        total = got_o[0].astype(F32)
        for other in range(1, plan.groups):
            total = total + got_o[other].astype(F32)
        w_grad[:, pl.ds(3 * width, width)] = total
        finish_u()
        wait_bytes(ga_out, ga_r)
        wait_bytes(ga_out.at[pl.ds(0, plan.devices - 1)], ga_s)
        wait_bytes(gq.at[pl.ds(0, width - own)], q_s)

        def sent_o(piece, carry):
            @pl.when(plan.head(index) * pieces + piece != me)
            def _():
                wait_bytes(go.at[pl.ds(0, own)], o_s)

            return carry

        lax.fori_loop(0, pieces, sent_o, 0)

    shapes = (
        ((rows, width), F32),
        ((own, 4 * width), F32),
        ((own, inner), BF),
        ((plan.devices, 8, 128), F32),
    )
    return pl.pallas_call(
        kernel,
        out_shape=[jax.ShapeDtypeStruct(*shape) for shape in shapes],
        in_specs=[VM, VM, VM, ANY] + [VM] * 5,
        out_specs=[VM, VM, ANY, VM],
        scratch_shapes=scatter_scratch(rows, width)
        + [
            pltpu.VMEM((3 * HEAD, tokens), BF),
            pltpu.VMEM((width, 3 * HEAD), BF),
            pltpu.VMEM((plan.groups, plan.size, own, 3 * HEAD), BF),
            pltpu.VMEM((plan.groups, own, width), BF),
            pltpu.VMEM((plan.devices, 8, 128), F32),
        ]
        + [DMA] * 8,
        compiler_params=pltpu.CompilerParams(
            collective_id=5, has_side_effects=True, vmem_limit_bytes=60 * 2**20
        ),
        cost_estimate=LIGHT,
        name="finish_backward",
    )(dqkv, w_qkv, x_all, g_up, g_out, g_head, g_attn, g_ffn, before)


def per_device(
    plan,
    hidden_in,
    segments,
    attn_weights,
    q_gain,
    k_gain,
    attn_gain,
    ffn_gain,
    gate_up_weights,
    down_weights,
    cotangent,
):
    x = hidden_in[0]
    rows, width = x.shape
    own = attn_weights.shape[0]
    inner = gate_up_weights.shape[1] // 2
    length = rows * plan.seq
    tokens = rows * plan.size
    groups = plan.groups
    dp, seq, index = plan.here()
    me = dp * plan.seq + seq
    group = dp // plan.low
    direct = (inner // (groups * plan.size)) % 128 == 0
    blocks = groups if direct else 1

    across = [[low + high * plan.low for high in range(groups)] for low in range(plan.low)]

    def join_groups(value):
        return lax.all_gather(value, "dp", axis_index_groups=across, axis=0, tiled=True)

    def sum_groups(value):
        return lax.psum_scatter(
            value.astype(BF), "dp", axis_index_groups=across, scatter_dimension=0, tiled=True
        )

    x_all, w_qkv, gate_part, w_out, gains_all, docs = start_gather(
        plan,
        x,
        attn_weights,
        gate_up_weights,
        [q_gain, k_gain, attn_gain, ffn_gain],
        segments,
        blocks,
    )
    w_gate = join_groups(gate_part)
    gains = jnp.transpose(gains_all[:, 2:4, :own], (1, 0, 2)).reshape(2, width)
    positions = np.arange(length, dtype=np.float32)
    frequency = rope_base ** (-2.0 * np.arange(HEAD // 2, dtype=np.float32) / HEAD)
    angles = positions[:, None] * frequency.astype(np.float32)[None, :]
    cosine = jnp.asarray(np.concatenate([np.cos(angles)] * 2, axis=1), F32)
    sine = jnp.asarray(np.concatenate([-np.sin(angles), np.sin(angles)], axis=1), F32)

    up_part, q, k, row_sums_qk, q_low, k_low, v_low, mixed = attend_forward(
        plan,
        x_all,
        w_qkv,
        gate_up_weights,
        gains_all,
        docs,
        cosine,
        sine,
        blocks,
    )
    w_up = join_groups(up_part)
    down_weights, _ = lax.optimization_barrier((down_weights, up_part))
    if direct:
        w_down = join_groups(down_weights)
    else:
        w_all = lax.all_gather(down_weights, ("dp", "seq"), axis=0, tiled=True)
        each = inner // plan.size
        w_down = lax.dynamic_slice_in_dim(w_all, index * each, each, 0)
    branch = scatter_dot(plan, mixed, [w_out], False, 2)
    branch, w_gate = lax.optimization_barrier((branch, w_gate))

    def rms(values):
        return lax.rsqrt(jnp.mean(values * values, axis=1, keepdims=True) + epsilon)

    def rms_back(values, r, gain, grad):
        scaled = gain * grad
        inner_sum = jnp.mean(scaled * values, axis=1, keepdims=True)
        return r * scaled - values * (r * r * r * inner_sum), jnp.sum(grad * values * r, axis=0)

    branch_r = rms(branch)
    hidden = x.astype(F32) + branch * branch_r * gains[0]
    hidden_low = hidden.astype(BF)

    h_all, gate, up, act = ffn_forward(plan, hidden_low, w_gate, w_up)
    down = scatter_dot(plan, act, [w_down], False, 6)
    down_r = rms(down)
    output = (hidden + down * down_r * gains[1]).astype(BF)

    grad_out = cotangent[0].astype(F32)
    grad_down_in, grad_fg = rms_back(down, down_r, gains[1], grad_out)
    gu_low, g_gate, g_up, g_down = ffn_backward(
        plan, grad_down_in.astype(BF), h_all, w_down, gate, up, act
    )
    g_gate = sum_groups(g_gate)
    g_up = sum_groups(g_up)
    if direct:
        grad_down = sum_groups(g_down).astype(F32)
    else:
        spread = jnp.zeros((inner, width), BF)
        spread = lax.dynamic_update_slice_in_dim(spread, g_down, index * g_down.shape[0], 0)
        grad_down = lax.psum_scatter(
            spread, ("dp", "seq"), scatter_dimension=0, tiled=True
        ).astype(F32)

    grad_hidden, grad_ag, grad_branch = hidden_backward(
        plan, gu_low, [w_gate, w_up], cotangent[0], branch, gains[:1]
    )
    dqkv, g_out, g_head, gate_rows = attend_backward(
        plan,
        grad_branch,
        w_out,
        q,
        k,
        row_sums_qk,
        q_low,
        k_low,
        v_low,
        mixed,
        gains_all,
        docs,
        cosine,
        sine,
        g_gate,
        blocks,
    )

    input_grad, grad_attn, up_rows, gain_rows = finish_backward(
        plan,
        dqkv,
        w_qkv,
        x_all,
        g_up,
        g_out,
        g_head,
        grad_ag,
        grad_fg.reshape(1, width),
        grad_hidden,
        blocks,
    )
    grad_gate_up = jnp.concatenate([gate_rows, up_rows], axis=1).astype(F32)
    gain_grads = jnp.sum(gain_rows, axis=0)[:4, :own]
    return (
        output[None],
        input_grad[None],
        grad_attn,
        grad_gate_up,
        grad_down,
        gain_grads[0],
        gain_grads[1],
        gain_grads[2],
        gain_grads[3],
    )


def solution(mesh):
    by_token = P("dp", "seq", None)
    by_row = P(("dp", "seq"), None)
    by_gain = P(("dp", "seq"))

    def run(hidden_in, segments, attn_weights, *rest):
        plan = Plan(mesh, hidden_in.shape[2] // HEAD)
        return jax.shard_map(
            functools.partial(per_device, plan),
            mesh=mesh,
            in_specs=(by_token, P("dp", "seq"), by_row)
            + (by_gain,) * 4
            + (by_row, by_row, by_token),
            out_specs=(by_token, by_token, by_row, by_row, by_row) + (by_gain,) * 4,
            check_vma=False,
        )(hidden_in, segments, attn_weights, *rest)

    return run
```

time: 724 us -> 631 us (0.87)
  matrix products: 66.7 us -> 0 us
  Pallas kernels: 595 us -> 560 us
  waiting for transfers between devices: 1.83 us -> 25.4 us
  local copies, waits for them, and re-layouts: 21.4 us -> 13.8 us
    pallas_call x3 -> x2, Pallas kernels: 175 us -> 87 us  [scatter_dot(): pl.pallas_call(kernel, out_shape=jax.ShapeDtypeStruct((rows, width), F32)...]
    dot_general x6 -> x0, matrix products: 66.7 us -> none  [the longest x3 29.4 us: contract_first(): lax.dot_general(left, right, (((0,), (0,)), ((), ())), preferred_element_...]
    pallas_call x1, Pallas kernels: 61 us -> 90.9 us  [attend_backward(): pl.pallas_call(kernel, out_shape=[jax.ShapeDtypeStruct(*shape) for shape...]
    pallas_call x3, Pallas kernels: 144 us -> 171 us  [the longest x1 64.3 us: ffn_backward(): pl.pallas_call(kernel, out_shape=[jax.ShapeDtypeStruct((tokens, 2 * units...]
    all_gather x3, waiting for transfers between devices: 0.01 us -> 23.8 us  [join_groups(): lax.all_gather(value, 'dp', axis_index_groups=across, axis=0, tiled=True)]
  transfers between devices with their start and end apart: 6 -> 6, of which waited for: 0 -> 2; matrix products, arithmetic and copies ran while one was open for 6% -> 1% of each run, Pallas kernels for 60% -> 60%
where the time goes in v3:
time: 631 us; the launch traced here: 625 us
  Pallas kernels  560 us (89%)
  waiting for transfers between devices  25.4 us (4%)
  between operations  14.5 us (2%)
  local copies, waits for them, and re-layouts  13.8 us (2%)
  other arithmetic  10.3 us (2%)
    pallas_call x1, Pallas kernels, attend_backward(): pl.pallas_call(kernel, out_shape=[jax.ShapeDtypeStruct(*shape) for shape...  90.9 us
    pallas_call x2, Pallas kernels, scatter_dot(): pl.pallas_call(kernel, out_shape=jax.ShapeDtypeStruct((rows, width), F32)...  87 us
    pallas_call x1, Pallas kernels, finish_backward(): pl.pallas_call(kernel, out_shape=[jax.ShapeDtypeStruct(*shape) for shape...  85.7 us
    pallas_call x1, Pallas kernels, start_gather(): pl.pallas_call(kernel, out_shape=[jax.ShapeDtypeStruct(*shape) for shape...  75.4 us
    pallas_call x1, Pallas kernels, ffn_backward(): pl.pallas_call(kernel, out_shape=[jax.ShapeDtypeStruct((tokens, 2 * units...  64.3 us
    pallas_call x1, Pallas kernels, hidden_backward(): pl.pallas_call(kernel, out_shape=[jax.ShapeDtypeStruct((rows, width), F32...  59.1 us
    pallas_call x1, Pallas kernels, attend_forward(): pl.pallas_call(kernel, out_shape=[jax.ShapeDtypeStruct(*shape) for shape...  49.2 us
    pallas_call x1, Pallas kernels, ffn_forward(): pl.pallas_call(kernel, out_shape=[jax.ShapeDtypeStruct((tokens, width), B...  48 us
  transfers between devices with their start and end apart: 6, of which 2 were waited for; matrix products, arithmetic and copies ran while one was open for 1% of the time, Pallas kernels for 60%

profile of v3, /device:TPU:15, one launch (start us, length us, event | category | flops | bytes accessed | tf_op | source)
XLA Modules:
  0.0 624.5 jit_solution(11965674889480082630)
XLA Ops:
  7.2 75.4 %start_gather.1 = (bf16[2048,2048]{1,0:T(8,128)(2,1)}, bf16[2048,384]{1,0:T(8,128)(2,1)}, bf16[1024,512]{1,0:T(8,128)(2,1)}, bf16[128,2048]{1,0:T(8,128)(2,1)}, ...) custom-call(bf16[128,2048]{1,0:T(8,128)(2,1)} %bitcast.27, bf16[64,8192]{1,0:T(8,128)(2,1)} %w_ref.1, bf16[64,16384]{1,0:T(8,128)(2,1)} %up.1, ...), custom_call_target="tpu_custom_call" | custom-call | tf_op jit(solution)/shard_map/start_gather/pallas_call | solution.py:665
  82.7 49.2 %attend_forward.1 = (bf16[1024,512]{1,0:T(8,128)(2,1)}, f32[2048,128]{1,0:T(8,128)}, f32[2048,128]{1,0:T(8,128)}, f32[2,1,2048]{2,1,0:T(1,128)}, bf16[2048,128]{...) custom-call(bf16[2048,2048]{1,0:T(8,128)(2,1)} %get-tuple-element.45.x, ...), custom_call_target="tpu_custom_call" | custom-call | tf_op jit(solution)/shard_map/attend_forward/pallas_call | solution.py:987
  132.1 0.7 all-gather.8.cloned.1.call-update
  132.7 0.5 reduce-scatter.4.cloned.1.call-start
  133.3 0.9 slice_bitcast_fusion
  134.4 42.2 %scatter_dot.2.refs_4_ = f32[128,2048]{1,0:T(8,128)S(1)} custom-call(bf16[2048,128]{1,0:T(8,128)(2,1)S(1)} %copy-done.5, bf16[128,2048]{1,0:T(8,128)(2,1)S(1)} %copy-done.4), custom_call_target="tpu_custom_call" | custom-call | tf_op jit(solution)/shard_map/scatter_dot/pallas_call | solution.py:401
  177.0 17.3 %all-gather.6.cloned.1.call-done.wu_ref.refs_2_ = bf16[2048,512]{1,0:T(8,128)(2,1)} async-done(((bf16[1024,512]{1,0:T(8,128)(2,1)}), bf16[2048,512]{1,0:T(8,128)(2,1)}) %all-gather.6.cloned.1.call-update) | async-done | bytes 2097168 | tf_op jit(solution)/shard_map/all_gather | solution.py:1340
  194.4 48.0 %ffn_forward.1 = (bf16[2048,2048]{1,0:T(8,128)(2,1)}, bf16[2048,512]{1,0:T(8,128)(2,1)S(1)}, bf16[2048,512]{1,0:T(8,128)(2,1)S(1)}, bf16[2048,512]{1,0:T(8,128)(2,1)}) custom-call(bf16[128,2048]{1,0:T(8,128)(2,1)S(1)} %fusion.7.h_ref, bf16[2048,512]{1,0:T(8,128)(2,1)} %all-gather.4.cloned.1.call-done.wg_ref.refs_1_, ...), custom_call_target="tpu_custom_call" | custom-call | tf_op jit(solution)/shard_map/ffn_forward/pallas_call | solution.py:738
  242.3 1.3 copy-done.6
  243.7 1.3 copy-done.7
  245.0 6.4 %all-gather.8.cloned.1.call-done.refs_1_ = bf16[512,2048]{1,0:T(8,128)(2,1)} async-done(((bf16[256,2048]{1,0:T(8,128)(2,1)}), bf16[512,2048]{1,0:T(8,128)(2,1)}) %all-gather.8.cloned.1.call-update) | async-done | bytes 2097168 | tf_op jit(solution)/shard_map/all_gather | solution.py:1340
  251.4 1.6 copy-done
  253.0 1.6 copy-done.1
  254.6 44.8 %scatter_dot.3 = f32[128,2048]{1,0:T(8,128)S(1)} custom-call(bf16[2048,512]{1,0:T(8,128)(2,1)S(1)} %copy-done.1, bf16[512,2048]{1,0:T(8,128)(2,1)S(1)} %copy-done), custom_call_target="tpu_custom_call" | custom-call | tf_op jit(solution)/shard_map/scatter_dot/pallas_call | solution.py:401
  299.5 0.9 fusion.6
  300.5 1.5 fusion.3
  301.9 64.3 %ffn_backward.1 = (bf16[2048,1024]{1,0:T(8,128)(2,1)}, bf16[2048,512]{1,0:T(8,128)(2,1)}, bf16[2048,512]{1,0:T(8,128)(2,1)}, bf16[512,2048]{1,0:T(8,128)(2,1)}) custom-call(bf16[128,2048]{1,0:T(8,128)(2,1)} %get-tuple-element.85.d_ref, bf16[2048,2048]{1,0:T(8,128)(2,1)} %get-tuple-element.57.refs_0_, bf16[512,2048]{1,0:T(8,128)(2,1)} %all-gather.8.cloned.1.call-done.refs_1_, ...), custom_call_target="tpu_custom_call" | custom-call | tf_op jit(solution)/shard_map/ffn_backward/pallas_call | solution.py:826
  366.3 0.5 reduce-scatter.6.cloned.1.call-update
  367.0 0.4 reduce-scatter.8.cloned.1.call-update
  367.5 1.6 copy-done.2
  369.1 59.1 %hidden_backward.1 = (f32[128,2048]{1,0:T(8,128)S(1)}, f32[1,2048]{1,0:T(1,128)S(1)}, bf16[128,2048]{1,0:T(8,128)(2,1)S(1)}) custom-call(bf16[2048,1024]{1,0:T(8,128)(2,1)} %get-tuple-element.60.refs_0_, bf16[2048,512]{1,0:T(8,128)(2,1)S(1)} %copy-done.2, bf16[2048,512]{1,0:T(8,128)(2,1)} %all-gather.6.cloned.1.call-done.wu_ref.refs_2_, ...), custom_call_target="tpu_custom_call" | custom-call | tf_op jit(solution)/shard_map/hidden_backward/pallas_call | solution.py:518
  428.2 1.0 copy-done.8
  429.2 0.8 copy-done.9
  430.0 0.6 copy-done.10
  430.6 90.9 %attend_backward.1 = (bf16[2048,384]{1,0:T(8,128)(2,1)}, bf16[128,2048]{1,0:T(8,128)(2,1)}, f32[8,128]{1,0:T(8,128)}, bf16[64,8192]{1,0:T(8,128)(2,1)}) custom-call(bf16[128,2048]{1,0:T(8,128)(2,1)} %copy-done.9, bf16[128,2048]{1,0:T(8,128)(2,1)} %get-tuple-element.50.refs_1_, f32[2048,128]{1,0:T(8,128)} %get-tuple-element.62.refs_2_, ...), custom_call_target="tpu_custom_call" | custom-call | tf_op jit(solution)/shard_map/attend_backward/pallas_call | solution.py:1119
  521.5 85.7 %finish_backward.1 = (f32[128,2048]{1,0:T(8,128)}, f32[64,8192]{1,0:T(8,128)}, bf16[64,8192]{1,0:T(8,128)(2,1)}, f32[32,8,128]{2,1,0:T(8,128)}) custom-call(bf16[2048,384]{1,0:T(8,128)(2,1)} %get-tuple-element.69.dq, bf16[2048,384]{1,0:T(8,128)(2,1)} %get-tuple-element.46.wq, bf16[2048,2048]{1,0:T(8,128)(2,1)} %get-tuple-element.45.x, ...), custom_call_target="tpu_custom_call" | custom-call | tf_op jit(solution)/shard_map/finish_backward/pallas_call | solution.py:1289
  607.2 0.9 reduce_sum.49
  608.2 0.5 slice_bitcast_fusion.1
  608.7 3.5 maximum_convert_fusion
  612.2 2.9 convert_element_type.27
  615.2 1.0 copy.23
  616.1 1.3 copy.24
  (46 shorter events, 1.4 us)
Async XLA Ops:
  7.2 169.5 %all-gather.4.cloned.1.call-start = ((), (), s32[]{:S(2)}) async-start(), calls=%async_computation.3 | async-start | bytes 3145728 | tf_op jit(solution)/shard_map/all_gather | solution.py:1340
  82.6 111.7 %all-gather.6.cloned.1.call-start = ((), (), s32[]{:S(2)}) async-start(), calls=%async_computation.4 | async-start | bytes 3145728 | tf_op jit(solution)/shard_map/all_gather | solution.py:1340
  131.9 2.5 copy-start.4
  132.0 2.5 copy-start.5
  132.0 44.8 %copy-start.11 = (bf16[1,128,2048]{2,1,0:T(8,128)(2,1)S(1)}, bf16[1,128,2048]{2,1,0:T(8,128)(2,1)}, u32[]{:S(2)}) copy-start(bf16[1,128,2048]{2,1,0:T(8,128)(2,1)} %param.12) | copy-start | bytes 1572868
  132.0 119.4 %all-gather.8.cloned.1.call-start = ((), (), s32[]{:S(2)}) async-start(), calls=%async_computation.5 | async-start | bytes 3145728 | tf_op jit(solution)/shard_map/all_gather | solution.py:1340
  132.7 297.8 %reduce-scatter.4.cloned.1.call-start = ((), (), s32[]{:S(2)}) async-start(), calls=%async_computation.6 | async-start | bytes 3145728 | tf_op jit(solution)/shard_map/reduce_scatter | solution.py:1343
  242.3 1.3 copy-start.6
  243.7 1.3 copy-start.7
  251.4 1.6 copy-start
  253.0 1.6 copy-start.1
  254.6 45.0 %copy-start.3 = (bf16[1,128,2048]{2,1,0:T(8,128)(2,1)S(1)}, bf16[1,128,2048]{2,1,0:T(8,128)(2,1)}, u32[]{:S(2)}) copy-start(bf16[1,128,2048]{2,1,0:T(8,128)(2,1)} %param.21) | copy-start | bytes 1572868
  299.4 1.1 copy-start.12
  366.2 155.3 %reduce-scatter.6.cloned.1.call-start = ((), (), s32[]{:S(2)}) async-start(), calls=%async_computation.7 | async-start | bytes 3145728 | tf_op jit(solution)/shard_map/reduce_scatter | solution.py:1343
  366.8 245.4 %reduce-scatter.8.cloned.1.call-start = ((), (), s32[]{:S(2)}) async-start(), calls=%async_computation.8 | async-start | bytes 3145728 | tf_op jit(solution)/shard_map/reduce_scatter | solution.py:1343
  367.5 1.6 copy-start.2
  428.2 1.0 copy-start.8
  429.2 0.8 copy-start.9
  430.0 0.6 copy-start.10
  521.5 87.2 %copy-start.15 = (bf16[64,8192]{1,0:T(8,128)(2,1)S(1)}, bf16[64,8192]{1,0:T(8,128)(2,1)}, u32[]{:S(2)}) copy-start(bf16[64,8192]{1,0:T(8,128)(2,1)} %get-tuple-element.77) | copy-start | bytes 3145732
  612.2 2.9 copy-start.14
  612.2 3.9 copy-start.13
Sparse Core Ops, SparseCore 0:
  82.8 54.4 all-gather.3
  138.8 55.5 all-gather.5
  195.9 55.4 all-gather.7
  366.4 51.4 reduce-scatter.3
  420.0 54.2 reduce-scatter.5
  476.4 54.2 reduce-scatter.7

commit v4 on v3

--- a/solution.py
+++ b/solution.py
@@ -29,25 +29,54 @@
         self.groups = self.dp // self.low
         self.devices = self.dp * self.seq
         self.pieces = self.devices // heads
+        self.chips = self.seq // 2
+        self.by_chip = self.groups == 2 and self.size == self.dp * self.chips
+
+    def group_of(self, dp):
+        return dp % self.groups + (dp // self.groups) * (self.groups - 1 - 2 * (dp % self.groups))
+
+    def dp_of(self, group, low):
+        return low * self.groups + group + low * (self.groups - 1 - 2 * group)
+
+    def flat(self, group, index):
+        return self.dp_of(group, index // self.seq) * self.seq + index % self.seq
+
+    def place(self, dp):
+        return self.group_of(dp) * self.low + dp // self.groups
+
+    def natural(self, rows):
+        if self.low == 1:
+            return [(0, 0, rows)]
+        count = rows // self.dp
+        return [(self.place(i) * count, i * count, count) for i in range(self.dp)]
 
     def here(self):
         dp = lax.axis_index("dp")
         seq = lax.axis_index("seq")
-        return dp, seq, (dp % self.low) * self.seq + seq
+        return dp, seq, (dp // self.groups) * self.seq + seq
 
     def head(self, index):
-        return index // 2 + (self.size // 2) * (index % 2)
+        if self.by_chip:
+            return self.dp_of(index % 2, index // self.seq) * self.chips + (index % self.seq) // 2
+        return index
 
     def of_head(self, head):
-        return (head % (self.size // 2)) * 2 + head // (self.size // 2)
+        if self.by_chip:
+            dp = head // self.chips
+            low = dp // self.groups
+            return low * self.seq + (head % self.chips) * 2 + self.group_of(dp)
+        return head
+
+    def in_group(self, group, index):
+        return self.dp_of(group, index // self.seq), index % self.seq
 
     def member(self, dp, index):
-        return (dp // self.low) * self.low + index // self.seq, index % self.seq
+        return self.in_group(self.group_of(dp), index)
 
     def across(self, dp, seq, bit):
         if bit < self.seq:
             return dp, flip(seq, bit)
-        return flip(dp, bit // self.seq), seq
+        return 2 * self.groups - 1 - dp, seq
 
 
 def flip(value, bit):
@@ -112,6 +141,24 @@
 
 def wait_bytes(ref, sem):
     pltpu.make_async_copy(ref, ref, sem).wait()
+
+
+class Loads:
+    def __init__(self, sources, buffers, sems):
+        self.copies = [
+            pltpu.make_async_copy(src, dst, sems.at[i])
+            for i, (src, dst) in enumerate(zip(sources, buffers))
+        ]
+        for copy in self.copies:
+            copy.start()
+
+    def wait(self, *which):
+        for i in which or range(len(self.copies)):
+            self.copies[i].wait()
+
+
+def like(value):
+    return pltpu.VMEM(value.shape, value.dtype)
 
 
 def halves(rows):
@@ -151,7 +198,14 @@
             push(x, place(0), near_send.at[bit // 4], near_recv.at[bit // 4], bit)
         push(x, place(0), core_send.at[0], core_recv.at[0], 1)
 
-    def own_plane():
+    def finish(use=None):
+        def here(chip):
+            if use is not None:
+                use(chip)
+
+        pltpu.make_async_copy(x, out.at[pl.ds(index * rows, rows)], local).wait()
+        wait_bytes(place(1), core_recv.at[0])
+        here(0)
         for bit, other in ORDERS:
             part = bit // 4
             wait_bytes(place(bit), near_recv.at[part])
@@ -162,38 +216,36 @@
             for bit in (2, 4):
                 near(8, part, 4 + 2 * part + bit // 4, bit)
             to_core(8, part, 5 + part)
+        for bit in (2, 4):
+            wait_bytes(place(1 | bit), core_recv.at[1 + bit // 4])
+            here(bit)
         for part in range(2):
             wait_bytes(place(6, part), near_recv.at[2 + part])
             to_core(6, part, 3 + part)
-        wait_bytes(place(1), core_recv.at[0])
         for part in range(2):
-            wait_bytes(place(1 | (2 + 2 * part)), core_recv.at[1 + part])
+            wait_bytes(place(9, part), core_recv.at[5 + part])
+        here(8)
+        for part in range(2):
             wait_bytes(place(7, part), core_recv.at[3 + part])
-        pltpu.make_async_copy(x, out.at[pl.ds(index * rows, rows)], local).wait()
-
-    def other_plane():
+        here(6)
         for part in range(2):
             for bit, other in ORDERS:
                 wait_bytes(place(8 | bit, part), near_recv.at[4 + 2 * part + bit // 4])
                 if part == bit // 4:
                     near(8 | bit, part, 8 + part, other)
                 to_core(8 | bit, part, 7 + 2 * part + bit // 4)
+        for bit in (2, 4):
+            for part in range(2):
+                wait_bytes(place(9 | bit, part), core_recv.at[7 + 2 * part + bit // 4])
+            if bit == 2:
+                here(10)
         for part in range(2):
             wait_bytes(place(14, part), near_recv.at[8 + part])
             to_core(14, part, 11 + part)
+        here(12)
         for part in range(2):
-            wait_bytes(place(9, part), core_recv.at[5 + part])
-            for bit in (2, 4):
-                wait_bytes(place(9 | bit, part), core_recv.at[7 + 2 * part + bit // 4])
             wait_bytes(place(15, part), core_recv.at[11 + part])
-
-    def finish(use=None):
-        own_plane()
-        if use is not None:
-            use(0)
-        other_plane()
-        if use is not None:
-            use(1)
+        here(14)
         for copy in copies:
             copy.wait_send()
 
@@ -380,42 +432,162 @@
     ]
 
 
-def scatter_dot(plan, left, rights, turned, collective_id):
+def scatter_call(
+    plan, left, rights, turned, collective_id, name, extras, outs, begin, write, gather=False, moves=None
+):
     rows = left.shape[0] // plan.size
     width = rights[0].shape[0] if turned else rights[0].shape[1]
     count = len(rights)
     depth = left.shape[1] // count
+    moves = moves or [(0, 0, rights[0].shape[0])]
 
     def kernel(*refs):
-        pairs = [(refs[0], i * depth, refs[1 + i]) for i in range(count)]
-        out_ref = refs[1 + count]
-        rest = refs[2 + count :]
+        refs = list(refs)
+
+        def take(number):
+            taken = refs[:number]
+            del refs[:number]
+            return taken
+
+        sources, more, results = take(1 + count), take(len(extras)), take(len(outs))
+        everyone = take(1) if gather else None
+        held, (sem,) = take(1 + count), take(1)
+        pieces = [(sources[0], held[0])] + [
+            (src.at[pl.ds(first, rows)], dst.at[pl.ds(to, rows)])
+            for src, dst in zip(sources[1:], held[1:])
+            for first, to, rows in moves
+        ]
+        loads = Loads(*zip(*pieces), sem)
+        pairs = [(held[0], i * depth, held[1 + i]) for i in range(count)]
         dp, seq, index = plan.here()
         greet([plan.across(dp, seq, bit) for bit in (1, 2, 4, 8)])
-
-        def write(here, value):
-            out_ref[here, :] = value
-
-        scatter_steps(plan, dp, seq, index, pairs, turned, write, rest[:6], rest[6:])
-
+        begin(results)
+        loads.wait()
+
+        def put(here, value):
+            write(here, value, more, results)
+
+        scatter_steps(plan, dp, seq, index, pairs, turned, put, refs[:6], refs[6:12])
+        if gather:
+            start, finish = gather_steps(
+                plan, results[-1], everyone[0], dp, seq, index, refs[12:]
+            )
+            start()
+            finish()
+
+    shapes = [jax.ShapeDtypeStruct(*out) for out in outs]
+    if gather:
+        shapes.append(jax.ShapeDtypeStruct((plan.size * rows, width), outs[-1][1]))
     return pl.pallas_call(
         kernel,
-        out_shape=jax.ShapeDtypeStruct((rows, width), F32),
-        in_specs=[VM] * (1 + count),
-        out_specs=VM,
-        scratch_shapes=scatter_scratch(rows, width),
+        out_shape=shapes,
+        in_specs=[ANY] * (1 + count) + [VM] * len(extras),
+        out_specs=[VM] * len(outs) + [ANY] * gather,
+        scratch_shapes=[like(value) for value in (left, *rights)]
+        + [DMA((1 + count * len(moves),))]
+        + scatter_scratch(rows, width)
+        + list(GATHER_SEMS) * gather,
         compiler_params=pltpu.CompilerParams(
-            collective_id=collective_id, has_side_effects=True, vmem_limit_bytes=48 * 2**20
+            collective_id=collective_id, has_side_effects=True, vmem_limit_bytes=60 * 2**20
         ),
         cost_estimate=LIGHT,
-        name="scatter_dot",
-    )(left, *rights)
+        name=name,
+    )(left, *rights, *extras)
+
+
+def rms(values):
+    return lax.rsqrt(jnp.mean(values * values, axis=1, keepdims=True) + epsilon)
+
+
+def rms_back(values, gain, grad):
+    r = rms(values)
+    scaled = grad * gain
+    inner = jnp.mean(scaled * values, axis=1, keepdims=True)
+    back = r * scaled - values * (r * r * r * inner)
+    return back, jnp.sum(grad * values * r, axis=0, keepdims=True)
+
+
+def hidden_forward(plan, mixed, w_out, x, gain):
+    def write(here, value, extras, outs):
+        x_ref, g = extras
+        branch, hidden, low = outs
+        branch[here, :] = value
+        h = x_ref[here, :].astype(F32) + value * rms(value) * g[...]
+        hidden[here, :] = h
+        low[here, :] = h.astype(BF)
+
+    outs = ((x.shape, F32), (x.shape, F32), (x.shape, BF))
+    return scatter_call(
+        plan,
+        mixed,
+        [w_out],
+        False,
+        2,
+        "hidden_forward",
+        (x, gain),
+        outs,
+        lambda outs: None,
+        write,
+        gather=True,
+    )
+
+
+def output_norm(plan, act, w_down, hidden, grad_out, gain):
+    def begin(outs):
+        outs[2][...] = jnp.zeros_like(outs[2])
+
+    def write(here, value, extras, outs):
+        hidden_ref, dy, g = extras
+        output, back, g_gain = outs
+        output[here, :] = (hidden_ref[here, :] + value * rms(value) * g[...]).astype(BF)
+        grad, part = rms_back(value, g[...], dy[here, :].astype(F32))
+        back[here, :] = grad.astype(BF)
+        g_gain[...] += part
+
+    outs = ((hidden.shape, BF), (hidden.shape, BF), (gain.shape, F32))
+    return scatter_call(
+        plan, act, [w_down], False, 6, "output_norm", (hidden, grad_out, gain), outs, begin, write
+    )
+
+
+def hidden_backward(plan, g_low, rights, grad_out, branch, gain):
+    def begin(outs):
+        outs[1][...] = jnp.zeros_like(outs[1])
+
+    def write(here, value, extras, outs):
+        dy, u, g = extras
+        grad, g_gain, low = outs
+        e = dy[here, :].astype(F32) + value
+        grad[here, :] = e
+        back, part = rms_back(u[here, :], g[...], e)
+        low[here, :] = back.astype(BF)
+        g_gain[...] += part
+
+    outs = ((branch.shape, F32), (gain.shape, F32), (branch.shape, BF))
+    return scatter_call(
+        plan,
+        g_low,
+        rights,
+        True,
+        7,
+        "hidden_backward",
+        (grad_out, branch, gain),
+        outs,
+        begin,
+        write,
+        moves=plan.natural(rights[0].shape[0]),
+    )
 
 
 def half_columns(plan, inner, blocks, half):
-    wide = inner // blocks
-    each = wide // plan.size
-    return [(half * inner + block * wide, each, block * each) for block in range(blocks)]
+    each = inner // blocks // plan.size
+
+    def offset(block):
+        if blocks > 1:
+            return lambda member: half * inner + plan.flat(block, member) * each
+        return lambda member: half * inner + member * each
+
+    return [(offset(block), each, block * each) for block in range(blocks)]
 
 
 def columns_out(plan, dp, index, w_ref, out_ref, table, send_sem, recv_sem):
@@ -424,9 +596,9 @@
     rows = pl.ds(pl.multiple_of(index * own, own), own)
 
     def moves(other):
-        for base, each, place in table:
+        for offset, each, place in table:
             yield (
-                w_ref.at[:, pl.ds(pl.multiple_of(base + other * each, 128), each)],
+                w_ref.at[:, pl.ds(pl.multiple_of(offset(other), 128), each)],
                 out_ref.at[rows, pl.ds(place, each)],
             )
 
@@ -458,10 +630,10 @@
 
     def moves(other):
         rows = pl.ds(pl.multiple_of(other * own, own), own)
-        for base, each, place in table:
+        for offset, each, place in table:
             yield (
                 g_ref.at[rows, pl.ds(place, each)],
-                out_ref.at[:, pl.ds(pl.multiple_of(base + index * each, 128), each)],
+                out_ref.at[:, pl.ds(pl.multiple_of(offset(index), 128), each)],
             )
 
     def begin(plane):
@@ -490,49 +662,6 @@
     return begin, finish
 
 
-def hidden_backward(plan, g_low, rights, grad_out, branch, gain):
-    rows, width = branch.shape
-    count = len(rights)
-    depth = g_low.shape[1] // count
-
-    def kernel(*refs):
-        pairs = [(refs[0], i * depth, refs[1 + i]) for i in range(count)]
-        dy, u, g, grad, g_gain, low = refs[1 + count : 7 + count]
-        rest = refs[7 + count :]
-        dp, seq, index = plan.here()
-        greet([plan.across(dp, seq, bit) for bit in (1, 2, 4, 8)])
-        g_gain[...] = jnp.zeros_like(g_gain)
-
-        def write(here, value):
-            e = dy[here, :].astype(F32) + value
-            grad[here, :] = e
-            values = u[here, :]
-            r = lax.rsqrt(jnp.mean(values * values, axis=1, keepdims=True) + epsilon)
-            scaled = e * g[...]
-            inner = jnp.mean(scaled * values, axis=1, keepdims=True)
-            low[here, :] = (r * scaled - values * (r * r * r * inner)).astype(BF)
-            g_gain[...] += jnp.sum(e * values * r, axis=0, keepdims=True)
-
-        scatter_steps(plan, dp, seq, index, pairs, True, write, rest[:6], rest[6:])
-
-    return pl.pallas_call(
-        kernel,
-        out_shape=[
-            jax.ShapeDtypeStruct((rows, width), F32),
-            jax.ShapeDtypeStruct((1, width), F32),
-            jax.ShapeDtypeStruct((rows, width), BF),
-        ],
-        in_specs=[VM] * (4 + count),
-        out_specs=[VM] * 3,
-        scratch_shapes=scatter_scratch(rows, width),
-        compiler_params=pltpu.CompilerParams(
-            collective_id=7, has_side_effects=True, vmem_limit_bytes=48 * 2**20
-        ),
-        cost_estimate=LIGHT,
-        name="hidden_backward",
-    )(g_low, *rights, grad_out, branch, gain)
-
-
 def start_gather(plan, x, attn_w, gate_up_w, gains, segments, blocks):
     rows, width = x.shape
     own, both = gate_up_w.shape
@@ -545,7 +674,8 @@
         g_ref, d_ref = refs[count + 6 : count + 8]
         sems = refs[count + 8 :]
         gather_sems = sems[:7]
-        w_send, w_recv, u_send, u_recv, o_send, o_recv, g_send, g_recv, d_send, d_recv = sems[7:]
+        w_send, w_recv, u_send, u_recv, o_send, o_recv, g_send, g_recv, d_send, d_recv = sems[7:17]
+        far_send, far_recv = sems[17:]
         g_ref[...] = jnp.zeros_like(g_ref)
         for i, gain in enumerate(gain_refs):
             g_ref[i : i + 1, :own] = gain[...].astype(F32)
@@ -554,35 +684,44 @@
         me = dp * plan.seq + seq
         greet_all(plan, dp, seq)
         begin, finish = gather_steps(plan, x_ref, xo, dp, seq, index, gather_sems)
-        begin()
-        group = dp // plan.low
+        group = plan.group_of(dp)
+
         def columns(part, other):
             return pl.ds(pl.multiple_of(part * width + plan.head(other) * HEAD, HEAD), HEAD)
 
-        mine = pl.ds(pl.multiple_of(me * own, own), own)
-
-        def w_to(away, step, carry):
+        def rows_of(member):
+            return pl.ds(pl.multiple_of(plan.flat(group, member) * own, own), own)
+
+        def w_to(step, carry):
             other = (index + step) % plan.size
-            to_group = (group + away) % plan.groups
-            device = (to_group * plan.low + other // plan.seq, other % plan.seq)
             for part in range(3):
                 send(
                     w_ref.at[:, columns(part, other)],
-                    wo.at[mine, pl.ds(part * HEAD, HEAD)],
+                    wo.at[rows_of(index), pl.ds(part * HEAD, HEAD)],
                     w_send,
-                    w_recv,
-                    device,
+                    w_recv.at[index],
+                    plan.member(dp, other),
                 )
             return carry
 
-        for away in range(1, plan.groups):
-            lax.fori_loop(0, plan.size, functools.partial(w_to, away), 0)
-        lax.fori_loop(1, plan.size, functools.partial(w_to, 0), 0)
+        lax.fori_loop(1, plan.size, w_to, 0)
+        begin()
         for part in range(3):
             pltpu.make_async_copy(
-                w_ref.at[:, columns(part, index)], wo.at[mine, pl.ds(part * HEAD, HEAD)], w_recv
+                w_ref.at[:, columns(part, index)],
+                wo.at[rows_of(index), pl.ds(part * HEAD, HEAD)],
+                w_recv.at[index],
             ).start()
 
+        def onward(step, carry):
+            rows = wo.at[rows_of((index + plan.size - step) % plan.size)]
+            wait_bytes(rows, w_recv.at[(index + plan.size - step) % plan.size])
+            for away in range(1, plan.groups):
+                to_group = (group + away) % plan.groups
+                send(rows, rows, far_send, far_recv, plan.in_group(to_group, index))
+            return carry
+
+        lax.fori_loop(0, plan.size, onward, 0)
         feature = me * own
         keeper = plan.of_head(feature // HEAD)
         o_dst = oo.at[pl.ds(pl.multiple_of(feature % HEAD, own), own)]
@@ -590,7 +729,7 @@
 
         def o_to(away, carry):
             to_group = (group + away) % plan.groups
-            to_dp, to_seq = to_group * plan.low + keeper // plan.seq, keeper % plan.seq
+            to_dp, to_seq = plan.in_group(to_group, keeper)
             same = to_dp * plan.seq + to_seq == me
 
             @pl.when(same)
@@ -604,6 +743,8 @@
             return carry
 
         lax.fori_loop(0, plan.groups, o_to, 0)
+        begin_u, finish_u = columns_out(plan, dp, index, u_ref, uo, table, u_send, u_recv)
+        begin_u()
 
         def g_to(step, carry):
             other = (me + step) % plan.devices
@@ -619,20 +760,25 @@
 
         lax.fori_loop(1, plan.size, d_to, 0)
         pltpu.make_async_copy(d_ref, do.at[index], d_recv).start()
-        begin_u, finish_u = columns_out(plan, dp, index, u_ref, uo, table, u_send, u_recv)
-        begin_u()
         finish()
         finish_u()
         wait_bytes(go, g_recv)
         wait_bytes(do, d_recv)
-        wait_bytes(wo, w_recv)
+        far = wo.at[pl.ds(0, (plan.groups - 1) * plan.size * own)]
+        wait_bytes(far, far_recv)
+        wait_bytes(far, far_send)
 
         def sent(step, carry):
-            wait_bytes(w_ref.at[:, pl.ds(0, 3 * HEAD)], w_send)
             wait_bytes(g_ref, g_send)
             return carry
 
         lax.fori_loop(1, plan.devices, sent, 0)
+
+        def sent_w(step, carry):
+            wait_bytes(w_ref.at[:, pl.ds(0, 3 * HEAD)], w_send)
+            return carry
+
+        lax.fori_loop(1, plan.size, sent_w, 0)
 
         def sent_docs(step, carry):
             wait_bytes(d_ref, d_send)
@@ -643,7 +789,7 @@
 
         def sent_o(away, carry):
             to_group = (group + away) % plan.groups
-            to_dp, to_seq = to_group * plan.low + keeper // plan.seq, keeper % plan.seq
+            to_dp, to_seq = plan.in_group(to_group, keeper)
 
             @pl.when(to_dp * plan.seq + to_seq != me)
             def _():
@@ -652,7 +798,6 @@
             return carry
 
         lax.fori_loop(0, plan.groups, sent_o, 0)
-
 
     shapes = (
         ((plan.size * rows, width), BF),
@@ -669,6 +814,7 @@
         out_specs=[ANY] * 6,
         scratch_shapes=[pltpu.VMEM((8, 128), F32), pltpu.VMEM((8, rows), jnp.int32)]
         + list(GATHER_SEMS)
+        + [DMA, DMA((plan.size,))]
         + [DMA] * 10,
         compiler_params=pltpu.CompilerParams(collective_id=0, has_side_effects=True),
         cost_estimate=LIGHT,
@@ -688,140 +834,135 @@
     return lax.dot_general(left, right, (((0,), (0,)), ((), ())), preferred_element_type=F32)
 
 
-def plane_rows(index, plane, rows):
-    return pl.multiple_of(flips(index, 8 * plane) // 8 * (8 * rows), 8 * rows)
-
-
-def ffn_forward(plan, h, w_gate, w_up):
-    rows, width = h.shape
-    tokens = rows * plan.size
+def chip_rows(index, chip, rows):
+    return pl.multiple_of(flips(index, chip) // 2 * (2 * rows), 2 * rows)
+
+
+def ffn_forward(plan, h_all, w_gate, w_up):
+    tokens, width = h_all.shape
     units = w_gate.shape[1]
-
-    def kernel(h_ref, wg_ref, wu_ref, h_out, gate, up, act, h_all, wg, wu, *sems):
-        wg_sem, wu_sem, out_sem = sems[7:]
-        dp, seq, index = plan.here()
-        loads = [
-            pltpu.make_async_copy(wg_ref, wg, wg_sem),
-            pltpu.make_async_copy(wu_ref, wu, wu_sem),
-        ]
-        for load in loads:
-            load.start()
-        greet([plan.across(dp, seq, bit) for bit in (1, 2, 4, 8)])
-        begin, finish = gather_steps(plan, h_ref, h_all, dp, seq, index, sems[:7])
-        begin()
-        stores = []
-
-        def use(plane):
-            if plane == 0:
-                for load in loads:
-                    load.wait()
-            first = plane_rows(index, plane, rows)
-            here = pl.ds(first, 8 * rows)
-            stores.append(pltpu.make_async_copy(h_all.at[here], h_out.at[here], out_sem.at[plane]))
-            stores[-1].start()
-
-            @pl.loop(0, 8 * rows // STEP)
-            def _(i):
-                some = pl.ds(pl.multiple_of(first + i * STEP, STEP), STEP)
-                values = h_all[some, :]
-                g = dot(values, wg[...])
-                u = dot(values, wu[...])
-                gate[some, :] = g.astype(BF)
-                up[some, :] = u.astype(BF)
-                act[some, :] = (g * jax.nn.sigmoid(g) * u).astype(BF)
-
-        finish(use)
-        for store in stores:
-            store.wait()
-
-    part = jax.ShapeDtypeStruct((tokens, units), BF)
+    moves = plan.natural(width)
+
+    def kernel(h, wg_ref, wu_ref, gate, up, act, wg, wu, sem):
+        @pl.when(pl.program_id(0) == 0)
+        def _():
+            pieces = [
+                (src.at[pl.ds(first, rows)], dst.at[pl.ds(to, rows)])
+                for src, dst in ((wg_ref, wg), (wu_ref, wu))
+                for first, to, rows in moves
+            ]
+            Loads(*zip(*pieces), sem).wait()
+
+        values = h[...]
+        g = dot(values, wg[...])
+        u = dot(values, wu[...])
+        gate[...] = g.astype(BF)
+        up[...] = u.astype(BF)
+        act[...] = (g * jax.nn.sigmoid(g) * u).astype(BF)
+
+    rows = 2 * STEP
+    part = pl.BlockSpec((rows, units), lambda i: (i, 0))
     return pl.pallas_call(
         kernel,
-        out_shape=[jax.ShapeDtypeStruct((tokens, width), BF), part, part, part],
-        in_specs=[VM, ANY, ANY],
-        out_specs=[ANY, VM, VM, VM],
-        scratch_shapes=[
-            pltpu.VMEM((tokens, width), BF),
-            pltpu.VMEM(w_gate.shape, BF),
-            pltpu.VMEM(w_up.shape, BF),
-        ]
-        + list(GATHER_SEMS)
-        + [DMA, DMA, DMA((2,))],
-        compiler_params=pltpu.CompilerParams(
-            collective_id=9, has_side_effects=True, vmem_limit_bytes=48 * 2**20
-        ),
+        grid=(tokens // rows,),
+        out_shape=[jax.ShapeDtypeStruct((tokens, units), BF)] * 3,
+        in_specs=[pl.BlockSpec((rows, width), lambda i: (i, 0)), ANY, ANY],
+        out_specs=[part] * 3,
+        scratch_shapes=[like(w_gate), like(w_up), DMA((2 * len(moves),))],
+        compiler_params=pltpu.CompilerParams(vmem_limit_bytes=60 * 2**20),
         cost_estimate=LIGHT,
         name="ffn_forward",
-    )(h, w_gate, w_up)
+    )(h_all, w_gate, w_up)
 
 
 def ffn_backward(plan, d, h_all, w_down, gate, up, act):
     rows, width = d.shape
     tokens = rows * plan.size
-    half = tokens // 2
-    units = w_down.shape[0]
+    units = gate.shape[1]
+    at_dp = width // plan.dp
     tile = 256
+    two = 2 * rows
 
     def kernel(d_ref, *refs):
-        ins, (out, g_gate, g_up, g_down), held = refs[:5], refs[5:9], refs[9:14]
-        d_all, gu_turned, act_turned, gu_sum, down_sum = refs[14:19]
-        sems, load_sems = refs[19:26], refs[26]
-        h_all, wd, gate, up, act = held
+        ins, refs = refs[:5], refs[5:]
+        outs, (h_all, wd, gate, up, act) = refs[:4], refs[4:9]
+        d_all, gu_turned, act_turned, gu_sum, down_sum, out, g_gate, g_up, g_down = refs[9:18]
+        sems, load_sems, store_sems, out_sems = refs[18:25], refs[25], refs[26], refs[27]
         dp, seq, index = plan.here()
-        loads = [
-            pltpu.make_async_copy(src, dst, load_sems.at[i])
-            for i, (src, dst) in enumerate(zip(ins, held))
-        ]
-        for load in loads[1:] + loads[:1]:
-            load.start()
+        loads = Loads(ins, (wd, gate, up, act, h_all), load_sems)
         greet([plan.across(dp, seq, bit) for bit in (1, 2, 4, 8)])
         begin, finish = gather_steps(plan, d_ref, d_all, dp, seq, index, sems)
         begin()
-
-        def use(plane):
-            if plane == 0:
-                for load in loads:
-                    load.wait()
-            first = plane_rows(index, plane, rows)
-            here = pl.ds(first, half)
-
-            @pl.loop(0, half // STEP)
-            def _(i):
-                some = pl.ds(pl.multiple_of(first + i * STEP, STEP), STEP)
-                columns = pl.ds(pl.multiple_of(i * STEP, STEP), STEP)
-                grad = contract_last(d_all[some, :], wd[...])
-                g = gate[some, :].astype(F32)
-                u = up[some, :].astype(F32)
-                sigma = jax.nn.sigmoid(g)
-                grad_gate = (grad * u * sigma * (1.0 + g * (1.0 - sigma))).astype(BF)
-                grad_up = (grad * (g * sigma)).astype(BF)
-                out[some, pl.ds(0, units)] = grad_gate
-                out[some, pl.ds(units, units)] = grad_up
-                gu_turned[pl.ds(0, units), columns] = grad_gate.T
-                gu_turned[pl.ds(units, units), columns] = grad_up.T
-                act_turned[:, columns] = act[some, :].T
+        stores = []
+        pair = []
+
+        def products(first, last):
+            chips = [pl.ds(chip_rows(index, chip, rows), two) for chip in pair]
 
             @pl.loop(0, width // tile)
             def _(i):
                 columns = pl.ds(pl.multiple_of(i * tile, tile), tile)
-                block = dot(gu_turned[...], h_all[here, columns])
-                if plane == 0:
+                block = dot(
+                    gu_turned[...],
+                    jnp.concatenate([h_all[chip, columns] for chip in chips], axis=0),
+                )
+                if not first:
+                    block = gu_sum[:, columns] + block
+                if last:
+                    block = block.T.astype(BF)
+                    row = i * tile
+                    row = plan.place(row // at_dp) * at_dp + row % at_dp
+                    to = pl.ds(pl.multiple_of(row, tile), tile)
+                    g_gate[to, :] = block[:, :units]
+                    g_up[to, :] = block[:, units:]
+                else:
                     gu_sum[:, columns] = block
-                else:
-                    block = (gu_sum[:, columns] + block).T.astype(BF)
-                    g_gate[columns, :] = block[:, :units]
-                    g_up[columns, :] = block[:, units:]
 
             @pl.loop(0, width // tile)
             def _(i):
                 columns = pl.ds(pl.multiple_of(i * tile, tile), tile)
-                block = dot(act_turned[...], d_all[here, columns])
-                if plane == 0:
+                block = dot(
+                    act_turned[...],
+                    jnp.concatenate([d_all[chip, columns] for chip in chips], axis=0),
+                )
+                if not first:
+                    block = down_sum[:, columns] + block
+                if last:
+                    g_down[:, columns] = block.astype(BF)
+                else:
                     down_sum[:, columns] = block
-                else:
-                    g_down[:, columns] = (down_sum[:, columns] + block).astype(BF)
+
+        def use(chip):
+            if chip == 0:
+                loads.wait()
+            some = pl.ds(chip_rows(index, chip, rows), two)
+            columns = pl.ds(len(pair) * two, two)
+            grad = contract_last(d_all[some, :], wd[...])
+            g = gate[some, :].astype(F32)
+            u = up[some, :].astype(F32)
+            sigma = jax.nn.sigmoid(g)
+            grad_gate = (grad * u * sigma * (1.0 + g * (1.0 - sigma))).astype(BF)
+            grad_up = (grad * (g * sigma)).astype(BF)
+            out[some, pl.ds(0, units)] = grad_gate
+            out[some, pl.ds(units, units)] = grad_up
+            store = pltpu.make_async_copy(out.at[some], outs[0].at[some], store_sems.at[chip // 2])
+            store.start()
+            stores.append(store)
+            gu_turned[pl.ds(0, units), columns] = grad_gate.T
+            gu_turned[pl.ds(units, units), columns] = grad_up.T
+            act_turned[:, columns] = act[some, :].T
+            pair.append(chip)
+            if len(pair) == 2:
+                products(len(stores) == 2, len(stores) == 8)
+                pair.clear()
 
         finish(use)
+        for i, src in enumerate((g_gate, g_up, g_down)):
+            store = pltpu.make_async_copy(src, outs[1 + i], out_sems.at[i])
+            store.start()
+            stores.append(store)
+        for store in stores:
+            store.wait()
 
     return pl.pallas_call(
         kernel,
@@ -832,24 +973,29 @@
             jax.ShapeDtypeStruct((units, width), BF),
         ],
         in_specs=[VM] + [ANY] * 5,
-        out_specs=[VM] * 4,
+        out_specs=[ANY] * 4,
         scratch_shapes=[
-            pltpu.VMEM(value.shape, BF) for value in (h_all, w_down, gate, up, act, h_all)
+            pltpu.VMEM(shape, BF)
+            for shape in (h_all.shape, (units, width), gate.shape, up.shape, act.shape, h_all.shape)
         ]
         + [
-            pltpu.VMEM((2 * units, half), BF),
-            pltpu.VMEM((units, half), BF),
+            pltpu.VMEM((2 * units, 2 * two), BF),
+            pltpu.VMEM((units, 2 * two), BF),
             pltpu.VMEM((2 * units, width), F32),
             pltpu.VMEM((units, width), F32),
+            pltpu.VMEM((tokens, 2 * units), BF),
+            pltpu.VMEM((width, units), BF),
+            pltpu.VMEM((width, units), BF),
+            pltpu.VMEM((units, width), BF),
         ]
         + list(GATHER_SEMS)
-        + [DMA((5,))],
+        + [DMA((5,)), DMA((8,)), DMA((3,))],
         compiler_params=pltpu.CompilerParams(
             collective_id=10, has_side_effects=True, vmem_limit_bytes=62 * 2**20
         ),
         cost_estimate=LIGHT,
         name="ffn_backward",
-    )(d, h_all, w_down, gate, up, act)
+    )(d, w_down, gate, up, act, h_all)
 
 
 def row_sums(values):
@@ -925,16 +1071,26 @@
     own, both = gate_up_w.shape
     table = half_columns(plan, both // 2, blocks, 1)
 
-    def kernel(x, wq, up, ga, do, cs, sn, uo, q, k, sums, ql, kl, vl, mixed, *rest):
+    def kernel(x_ref, wq_ref, up, ga, do, cs_ref, sn_ref, uo, q, k, sums, ql, kl, vl, mixed, *rest):
+        x, wq, cs, sn, sem = rest[:5]
+        loads = Loads((wq_ref, cs_ref, sn_ref), (wq, cs, sn), sem)
+        step_rows = [pl.ds(i * STEP, STEP) for i in range(tokens // STEP)]
+        Loads(
+            [x_ref.at[rows] for rows in step_rows], [x.at[rows] for rows in step_rows], rest[5]
+        )
+        tile_sem, rest = rest[5], rest[6:]
         gn, dr, stats, held, t_send, t_recv, u_send, u_recv = rest
         dp, seq, index = plan.here()
         greet_group(plan, dp, index)
         lay_out(do, dr)
         for which in range(2):
             gn[which : which + 1, :] = my_gain(plan, ga, which, plan.head(index))
+        loads.wait()
+
         @pl.loop(0, tokens // STEP)
         def _(i):
             rows = pl.ds(pl.multiple_of(i * STEP, STEP), STEP)
+            pltpu.make_async_copy(x_ref.at[rows], x.at[rows], tile_sem.at[i]).wait()
             block = dot(x[rows, :], wq[...])
             q[rows, :] = block[:, :HEAD]
             k[rows, :] = block[:, HEAD : 2 * HEAD]
@@ -987,9 +1143,11 @@
     return pl.pallas_call(
         kernel,
         out_shape=[jax.ShapeDtypeStruct(*shape) for shape in shapes],
-        in_specs=[VM, VM, ANY] + [VM] * 4,
+        in_specs=[ANY] * 3 + [VM] * 2 + [ANY] * 2,
         out_specs=[ANY] + [VM] * 7,
-        scratch_shapes=[
+        scratch_shapes=[like(value) for value in (x_all, w_qkv, cosine, sine)]
+        + [DMA((3,)), DMA((tokens // STEP,))]
+        + [
             pltpu.VMEM((8, HEAD), F32),
             pltpu.VMEM((1, tokens), F32),
             pltpu.VMEM((2, 1, tokens), F32),
@@ -1024,19 +1182,20 @@
 ):
     rows_here, width = b.shape
     tokens = rows_here * plan.size
-    in_plane = 8 * rows_here
     own = g_gate.shape[0] // plan.size
     inner = g_gate.shape[1] * plan.size
     length = cosine.shape[0]
     scale = HEAD ** (-0.5)
 
     def kernel(*refs):
-        b_ref, wo, q, k, sums, ql, kl, vl, mx, ga, do, cs, sn, gg = refs[:14]
+        b_ref, sums, ga, do, gg = refs[:5]
+        wo, q, k, ql, kl, vl, mx, cs, sn = refs[30:39]
+        loads = Loads(refs[5:14], refs[30:39], refs[39])
         dqkv, g_out, g_gain, gate_out = refs[14:18]
         ba, dq, dk, dv, gn, dr, stats, held, t_send, t_recv, gg_send, gg_recv = refs[18:30]
         dp, seq, index = plan.here()
         greet_group(plan, dp, index)
-        begin_b, finish_b = gather_steps(plan, b_ref, ba, dp, seq, index, refs[30:])
+        begin_b, finish_b = gather_steps(plan, b_ref, ba, dp, seq, index, refs[40:])
         begin_b()
         lay_out(do, dr)
         for which in range(2):
@@ -1047,27 +1206,35 @@
         dk[...] = jnp.zeros_like(dk)
         dv[...] = jnp.zeros_like(dv)
 
-        def use(plane):
-            if plane == 1:
+        def use(chip):
+            if chip == 0:
+                loads.wait()
+            if chip == 8:
+                begin_g(1)
+            if chip == 10:
                 begin_g(0)
-            plane_first = plane_rows(index, plane, rows_here)
-            for j in range(in_plane // STEP):
-                first = pl.multiple_of(plane_first + j * STEP, STEP)
-                rows = pl.ds(first, STEP)
-                start = first % length
-                count = (j + 1) * STEP if length == in_plane else length
-                base = pl.multiple_of(first - start, STEP)
-                keys = pl.ds(base, count)
+            first = chip_rows(index, chip, rows_here)
+            rows = pl.ds(first, STEP)
+            start = first % length
+
+            def block(count):
+                keys = pl.ds(pl.multiple_of(first - start, STEP), count)
                 grad = contract_last(ba[rows, :], wo[...]).astype(BF)
-                probs = scores_of(
-                    ql[rows, :], kl[keys, :], dr[:, rows], dr[:, keys], start
-                )
+                probs = scores_of(ql[rows, :], kl[keys, :], dr[:, rows], dr[:, keys], start)
                 grad_probs = contract_last(grad, vl[keys, :])
                 delta = jnp.sum(probs * grad_probs, axis=1, keepdims=True)
                 grad_scores = (probs * (grad_probs - delta)).astype(BF)
                 dq[rows, :] = dot(grad_scores, kl[keys, :]) * scale
                 dk[keys, :] += contract_first(grad_scores, ql[rows, :]) * scale
                 dv[keys, :] += contract_first(probs.astype(BF), grad)
+
+            @pl.when(start < length // 2)
+            def _():
+                block(length // 2)
+
+            @pl.when(start >= length // 2)
+            def _():
+                block(length)
 
         finish_b(use)
 
@@ -1083,7 +1250,6 @@
 
         begin, finish = swap_sums(plan, dp, index, stats, held, t_send, t_recv)
         begin()
-        begin_g(1)
         turned_mixed = mx[...].T
 
         @pl.loop(0, width // 512)
@@ -1119,7 +1285,7 @@
     return pl.pallas_call(
         kernel,
         out_shape=[jax.ShapeDtypeStruct(*shape) for shape in shapes],
-        in_specs=[VM] * 13 + [ANY],
+        in_specs=[VM] * 4 + [ANY] * 10,
         out_specs=[VM] * 3 + [ANY],
         scratch_shapes=[
             pltpu.VMEM((tokens, width), BF),
@@ -1132,28 +1298,15 @@
             pltpu.VMEM((plan.size, 2, 1, tokens), F32),
         ]
         + [DMA] * 4
+        + [like(value) for value in (w_out, q, k, ql, kl, vl, mixed, cosine, sine)]
+        + [DMA((9,))]
         + list(GATHER_SEMS),
         compiler_params=pltpu.CompilerParams(
             collective_id=4, has_side_effects=True, vmem_limit_bytes=56 * 2**20
         ),
         cost_estimate=LIGHT,
         name="attend_backward",
-    )(
-        b,
-        w_out,
-        q,
-        k,
-        sums,
-        ql,
-        kl,
-        vl,
-        mixed,
-        gains,
-        docs,
-        cosine,
-        sine,
-        g_gate,
-    )
+    )(b, sums, gains, docs, g_gate, w_out, q, k, ql, kl, vl, mixed, cosine, sine)
 
 
 def finish_backward(
@@ -1165,14 +1318,20 @@
     inner = g_up.shape[1] * plan.size
     pieces = HEAD // own
     tile = 256
-
-    def kernel(dq, wq, x, gu, go, gh, gat, gff, bf, ig, w_grad, up_out, ga_out, *rest):
+    at_dp = width // plan.dp
+    per_dp = at_dp // tile
+    tiles = width // plan.groups // tile
+
+    def kernel(dq_ref, wq_ref, x_ref, gu, go, gh, gat, gff, bf, ig, w_grad, up_out, ga_out, *rest):
+        (dq, wq, x), load_sem = rest[:3], rest[3]
+        loads = Loads((dq_ref, wq_ref, x_ref), (dq, wq, x), load_sem)
+        rest = rest[4:]
         bufs, sems = rest[:6], rest[6:12]
-        turned, gq, got_q, got_o, ga = rest[12:17]
-        q_s, q_r, o_s, o_r, ga_s, ga_r, gu_s, gu_r = rest[17:]
+        turned, gq, gq_far, got_x, got_q, got_o, ga = rest[12:19]
+        q_s, q_r, o_s, o_r, ga_s, ga_r, gu_s, gu_r, x_s, x_r = rest[19:]
         dp, seq, index = plan.here()
         me = dp * plan.seq + seq
-        group = dp // plan.low
+        group = plan.group_of(dp)
         greet_all(plan, dp, seq)
 
         def device_of(flat):
@@ -1197,46 +1356,67 @@
             send(ga.at[other], ga_out.at[me], ga_s, ga_r, device_of(other))
             return carry
 
-        tiles = width // tile
         table = half_columns(plan, inner, blocks, 0)
         begin_u, finish_u = columns_back(plan, dp, index, gu, up_out, table, gu_s, gu_r)
 
-        def weights(first, last):
-            @pl.loop(first, last)
-            def _(i):
-                at = (i + (me * own) // tile) % tiles
-                columns = pl.ds(pl.multiple_of(at * tile, tile), tile)
-                block = dot(turned[...], x[:, columns])
-                gq[columns, :] = block.T.astype(BF)
-
-                def q_to(piece, carry):
-                    other = at * (tile // own) + piece
-                    src = gq.at[pl.ds(pl.multiple_of(other * own, own), own)]
-
-                    @pl.when(other == me)
-                    def _():
-                        pltpu.make_async_copy(src, got_q.at[group, index], q_r).start()
-
-                    @pl.when(other != me)
-                    def _():
-                        send(src, got_q.at[group, index], q_s, q_r, device_of(other))
-
-                    return carry
-
-                lax.fori_loop(0, tile // own, q_to, 0)
+        def product(of_group, u):
+            row = plan.dp_of(of_group, u // per_dp) * at_dp + (u % per_dp) * tile
+            block = dot(turned[...], x[:, pl.ds(pl.multiple_of(row, tile), tile)])
+            return block.T.astype(BF)
+
+        def others():
+            for away in range(1, plan.groups):
+                to_group = (group + away) % plan.groups
+
+                @pl.loop(0, tiles)
+                def _(u, away=away, to_group=to_group):
+                    gq_far[away - 1, u] = product(to_group, u)
+                    send(
+                        gq_far.at[away - 1, u],
+                        got_x.at[away - 1, u],
+                        x_s,
+                        x_r.at[away - 1, u],
+                        plan.in_group(to_group, index),
+                    )
+
+        def ours():
+            @pl.loop(0, tiles)
+            def _(u):
+                gq[u] = product(group, u)
+
+        def collect():
+            @pl.loop(0, tiles)
+            def _(u):
+                total = gq[u].astype(F32)
+                for away in range(1, plan.groups):
+                    wait_bytes(got_x.at[away - 1, u], x_r.at[away - 1, u])
+                    total = total + got_x[away - 1, u].astype(F32)
+                gq[u] = total.astype(BF)
+                owner_dp = plan.dp_of(group, u // per_dp)
+                for piece in range(tile // own):
+                    owner_seq = (u % per_dp) * (tile // own) + piece
+                    src = gq.at[u, pl.ds(piece * own, own)]
+                    mine = owner_dp * plan.seq + owner_seq == me
+
+                    @pl.when(mine)
+                    def _(src=src):
+                        pltpu.make_async_copy(src, got_q.at[index], q_r).start()
+
+                    @pl.when(jnp.logical_not(mine))
+                    def _(src=src, owner_seq=owner_seq):
+                        send(src, got_q.at[index], q_s, q_r, (owner_dp, owner_seq))
 
         def meanwhile(i):
             if i == 0:
+                loads.wait(2)
                 turned[...] = dq[...].T
-                weights(0, tiles // 4)
+                others()
             elif i == 1:
-                weights(tiles // 4, 5 * tiles // 8)
+                ours()
             elif i == 2:
                 lax.fori_loop(0, pieces, o_to, 0)
-                begin_u(1)
             else:
-                begin_u(0)
-                weights(5 * tiles // 8, tiles)
+                collect()
                 ga[...] = jnp.zeros_like(ga)
                 for other in range(plan.devices):
                     part = slice(other * own, (other + 1) * own)
@@ -1251,16 +1431,15 @@
         def write(here, value):
             ig[here, :] = bf[here, :] + value
 
+        begin_u(1)
+        begin_u(0)
+        loads.wait(0, 1)
         scatter_steps(plan, dp, seq, index, [(dq, 0, wq)], True, write, bufs, sems, meanwhile)
         wait_bytes(got_o, o_r)
         wait_bytes(got_q, q_r)
         for part in range(3):
             for member in range(plan.size):
-                total = got_q[0, member, :, part * HEAD : (part + 1) * HEAD].astype(F32)
-                for other in range(1, plan.groups):
-                    total = total + got_q[
-                        other, member, :, part * HEAD : (part + 1) * HEAD
-                    ].astype(F32)
+                total = got_q[member, :, part * HEAD : (part + 1) * HEAD].astype(F32)
                 w_grad[:, pl.ds(part * width + plan.head(member) * HEAD, HEAD)] = total
         total = got_o[0].astype(F32)
         for other in range(1, plan.groups):
@@ -1269,7 +1448,8 @@
         finish_u()
         wait_bytes(ga_out, ga_r)
         wait_bytes(ga_out.at[pl.ds(0, plan.devices - 1)], ga_s)
-        wait_bytes(gq.at[pl.ds(0, width - own)], q_s)
+        wait_bytes(got_q.at[pl.ds(0, plan.size - 1)], q_s)
+        wait_bytes(gq_far, x_s)
 
         def sent_o(piece, carry):
             @pl.when(plan.head(index) * pieces + piece != me)
@@ -1289,17 +1469,22 @@
     return pl.pallas_call(
         kernel,
         out_shape=[jax.ShapeDtypeStruct(*shape) for shape in shapes],
-        in_specs=[VM, VM, VM, ANY] + [VM] * 5,
+        in_specs=[ANY] * 5 + [VM] * 4,
         out_specs=[VM, VM, ANY, VM],
-        scratch_shapes=scatter_scratch(rows, width)
+        scratch_shapes=[like(value) for value in (dqkv, w_qkv, x_all)]
+        + [DMA((3,))]
+        + scatter_scratch(rows, width)
         + [
             pltpu.VMEM((3 * HEAD, tokens), BF),
-            pltpu.VMEM((width, 3 * HEAD), BF),
-            pltpu.VMEM((plan.groups, plan.size, own, 3 * HEAD), BF),
+            pltpu.VMEM((tiles, tile, 3 * HEAD), BF),
+            pltpu.VMEM((plan.groups - 1, tiles, tile, 3 * HEAD), BF),
+            pltpu.VMEM((plan.groups - 1, tiles, tile, 3 * HEAD), BF),
+            pltpu.VMEM((plan.size, own, 3 * HEAD), BF),
             pltpu.VMEM((plan.groups, own, width), BF),
             pltpu.VMEM((plan.devices, 8, 128), F32),
         ]
-        + [DMA] * 8,
+        + [DMA] * 9
+        + [DMA((plan.groups - 1, tiles))],
         compiler_params=pltpu.CompilerParams(
             collective_id=5, has_side_effects=True, vmem_limit_bytes=60 * 2**20
         ),
@@ -1330,11 +1515,10 @@
     groups = plan.groups
     dp, seq, index = plan.here()
     me = dp * plan.seq + seq
-    group = dp // plan.low
     direct = (inner // (groups * plan.size)) % 128 == 0
     blocks = groups if direct else 1
 
-    across = [[low + high * plan.low for high in range(groups)] for low in range(plan.low)]
+    across = [[plan.dp_of(high, low) for high in range(groups)] for low in range(plan.low)]
 
     def join_groups(value):
         return lax.all_gather(value, "dp", axis_index_groups=across, axis=0, tiled=True)
@@ -1380,30 +1564,16 @@
         w_all = lax.all_gather(down_weights, ("dp", "seq"), axis=0, tiled=True)
         each = inner // plan.size
         w_down = lax.dynamic_slice_in_dim(w_all, index * each, each, 0)
-    branch = scatter_dot(plan, mixed, [w_out], False, 2)
+    branch, hidden, _, h_all = hidden_forward(plan, mixed, w_out, x, gains[:1])
     branch, w_gate = lax.optimization_barrier((branch, w_gate))
 
-    def rms(values):
-        return lax.rsqrt(jnp.mean(values * values, axis=1, keepdims=True) + epsilon)
-
-    def rms_back(values, r, gain, grad):
-        scaled = gain * grad
-        inner_sum = jnp.mean(scaled * values, axis=1, keepdims=True)
-        return r * scaled - values * (r * r * r * inner_sum), jnp.sum(grad * values * r, axis=0)
-
-    branch_r = rms(branch)
-    hidden = x.astype(F32) + branch * branch_r * gains[0]
-    hidden_low = hidden.astype(BF)
-
-    h_all, gate, up, act = ffn_forward(plan, hidden_low, w_gate, w_up)
-    down = scatter_dot(plan, act, [w_down], False, 6)
-    down_r = rms(down)
-    output = (hidden + down * down_r * gains[1]).astype(BF)
-
-    grad_out = cotangent[0].astype(F32)
-    grad_down_in, grad_fg = rms_back(down, down_r, gains[1], grad_out)
+    gate, up, act = ffn_forward(plan, h_all, w_gate, w_up)
+    output, grad_down_in, grad_fg = output_norm(
+        plan, act, w_down, hidden, cotangent[0], gains[1:]
+    )
+
     gu_low, g_gate, g_up, g_down = ffn_backward(
-        plan, grad_down_in.astype(BF), h_all, w_down, gate, up, act
+        plan, grad_down_in, h_all, w_down, gate, up, act
     )
     g_gate = sum_groups(g_gate)
     g_up = sum_groups(g_up)
@@ -1447,7 +1617,7 @@
         g_out,
         g_head,
         grad_ag,
-        grad_fg.reshape(1, width),
+        grad_fg,
         grad_hidden,
         blocks,
     )

time: 631 us -> 575 us (0.911)
  waiting for transfers between devices: 25.4 us -> 1.89 us
  Pallas kernels: 560 us -> 538 us
  local copies, waits for them, and re-layouts: 13.8 us -> 6 us
    all_gather x3, waiting for transfers between devices: 23.8 us -> 0.06 us  [join_groups(): lax.all_gather(value, 'dp', axis_index_groups=across, axis=0, tiled=True)]
    pallas_call x1, Pallas kernels: 90.9 us -> 69.9 us  [attend_backward(): pl.pallas_call(kernel, out_shape=[jax.ShapeDtypeStruct(*shape) for shape...]
    pallas_call x4, Pallas kernels: 194 us -> 204 us  [the longest x3 190 us: scatter_call(): pl.pallas_call(kernel, out_shape=shapes, in_specs=[ANY] * (1 + count) + [...]
    unnamed x34 -> x11, local copies, waits for them, and re-layouts: 12.1 us -> 3.1 us
    pallas_call x1, Pallas kernels: 64.3 us -> 56.6 us  [ffn_backward(): pl.pallas_call(kernel, out_shape=[jax.ShapeDtypeStruct((tokens, 2 * units...]
  transfers between devices with their start and end apart: 6 -> 6, of which waited for: 2 -> 0; matrix products, arithmetic and copies ran while one was open for 1% -> 1% of each run, Pallas kernels for 60% -> 62%
where the time goes in v4:
time: 575 us; the launch traced here: 569 us
  Pallas kernels  538 us (94%)
  between operations  14.4 us (3%)
  other arithmetic  7.36 us (1%)
  local copies, waits for them, and re-layouts  6 us (1%)
    pallas_call x3, Pallas kernels, scatter_call(): pl.pallas_call(kernel, out_shape=shapes, in_specs=[ANY] * (1 + count) + [...  190 us
    pallas_call x1, Pallas kernels, finish_backward(): pl.pallas_call(kernel, out_shape=[jax.ShapeDtypeStruct(*shape) for shape...  82 us
    pallas_call x1, Pallas kernels, start_gather(): pl.pallas_call(kernel, out_shape=[jax.ShapeDtypeStruct(*shape) for shape...  81.5 us
    pallas_call x1, Pallas kernels, attend_backward(): pl.pallas_call(kernel, out_shape=[jax.ShapeDtypeStruct(*shape) for shape...  69.9 us
    pallas_call x1, Pallas kernels, ffn_backward(): pl.pallas_call(kernel, out_shape=[jax.ShapeDtypeStruct((tokens, 2 * units...  56.6 us
    pallas_call x1, Pallas kernels, attend_forward(): pl.pallas_call(kernel, out_shape=[jax.ShapeDtypeStruct(*shape) for shape...  44.4 us
    pallas_call x1, Pallas kernels, ffn_forward(): pl.pallas_call(kernel, grid=(tokens // rows,), out_shape=[jax.ShapeDtypeS...  14.4 us
  transfers between devices with their start and end apart: 6, of which 0 were waited for; matrix products, arithmetic and copies ran while one was open for 1% of the time, Pallas kernels for 62%

profile of v4, /device:TPU:15, one launch (start us, length us, event | category | flops | bytes accessed | tf_op | source)
XLA Modules:
  0.0 568.7 jit_solution(6554368097195414649)
XLA Ops:
  7.2 0.0 all-gather.4.cloned.1.call-start
  7.2 81.5 %start_gather.1 = (bf16[2048,2048]{1,0:T(8,128)(2,1)}, bf16[2048,384]{1,0:T(8,128)(2,1)}, bf16[1024,512]{1,0:T(8,128)(2,1)}, bf16[128,2048]{1,0:T(8,128)(2,1)}, ...) custom-call(bf16[128,2048]{1,0:T(8,128)(2,1)} %bitcast.18, bf16[64,8192]{1,0:T(8,128)(2,1)} %w_ref.1, bf16[64,16384]{1,0:T(8,128)(2,1)} %up.1, ...), custom_call_target="tpu_custom_call" | custom-call | tf_op jit(solution)/shard_map/start_gather/pallas_call | solution.py:810
  88.7 0.0 all-gather.6.cloned.1.call-start
  88.8 44.4 %attend_forward.1 = (bf16[1024,512]{1,0:T(8,128)(2,1)}, f32[2048,128]{1,0:T(8,128)}, f32[2048,128]{1,0:T(8,128)}, f32[2,1,2048]{2,1,0:T(1,128)}, bf16[2048,128]{...) custom-call(bf16[2048,2048]{1,0:T(8,128)(2,1)} %get-tuple-element.50.x_ref, ...), custom_call_target="tpu_custom_call" | custom-call | tf_op jit(solution)/shard_map/attend_forward/pallas_call | solution.py:1143
  133.2 0.0 all-gather.8.cloned.1.call-start
  133.2 0.7 all-gather.8.cloned.1.call-update
  133.9 0.6 reduce-scatter.4.cloned.1.call-start
  134.5 0.9 slice_bitcast_fusion
  135.4 0.1 slice_reduce_fusion
  135.5 0.7 slice.37.refs_4_
  136.2 0.7 slice.35.refs_3_.refs_5_
  136.9 91.7 %hidden_forward.1 = (f32[128,2048]{1,0:T(8,128)}, f32[128,2048]{1,0:T(8,128)}, bf16[128,2048]{1,0:T(8,128)(2,1)}, bf16[2048,2048]{1,0:T(8,128)(2,1)}) custom-call(bf16[2048,128]{1,0:T(8,128)(2,1)} %get-tuple-element.54.refs_0_.refs_11_, bf16[128,2048]{1,0:T(8,128)(2,1)} %get-tuple-element.55.refs_1_.refs_5_, bf16[128,2048]{1,0:T(8,128)(2,1)} %bitcast.19, ...), custom_call_target="tpu_custom_call" | custom-call | tf_op jit(solution)/shard_map/hidden_forward/pallas_call | solution.py:481
  228.6 0.0 all-gather.4.cloned.1.call-done.wg_ref.refs_1_
  228.6 14.4 %ffn_forward.1 = (bf16[2048,512]{1,0:T(8,128)(2,1)}, bf16[2048,512]{1,0:T(8,128)(2,1)}, bf16[2048,512]{1,0:T(8,128)(2,1)}) custom-call(bf16[2048,2048]{1,0:T(8,128)(2,1)} %get-tuple-element.56.h.refs_4_, bf16[2048,512]{1,0:T(8,128)(2,1)} %all-gather.4.cloned.1.call-done.wg_ref.refs_1_, bf16[2048,512]{1,0:T(8,128)(2,1)} %all-gather.6.cloned.1.call-done.wu_ref.refs_2_), custom_call_target="tpu_custom_call" | custom-call | tf_op jit(solution)/shard_map/ffn_forward/pallas_call | solution.py:865
  243.0 0.0 all-gather.8.cloned.1.call-done.refs_1_.refs_0_
  243.0 48.7 %output_norm.1 = (bf16[128,2048]{1,0:T(8,128)(2,1)}, bf16[128,2048]{1,0:T(8,128)(2,1)}, f32[1,2048]{1,0:T(1,128)}) custom-call(bf16[2048,512]{1,0:T(8,128)(2,1)} %get-tuple-element.61.refs_0_.refs_3_, bf16[512,2048]{1,0:T(8,128)(2,1)} %all-gather.8.cloned.1.call-done.refs_1_.refs_0_, f32[128,2048]{1,0:T(8,128)} %get-tuple-element.63.refs_2_, ...), custom_call_target="tpu_custom_call" | custom-call | tf_op jit(solution)/shard_map/output_norm/pallas_call | solution.py:481
  291.8 56.6 %ffn_backward.1 = (bf16[2048,1024]{1,0:T(8,128)(2,1)}, bf16[2048,512]{1,0:T(8,128)(2,1)}, bf16[2048,512]{1,0:T(8,128)(2,1)}, bf16[512,2048]{1,0:T(8,128)(2,1)}) custom-call(bf16[128,2048]{1,0:T(8,128)(2,1)} %get-tuple-element.65.d_ref, bf16[512,2048]{1,0:T(8,128)(2,1)} %all-gather.8.cloned.1.call-done.refs_1_.refs_0_, ...), custom_call_target="tpu_custom_call" | custom-call | tf_op jit(solution)/shard_map/ffn_backward/pallas_call | solution.py:967
  348.4 0.0 reduce-scatter.6.cloned.1.call-start
  348.4 0.5 reduce-scatter.6.cloned.1.call-update
  349.0 0.0 reduce-scatter.8.cloned.1.call-start
  349.0 0.5 reduce-scatter.8.cloned.1.call-update
  349.5 49.1 %hidden_backward.1 = (f32[128,2048]{1,0:T(8,128)}, f32[1,2048]{1,0:T(1,128)}, bf16[128,2048]{1,0:T(8,128)(2,1)}) custom-call(bf16[2048,1024]{1,0:T(8,128)(2,1)} %get-tuple-element.68.refs_0_, bf16[2048,512]{1,0:T(8,128)(2,1)} %all-gather.4.cloned.1.call-done.wg_ref.refs_1_, bf16[2048,512]{1,0:T(8,128)(2,1)} %all-gather.6.cloned.1.call-done.wu_ref.refs_2_, ...), custom_call_target="tpu_custom_call" | custom-call | tf_op jit(solution)/shard_map/hidden_backward/pallas_call | solution.py:481
  398.7 69.9 %attend_backward.1 = (bf16[2048,384]{1,0:T(8,128)(2,1)}, bf16[128,2048]{1,0:T(8,128)(2,1)}, f32[8,128]{1,0:T(8,128)}, bf16[64,8192]{1,0:T(8,128)(2,1)}) custom-call(bf16[128,2048]{1,0:T(8,128)(2,1)} %get-tuple-element.70.refs_0_, f32[2,1,2048]{2,1,0:T(1,128)} %get-tuple-element.71.refs_1_, f32[32,8,128]{2,1,0:T(8,128)} %get-tuple-element.52.ga.refs_2_, ...), custom_call_target="tpu_custom_call" | custom-call | tf_op jit(solution)/shard_map/attend_backward/pallas_call | solution.py:1285
  468.6 0.0 reduce-scatter.6.cloned.1.call-done.gu
  468.6 82.0 %finish_backward.1 = (f32[128,2048]{1,0:T(8,128)}, f32[64,8192]{1,0:T(8,128)}, bf16[64,8192]{1,0:T(8,128)(2,1)}, f32[32,8,128]{2,1,0:T(8,128)}) custom-call(bf16[2048,384]{1,0:T(8,128)(2,1)} %get-tuple-element.78.dq_ref, bf16[2048,384]{1,0:T(8,128)(2,1)} %get-tuple-element.51.wq_ref, bf16[2048,2048]{1,0:T(8,128)(2,1)} %get-tuple-element.50.x_ref, ...), custom_call_target="tpu_custom_call" | custom-call | tf_op jit(solution)/shard_map/finish_backward/pallas_call | solution.py:1469
  550.7 0.9 reduce_sum.9
  551.6 0.5 slice_bitcast_fusion.1
  552.2 3.5 maximum_convert_fusion
  555.7 2.9 convert_element_type.7
  558.6 0.8 copy.24
  559.4 1.0 copy.25
  560.4 1.3 copy.26
  (14 shorter events, 0.1 us)
Async XLA Ops:
  7.2 221.4 %all-gather.4.cloned.1.call-start = ((), (), s32[]{:S(2)}) async-start(), calls=%async_computation.3 | async-start | bytes 3145728 | tf_op jit(solution)/shard_map/all_gather | solution.py:1524
  88.7 139.9 %all-gather.6.cloned.1.call-start = ((), (), s32[]{:S(2)}) async-start(), calls=%async_computation.4 | async-start | bytes 3145728 | tf_op jit(solution)/shard_map/all_gather | solution.py:1524
  133.2 109.8 %all-gather.8.cloned.1.call-start = ((), (), s32[]{:S(2)}) async-start(), calls=%async_computation.5 | async-start | bytes 3145728 | tf_op jit(solution)/shard_map/all_gather | solution.py:1524
  133.9 264.8 %reduce-scatter.4.cloned.1.call-start = ((), (), s32[]{:S(2)}) async-start(), calls=%async_computation.6 | async-start | bytes 3145728 | tf_op jit(solution)/shard_map/reduce_scatter | solution.py:1527
  348.4 120.3 %reduce-scatter.6.cloned.1.call-start = ((), (), s32[]{:S(2)}) async-start(), calls=%async_computation.7 | async-start | bytes 3145728 | tf_op jit(solution)/shard_map/reduce_scatter | solution.py:1527
  349.0 206.7 %reduce-scatter.8.cloned.1.call-start = ((), (), s32[]{:S(2)}) async-start(), calls=%async_computation.8 | async-start | bytes 3145728 | tf_op jit(solution)/shard_map/reduce_scatter | solution.py:1527
  468.6 83.5 %copy-start.2 = (bf16[64,8192]{1,0:T(8,128)(2,1)S(1)}, bf16[64,8192]{1,0:T(8,128)(2,1)}, u32[]{:S(2)}) copy-start(bf16[64,8192]{1,0:T(8,128)(2,1)} %get-tuple-element.87) | copy-start | bytes 3145732
  555.7 2.9 copy-start.3
  555.7 3.7 copy-start.1
  558.6 1.8 copy-start
Sparse Core Ops, SparseCore 0:
  88.8 44.9 all-gather.3
  135.4 44.4 all-gather.5
  181.4 34.1 all-gather.7
  348.5 37.5 reduce-scatter.3
  388.2 48.7 reduce-scatter.5
  439.1 37.5 reduce-scatter.7

commit v5 on v4

--- a/solution.py
+++ b/solution.py
@@ -211,23 +211,27 @@
             wait_bytes(place(bit), near_recv.at[part])
             near(bit, part, 2 + part, other)
             to_core(bit, None, 1 + part)
-        for part in range(2):
+        def from_far(part):
             wait_bytes(place(8, part), far_recv.at[part])
             for bit in (2, 4):
                 near(8, part, 4 + 2 * part + bit // 4, bit)
             to_core(8, part, 5 + part)
-        for bit in (2, 4):
-            wait_bytes(place(1 | bit), core_recv.at[1 + bit // 4])
-            here(bit)
+
+        wait_bytes(place(3), core_recv.at[1])
+        here(2)
+        from_far(0)
+        wait_bytes(place(5), core_recv.at[2])
+        here(4)
         for part in range(2):
             wait_bytes(place(6, part), near_recv.at[2 + part])
             to_core(6, part, 3 + part)
+        from_far(1)
+        for part in range(2):
+            wait_bytes(place(7, part), core_recv.at[3 + part])
+        here(6)
         for part in range(2):
             wait_bytes(place(9, part), core_recv.at[5 + part])
         here(8)
-        for part in range(2):
-            wait_bytes(place(7, part), core_recv.at[3 + part])
-        here(6)
         for part in range(2):
             for bit, other in ORDERS:
                 wait_bytes(place(8 | bit, part), near_recv.at[4 + 2 * part + bit // 4])
@@ -260,7 +264,7 @@
     core_send, core_recv, send_sems, recv_sems, far_send, far_recv = sems
     rows, width = got_far.shape
     tile = 512
-    piece = rows // 4
+    piece = rows // (2 * CHUNKS)
     copies = []
 
     def compute(dst, plane, core, blocks):
@@ -330,7 +334,7 @@
         for part, (bit, other) in enumerate(ORDERS):
             here = pl.ds(start_of(chunk, part), piece)
             for k, keep in enumerate((other, 0)):
-                number = (plane * 2 + chunk) * 6 + part * 2 + k
+                number = (plane * CHUNKS + chunk) * 6 + part * 2 + k
                 buffer = got_first.at[plane, chunk, part * 2 + k]
                 copy = push(
                     mine.at[plane, (keep | bit) // 2, here],
@@ -346,7 +350,7 @@
         started = []
         for part, (bit, other) in enumerate(ORDERS):
             here = pl.ds(start_of(chunk, part), piece)
-            number = (plane * 2 + chunk) * 6 + 4 + part
+            number = (plane * CHUNKS + chunk) * 6 + 4 + part
             buffer = got_second.at[plane, chunk, part]
             copy = push(
                 mine.at[plane, other // 2, here],
@@ -381,26 +385,39 @@
     hook(0)
     add_core(1, core_a)
     add_core(1, core_b)
-    one = [first(1, chunk) for chunk in range(2)]
+    one = [first(1, chunk) if chunk < 2 else None for chunk in range(CHUNKS)]
     compute(theirs, 0, 1, (3, 1, 2, 0))
     core = to_core(0, (3, 1, 2, 0))
+    fars = []
+
+    def advance(chunk):
+        settle(1, one[chunk])
+        one[chunk] = second(1, chunk)
+        if chunk + 2 < CHUNKS:
+            one[chunk + 2] = first(1, chunk + 2)
+
+    def cross(chunk):
+        settle(1, one[chunk])
+        fars.append(far(chunk))
+
+    advance(0)
     compute(mine, 0, 0, (3, 1, 2, 0))
     hook(1)
-    for chunk in range(2):
-        settle(1, one[chunk])
-        one[chunk] = second(1, chunk)
+    advance(1)
     add_core(0, core)
-    zero = [first(0, chunk) for chunk in range(2)]
+    for chunk in range(2, CHUNKS):
+        cross(chunk - 2)
+        advance(chunk)
+    zero = [first(0, chunk) for chunk in range(CHUNKS)]
     hook(2)
-    fars = []
-    for chunk in range(2):
-        settle(1, one[chunk])
-        fars.append(far(chunk))
+    for chunk in range(CHUNKS - 2, CHUNKS):
+        cross(chunk)
     hook(3)
-    for chunk in range(2):
+    for chunk in range(CHUNKS):
         settle(0, zero[chunk])
         zero[chunk] = second(0, chunk)
-    for chunk in range(2):
+    hook(4)
+    for chunk in range(CHUNKS):
         settle(0, zero[chunk])
         fars[chunk].wait_recv()
 
@@ -413,27 +430,43 @@
         copy.wait_send()
 
 
+CHUNKS = 4
+
+
 def scatter_scratch(rows, width):
     block = (rows, width)
-    piece = (rows // 4, width)
+    piece = (rows // (2 * CHUNKS), width)
     return [
         pltpu.VMEM((2, 4) + block, BF),
         pltpu.VMEM((2, 4) + block, BF),
         pltpu.VMEM((2, 4) + block, BF),
-        pltpu.VMEM((2, 2, 4) + piece, BF),
-        pltpu.VMEM((2, 2, 2) + piece, BF),
+        pltpu.VMEM((2, CHUNKS, 4) + piece, BF),
+        pltpu.VMEM((2, CHUNKS, 2) + piece, BF),
         pltpu.VMEM(block, BF),
         DMA((8,)),
         DMA((8,)),
-        DMA((24,)),
-        DMA((24,)),
-        DMA((2,)),
-        DMA((2,)),
+        DMA((12 * CHUNKS,)),
+        DMA((12 * CHUNKS,)),
+        DMA((CHUNKS,)),
+        DMA((CHUNKS,)),
     ]
 
 
 def scatter_call(
-    plan, left, rights, turned, collective_id, name, extras, outs, begin, write, gather=False, moves=None
+    plan,
+    left,
+    rights,
+    turned,
+    collective_id,
+    name,
+    gains,
+    which,
+    extras,
+    outs,
+    begin,
+    write,
+    gather=False,
+    moves=None,
 ):
     rows = left.shape[0] // plan.size
     width = rights[0].shape[0] if turned else rights[0].shape[1]
@@ -449,15 +482,22 @@
             del refs[:number]
             return taken
 
-        sources, more, results = take(1 + count), take(len(extras)), take(len(outs))
+        sources, (gains_ref,), more = take(1 + count), take(1), take(len(extras))
+        results = take(len(outs))
         everyone = take(1) if gather else None
-        held, (sem,) = take(1 + count), take(1)
+        held, (sem, gain_row) = take(1 + count), take(2)
         pieces = [(sources[0], held[0])] + [
             (src.at[pl.ds(first, rows)], dst.at[pl.ds(to, rows)])
             for src, dst in zip(sources[1:], held[1:])
             for first, to, rows in moves
         ]
         loads = Loads(*zip(*pieces), sem)
+        own = width // plan.devices
+        for device in range(plan.devices):
+            gain_row[:, device * own : (device + 1) * own] = gains_ref[
+                device, which : which + 1, :own
+            ]
+        more = [*more, gain_row]
         pairs = [(held[0], i * depth, held[1 + i]) for i in range(count)]
         dp, seq, index = plan.here()
         greet([plan.across(dp, seq, bit) for bit in (1, 2, 4, 8)])
@@ -481,10 +521,10 @@
     return pl.pallas_call(
         kernel,
         out_shape=shapes,
-        in_specs=[ANY] * (1 + count) + [VM] * len(extras),
+        in_specs=[ANY] * (1 + count) + [VM] * (1 + len(extras)),
         out_specs=[VM] * len(outs) + [ANY] * gather,
         scratch_shapes=[like(value) for value in (left, *rights)]
-        + [DMA((1 + count * len(moves),))]
+        + [DMA((1 + count * len(moves),)), pltpu.VMEM((1, width), F32)]
         + scatter_scratch(rows, width)
         + list(GATHER_SEMS) * gather,
         compiler_params=pltpu.CompilerParams(
@@ -492,7 +532,7 @@
         ),
         cost_estimate=LIGHT,
         name=name,
-    )(left, *rights, *extras)
+    )(left, *rights, gains, *extras)
 
 
 def rms(values):
@@ -507,7 +547,7 @@
     return back, jnp.sum(grad * values * r, axis=0, keepdims=True)
 
 
-def hidden_forward(plan, mixed, w_out, x, gain):
+def hidden_forward(plan, mixed, w_out, x, gains):
     def write(here, value, extras, outs):
         x_ref, g = extras
         branch, hidden, low = outs
@@ -524,7 +564,9 @@
         False,
         2,
         "hidden_forward",
-        (x, gain),
+        gains,
+        2,
+        (x,),
         outs,
         lambda outs: None,
         write,
@@ -532,7 +574,7 @@
     )
 
 
-def output_norm(plan, act, w_down, hidden, grad_out, gain):
+def output_norm(plan, act, w_down, hidden, grad_out, gains):
     def begin(outs):
         outs[2][...] = jnp.zeros_like(outs[2])
 
@@ -544,13 +586,24 @@
         back[here, :] = grad.astype(BF)
         g_gain[...] += part
 
-    outs = ((hidden.shape, BF), (hidden.shape, BF), (gain.shape, F32))
+    outs = ((hidden.shape, BF), (hidden.shape, BF), ((1, hidden.shape[1]), F32))
     return scatter_call(
-        plan, act, [w_down], False, 6, "output_norm", (hidden, grad_out, gain), outs, begin, write
+        plan,
+        act,
+        [w_down],
+        False,
+        6,
+        "output_norm",
+        gains,
+        3,
+        (hidden, grad_out),
+        outs,
+        begin,
+        write,
     )
 
 
-def hidden_backward(plan, g_low, rights, grad_out, branch, gain):
+def hidden_backward(plan, g_low, rights, grad_out, branch, gains):
     def begin(outs):
         outs[1][...] = jnp.zeros_like(outs[1])
 
@@ -563,7 +616,7 @@
         low[here, :] = back.astype(BF)
         g_gain[...] += part
 
-    outs = ((branch.shape, F32), (gain.shape, F32), (branch.shape, BF))
+    outs = ((branch.shape, F32), ((1, branch.shape[1]), F32), (branch.shape, BF))
     return scatter_call(
         plan,
         g_low,
@@ -571,7 +624,9 @@
         True,
         7,
         "hidden_backward",
-        (grad_out, branch, gain),
+        gains,
+        2,
+        (grad_out, branch),
         outs,
         begin,
         write,
@@ -1415,8 +1470,6 @@
                 ours()
             elif i == 2:
                 lax.fori_loop(0, pieces, o_to, 0)
-            else:
-                collect()
                 ga[...] = jnp.zeros_like(ga)
                 for other in range(plan.devices):
                     part = slice(other * own, (other + 1) * own)
@@ -1427,6 +1480,8 @@
                     ga[plan.head(index) * pieces + piece, 0:2, :own] = gh[0:2, part]
                 lax.fori_loop(1, plan.devices, ga_to, 0)
                 pltpu.make_async_copy(ga.at[me], ga_out.at[me], ga_r).start()
+            elif i == 3:
+                collect()
 
         def write(here, value):
             ig[here, :] = bf[here, :] + value
@@ -1538,7 +1593,6 @@
         blocks,
     )
     w_gate = join_groups(gate_part)
-    gains = jnp.transpose(gains_all[:, 2:4, :own], (1, 0, 2)).reshape(2, width)
     positions = np.arange(length, dtype=np.float32)
     frequency = rope_base ** (-2.0 * np.arange(HEAD // 2, dtype=np.float32) / HEAD)
     angles = positions[:, None] * frequency.astype(np.float32)[None, :]
@@ -1564,12 +1618,12 @@
         w_all = lax.all_gather(down_weights, ("dp", "seq"), axis=0, tiled=True)
         each = inner // plan.size
         w_down = lax.dynamic_slice_in_dim(w_all, index * each, each, 0)
-    branch, hidden, _, h_all = hidden_forward(plan, mixed, w_out, x, gains[:1])
+    branch, hidden, _, h_all = hidden_forward(plan, mixed, w_out, x, gains_all)
     branch, w_gate = lax.optimization_barrier((branch, w_gate))
 
     gate, up, act = ffn_forward(plan, h_all, w_gate, w_up)
     output, grad_down_in, grad_fg = output_norm(
-        plan, act, w_down, hidden, cotangent[0], gains[1:]
+        plan, act, w_down, hidden, cotangent[0], gains_all
     )
 
     gu_low, g_gate, g_up, g_down = ffn_backward(
@@ -1587,7 +1641,7 @@
         ).astype(F32)
 
     grad_hidden, grad_ag, grad_branch = hidden_backward(
-        plan, gu_low, [w_gate, w_up], cotangent[0], branch, gains[:1]
+        plan, gu_low, [w_gate, w_up], cotangent[0], branch, gains_all
     )
     dqkv, g_out, g_head, gate_rows = attend_backward(
         plan,

time: 575 us -> 561 us (0.976)
  Pallas kernels: 538 us -> 529 us
    pallas_call x3, Pallas kernels: 190 us -> 181 us  [scatter_call(): pl.pallas_call(kernel, out_shape=shapes, in_specs=[ANY] * (1 + count) + [...]
where the time goes in v5:
time: 561 us; the launch traced here: 557 us
  Pallas kernels  529 us (94%)
  between operations  14.4 us (3%)
  other arithmetic  7.36 us (1%)
    pallas_call x3, Pallas kernels, scatter_call(): pl.pallas_call(kernel, out_shape=shapes, in_specs=[ANY] * (1 + count) + [...  181 us
    pallas_call x1, Pallas kernels, finish_backward(): pl.pallas_call(kernel, out_shape=[jax.ShapeDtypeStruct(*shape) for shape...  84.2 us
    pallas_call x1, Pallas kernels, start_gather(): pl.pallas_call(kernel, out_shape=[jax.ShapeDtypeStruct(*shape) for shape...  81.5 us
    pallas_call x1, Pallas kernels, attend_backward(): pl.pallas_call(kernel, out_shape=[jax.ShapeDtypeStruct(*shape) for shape...  65.2 us
    pallas_call x1, Pallas kernels, ffn_backward(): pl.pallas_call(kernel, out_shape=[jax.ShapeDtypeStruct((tokens, 2 * units...  58.3 us
    pallas_call x1, Pallas kernels, attend_forward(): pl.pallas_call(kernel, out_shape=[jax.ShapeDtypeStruct(*shape) for shape...  44.5 us
    pallas_call x1, Pallas kernels, ffn_forward(): pl.pallas_call(kernel, grid=(tokens // rows,), out_shape=[jax.ShapeDtypeS...  14.4 us
  transfers between devices with their start and end apart: 6, of which 0 were waited for; matrix products, arithmetic and copies ran while one was open for 1% of the time, Pallas kernels for 62%

profile of v5, /device:TPU:15, one launch (start us, length us, event | category | flops | bytes accessed | tf_op | source)
XLA Modules:
  0.0 556.8 jit_solution(16253473575528449655)
XLA Ops:
  7.2 0.0 all-gather.4.cloned.1.call-start
  7.2 81.5 %start_gather.1 = (bf16[2048,2048]{1,0:T(8,128)(2,1)}, bf16[2048,384]{1,0:T(8,128)(2,1)}, bf16[1024,512]{1,0:T(8,128)(2,1)}, bf16[128,2048]{1,0:T(8,128)(2,1)}, ...) custom-call(bf16[128,2048]{1,0:T(8,128)(2,1)} %bitcast.18, bf16[64,8192]{1,0:T(8,128)(2,1)} %w_ref.1, bf16[64,16384]{1,0:T(8,128)(2,1)} %up.1, ...), custom_call_target="tpu_custom_call" | custom-call | tf_op jit(solution)/shard_map/start_gather/pallas_call | solution.py:865
  88.7 0.0 all-gather.4.cloned.1.call-update
  88.7 0.0 all-gather.6.cloned.1.call-start
  88.8 44.5 %attend_forward.1 = (bf16[1024,512]{1,0:T(8,128)(2,1)}, f32[2048,128]{1,0:T(8,128)}, f32[2048,128]{1,0:T(8,128)}, f32[2,1,2048]{2,1,0:T(1,128)}, bf16[2048,128]{...) custom-call(bf16[2048,2048]{1,0:T(8,128)(2,1)} %get-tuple-element.50.x_ref, ...), custom_call_target="tpu_custom_call" | custom-call | tf_op jit(solution)/shard_map/attend_forward/pallas_call | solution.py:1198
  133.2 0.0 all-gather.6.cloned.1.call-update
  133.3 0.0 all-gather.8.cloned.1.call-start
  133.3 0.7 all-gather.8.cloned.1.call-update
  134.0 0.6 reduce-scatter.4.cloned.1.call-start
  134.6 84.1 %hidden_forward.1 = (f32[128,2048]{1,0:T(8,128)}, f32[128,2048]{1,0:T(8,128)}, bf16[128,2048]{1,0:T(8,128)(2,1)}, bf16[2048,2048]{1,0:T(8,128)(2,1)}) custom-call(bf16[2048,128]{1,0:T(8,128)(2,1)} %get-tuple-element.54.refs_0_.refs_11_, bf16[128,2048]{1,0:T(8,128)(2,1)} %get-tuple-element.55.refs_1_.refs_5_, ...), custom_call_target="tpu_custom_call" | custom-call | tf_op jit(solution)/shard_map/hidden_forward/pallas_call | solution.py:521
  218.7 0.0 all-gather.4.cloned.1.call-done.wg_ref.refs_1_
  218.7 0.0 all-gather.6.cloned.1.call-done.wu_ref.refs_2_
  218.7 14.4 %ffn_forward.1 = (bf16[2048,512]{1,0:T(8,128)(2,1)}, bf16[2048,512]{1,0:T(8,128)(2,1)}, bf16[2048,512]{1,0:T(8,128)(2,1)}) custom-call(bf16[2048,2048]{1,0:T(8,128)(2,1)} %get-tuple-element.56.h.refs_4_, bf16[2048,512]{1,0:T(8,128)(2,1)} %all-gather.4.cloned.1.call-done.wg_ref.refs_1_, bf16[2048,512]{1,0:T(8,128)(2,1)} %all-gather.6.cloned.1.call-done.wu_ref.refs_2_), custom_call_target="tpu_custom_call" | custom-call | tf_op jit(solution)/shard_map/ffn_forward/pallas_call | solution.py:920
  233.1 0.0 all-gather.8.cloned.1.call-done.refs_1_.refs_0_
  233.2 45.3 %output_norm.1 = (bf16[128,2048]{1,0:T(8,128)(2,1)}, bf16[128,2048]{1,0:T(8,128)(2,1)}, f32[1,2048]{1,0:T(1,128)}) custom-call(bf16[2048,512]{1,0:T(8,128)(2,1)} %get-tuple-element.61.refs_0_.refs_3_, bf16[512,2048]{1,0:T(8,128)(2,1)} %all-gather.8.cloned.1.call-done.refs_1_.refs_0_, f32[32,8,128]{2,1,0:T(8,128)} %get-tuple-element.52.ga.refs_2_.refs_3_, ...), custom_call_target="tpu_custom_call" | custom-call | tf_op jit(solution)/shard_map/output_norm/pallas_call | solution.py:521
  278.4 58.3 %ffn_backward.1 = (bf16[2048,1024]{1,0:T(8,128)(2,1)}, bf16[2048,512]{1,0:T(8,128)(2,1)}, bf16[2048,512]{1,0:T(8,128)(2,1)}, bf16[512,2048]{1,0:T(8,128)(2,1)}) custom-call(bf16[128,2048]{1,0:T(8,128)(2,1)} %get-tuple-element.65.d_ref, bf16[512,2048]{1,0:T(8,128)(2,1)} %all-gather.8.cloned.1.call-done.refs_1_.refs_0_, ...), custom_call_target="tpu_custom_call" | custom-call | tf_op jit(solution)/shard_map/ffn_backward/pallas_call | solution.py:1022
  336.8 0.0 reduce-scatter.6.cloned.1.call-start
  336.8 0.5 reduce-scatter.6.cloned.1.call-update
  337.4 0.0 reduce-scatter.8.cloned.1.call-start
  337.4 0.5 reduce-scatter.8.cloned.1.call-update
  338.0 51.3 %hidden_backward.1 = (f32[128,2048]{1,0:T(8,128)}, f32[1,2048]{1,0:T(1,128)}, bf16[128,2048]{1,0:T(8,128)(2,1)}) custom-call(bf16[2048,1024]{1,0:T(8,128)(2,1)} %get-tuple-element.68.refs_0_, bf16[2048,512]{1,0:T(8,128)(2,1)} %all-gather.4.cloned.1.call-done.wg_ref.refs_1_, bf16[2048,512]{1,0:T(8,128)(2,1)} %all-gather.6.cloned.1.call-done.wu_ref.refs_2_, ...), custom_call_target="tpu_custom_call" | custom-call | tf_op jit(solution)/shard_map/hidden_backward/pallas_call | solution.py:521
  389.3 0.0 reduce-scatter.4.cloned.1.call-done.refs_4_
  389.3 65.2 %attend_backward.1 = (bf16[2048,384]{1,0:T(8,128)(2,1)}, bf16[128,2048]{1,0:T(8,128)(2,1)}, f32[8,128]{1,0:T(8,128)}, bf16[64,8192]{1,0:T(8,128)(2,1)}) custom-call(bf16[128,2048]{1,0:T(8,128)(2,1)} %get-tuple-element.70.refs_0_, f32[2,1,2048]{2,1,0:T(1,128)} %get-tuple-element.71.refs_1_, f32[32,8,128]{2,1,0:T(8,128)} %get-tuple-element.52.ga.refs_2_.refs_3_, ...), custom_call_target="tpu_custom_call" | custom-call | tf_op jit(solution)/shard_map/attend_backward/pallas_call | solution.py:1340
  454.5 0.0 reduce-scatter.6.cloned.1.call-done.gu
  454.5 84.2 %finish_backward.1 = (f32[128,2048]{1,0:T(8,128)}, f32[64,8192]{1,0:T(8,128)}, bf16[64,8192]{1,0:T(8,128)(2,1)}, f32[32,8,128]{2,1,0:T(8,128)}) custom-call(bf16[2048,384]{1,0:T(8,128)(2,1)} %get-tuple-element.78.dq_ref, bf16[2048,384]{1,0:T(8,128)(2,1)} %get-tuple-element.51.wq_ref, bf16[2048,2048]{1,0:T(8,128)(2,1)} %get-tuple-element.50.x_ref, ...), custom_call_target="tpu_custom_call" | custom-call | tf_op jit(solution)/shard_map/finish_backward/pallas_call | solution.py:1524
  538.8 0.9 reduce_sum.9
  539.7 0.5 slice_bitcast_fusion
  540.3 3.5 maximum_convert_fusion
  543.8 2.9 convert_element_type.7
  546.7 0.8 copy.24
  547.5 1.0 copy.25
  548.5 1.3 copy.26
  (10 shorter events, 0.0 us)
Async XLA Ops:
  7.2 211.5 %all-gather.4.cloned.1.call-start = ((), (), s32[]{:S(2)}) async-start(), calls=%async_computation.3 | async-start | bytes 3145728 | tf_op jit(solution)/shard_map/all_gather | solution.py:1579
  88.7 130.0 %all-gather.6.cloned.1.call-start = ((), (), s32[]{:S(2)}) async-start(), calls=%async_computation.4 | async-start | bytes 3145728 | tf_op jit(solution)/shard_map/all_gather | solution.py:1579
  133.3 99.9 %all-gather.8.cloned.1.call-start = ((), (), s32[]{:S(2)}) async-start(), calls=%async_computation.5 | async-start | bytes 3145728 | tf_op jit(solution)/shard_map/all_gather | solution.py:1579
  134.0 255.3 %reduce-scatter.4.cloned.1.call-start = ((), (), s32[]{:S(2)}) async-start(), calls=%async_computation.6 | async-start | bytes 3145728 | tf_op jit(solution)/shard_map/reduce_scatter | solution.py:1582
  336.8 117.7 %reduce-scatter.6.cloned.1.call-start = ((), (), s32[]{:S(2)}) async-start(), calls=%async_computation.7 | async-start | bytes 3145728 | tf_op jit(solution)/shard_map/reduce_scatter | solution.py:1582
  337.4 206.4 %reduce-scatter.8.cloned.1.call-start = ((), (), s32[]{:S(2)}) async-start(), calls=%async_computation.8 | async-start | bytes 3145728 | tf_op jit(solution)/shard_map/reduce_scatter | solution.py:1582
  454.5 85.7 %copy-start.2 = (bf16[64,8192]{1,0:T(8,128)(2,1)S(1)}, bf16[64,8192]{1,0:T(8,128)(2,1)}, u32[]{:S(2)}) copy-start(bf16[64,8192]{1,0:T(8,128)(2,1)} %get-tuple-element.87) | copy-start | bytes 3145732
  543.8 2.9 copy-start.3
  543.8 3.7 copy-start.1
  546.7 1.8 copy-start
Sparse Core Ops, SparseCore 0:
  88.8 44.8 all-gather.3
  135.3 51.4 all-gather.5
  188.3 35.4 all-gather.7
  336.9 35.7 reduce-scatter.3
  374.8 46.1 reduce-scatter.5
  423.2 36.6 reduce-scatter.7

commit v6 on v5

--- a/solution.py
+++ b/solution.py
@@ -1313,20 +1313,27 @@
             g_out[:, columns] = dot(turned_mixed, ba[:, columns]).astype(BF)
 
         g_gain[...] = jnp.zeros_like(g_gain)
-        finish()
 
         @pl.loop(0, tokens // STEP)
         def _(i):
             rows = pl.ds(pl.multiple_of(i * STEP, STEP), STEP)
             for which, raw, grad in ((0, q, dq), (1, k, dk)):
-                total = spread_sums(held[:, which, 0, rows])
                 r = lax.rsqrt(spread_sums(sums[which, :, rows]) / width + epsilon)
                 u = raw[rows, :]
                 e = grad[rows, :]
-                back = r * (gn[which : which + 1, :] * e) - u * (r * r * r * (total / width))
+                g_gain[which : which + 1, :] += jnp.sum(e * u * r, axis=0, keepdims=True)
+                grad[rows, :] = r * (gn[which : which + 1, :] * e)
+                raw[rows, :] = u * (r * r * r) / width
+            dqkv[rows, pl.ds(2 * HEAD, HEAD)] = dv[rows, :].astype(BF)
+
+        finish()
+
+        @pl.loop(0, tokens // STEP)
+        def _(i):
+            rows = pl.ds(pl.multiple_of(i * STEP, STEP), STEP)
+            for which, raw, grad in ((0, q, dq), (1, k, dk)):
+                back = grad[rows, :] - raw[rows, :] * spread_sums(held[:, which, 0, rows])
                 dqkv[rows, pl.ds(which * HEAD, HEAD)] = back.astype(BF)
-                g_gain[which : which + 1, :] += jnp.sum(e * u * r, axis=0, keepdims=True)
-            dqkv[rows, pl.ds(2 * HEAD, HEAD)] = dv[rows, :].astype(BF)
 
         finish_g()
 

time: 561 us -> 559 us (level)
  no operation moved by 1% of the time
where the time goes in v6:
time: 559 us; the launch traced here: 555 us
  Pallas kernels  527 us (94%)
  between operations  14.4 us (3%)
  other arithmetic  7.36 us (1%)
    pallas_call x3, Pallas kernels, scatter_call(): pl.pallas_call(kernel, out_shape=shapes, in_specs=[ANY] * (1 + count) + [...  181 us
    pallas_call x1, Pallas kernels, finish_backward(): pl.pallas_call(kernel, out_shape=[jax.ShapeDtypeStruct(*shape) for shape...  84.3 us
    pallas_call x1, Pallas kernels, start_gather(): pl.pallas_call(kernel, out_shape=[jax.ShapeDtypeStruct(*shape) for shape...  81.5 us
    pallas_call x1, Pallas kernels, attend_backward(): pl.pallas_call(kernel, out_shape=[jax.ShapeDtypeStruct(*shape) for shape...  63.2 us
    pallas_call x1, Pallas kernels, ffn_backward(): pl.pallas_call(kernel, out_shape=[jax.ShapeDtypeStruct((tokens, 2 * units...  58.3 us
    pallas_call x1, Pallas kernels, attend_forward(): pl.pallas_call(kernel, out_shape=[jax.ShapeDtypeStruct(*shape) for shape...  44.5 us
    pallas_call x1, Pallas kernels, ffn_forward(): pl.pallas_call(kernel, grid=(tokens // rows,), out_shape=[jax.ShapeDtypeS...  14.4 us
  transfers between devices with their start and end apart: 6, of which 0 were waited for; matrix products, arithmetic and copies ran while one was open for 1% of the time, Pallas kernels for 62%

profile of v6, /device:TPU:15, one launch (start us, length us, event | category | flops | bytes accessed | tf_op | source)
XLA Modules:
  0.0 554.8 jit_solution(12772976198829676478)
XLA Ops:
  7.2 0.0 all-gather.4.cloned.1.call-start
  7.2 81.5 %start_gather.1 = (bf16[2048,2048]{1,0:T(8,128)(2,1)}, bf16[2048,384]{1,0:T(8,128)(2,1)}, bf16[1024,512]{1,0:T(8,128)(2,1)}, bf16[128,2048]{1,0:T(8,128)(2,1)}, ...) custom-call(bf16[128,2048]{1,0:T(8,128)(2,1)} %bitcast.18, bf16[64,8192]{1,0:T(8,128)(2,1)} %w_ref.1, bf16[64,16384]{1,0:T(8,128)(2,1)} %up.1, ...), custom_call_target="tpu_custom_call" | custom-call | tf_op jit(solution)/shard_map/start_gather/pallas_call | solution.py:865
  88.7 0.0 all-gather.4.cloned.1.call-update
  88.7 0.0 all-gather.6.cloned.1.call-start
  88.8 44.5 %attend_forward.1 = (bf16[1024,512]{1,0:T(8,128)(2,1)}, f32[2048,128]{1,0:T(8,128)}, f32[2048,128]{1,0:T(8,128)}, f32[2,1,2048]{2,1,0:T(1,128)}, bf16[2048,128]{...) custom-call(bf16[2048,2048]{1,0:T(8,128)(2,1)} %get-tuple-element.50.x_ref, ...), custom_call_target="tpu_custom_call" | custom-call | tf_op jit(solution)/shard_map/attend_forward/pallas_call | solution.py:1198
  133.2 0.0 all-gather.6.cloned.1.call-update
  133.3 0.0 all-gather.8.cloned.1.call-start
  133.3 0.7 all-gather.8.cloned.1.call-update
  134.0 0.6 reduce-scatter.4.cloned.1.call-start
  134.6 84.1 %hidden_forward.1 = (f32[128,2048]{1,0:T(8,128)}, f32[128,2048]{1,0:T(8,128)}, bf16[128,2048]{1,0:T(8,128)(2,1)}, bf16[2048,2048]{1,0:T(8,128)(2,1)}) custom-call(bf16[2048,128]{1,0:T(8,128)(2,1)} %get-tuple-element.54.refs_0_.refs_11_, bf16[128,2048]{1,0:T(8,128)(2,1)} %get-tuple-element.55.refs_1_.refs_5_, ...), custom_call_target="tpu_custom_call" | custom-call | tf_op jit(solution)/shard_map/hidden_forward/pallas_call | solution.py:521
  218.7 0.0 all-gather.4.cloned.1.call-done.wg_ref.refs_1_
  218.7 0.0 all-gather.6.cloned.1.call-done.wu_ref.refs_2_
  218.7 14.4 %ffn_forward.1 = (bf16[2048,512]{1,0:T(8,128)(2,1)}, bf16[2048,512]{1,0:T(8,128)(2,1)}, bf16[2048,512]{1,0:T(8,128)(2,1)}) custom-call(bf16[2048,2048]{1,0:T(8,128)(2,1)} %get-tuple-element.56.h.refs_4_, bf16[2048,512]{1,0:T(8,128)(2,1)} %all-gather.4.cloned.1.call-done.wg_ref.refs_1_, bf16[2048,512]{1,0:T(8,128)(2,1)} %all-gather.6.cloned.1.call-done.wu_ref.refs_2_), custom_call_target="tpu_custom_call" | custom-call | tf_op jit(solution)/shard_map/ffn_forward/pallas_call | solution.py:920
  233.1 0.0 all-gather.8.cloned.1.call-done.refs_1_.refs_0_
  233.2 45.3 %output_norm.1 = (bf16[128,2048]{1,0:T(8,128)(2,1)}, bf16[128,2048]{1,0:T(8,128)(2,1)}, f32[1,2048]{1,0:T(1,128)}) custom-call(bf16[2048,512]{1,0:T(8,128)(2,1)} %get-tuple-element.61.refs_0_.refs_3_, bf16[512,2048]{1,0:T(8,128)(2,1)} %all-gather.8.cloned.1.call-done.refs_1_.refs_0_, f32[32,8,128]{2,1,0:T(8,128)} %get-tuple-element.52.ga.refs_2_.refs_3_, ...), custom_call_target="tpu_custom_call" | custom-call | tf_op jit(solution)/shard_map/output_norm/pallas_call | solution.py:521
  278.4 58.3 %ffn_backward.1 = (bf16[2048,1024]{1,0:T(8,128)(2,1)}, bf16[2048,512]{1,0:T(8,128)(2,1)}, bf16[2048,512]{1,0:T(8,128)(2,1)}, bf16[512,2048]{1,0:T(8,128)(2,1)}) custom-call(bf16[128,2048]{1,0:T(8,128)(2,1)} %get-tuple-element.65.d_ref, bf16[512,2048]{1,0:T(8,128)(2,1)} %all-gather.8.cloned.1.call-done.refs_1_.refs_0_, ...), custom_call_target="tpu_custom_call" | custom-call | tf_op jit(solution)/shard_map/ffn_backward/pallas_call | solution.py:1022
  336.8 0.0 reduce-scatter.6.cloned.1.call-start
  336.8 0.5 reduce-scatter.6.cloned.1.call-update
  337.4 0.0 reduce-scatter.8.cloned.1.call-start
  337.4 0.5 reduce-scatter.8.cloned.1.call-update
  338.0 51.3 %hidden_backward.1 = (f32[128,2048]{1,0:T(8,128)}, f32[1,2048]{1,0:T(1,128)}, bf16[128,2048]{1,0:T(8,128)(2,1)}) custom-call(bf16[2048,1024]{1,0:T(8,128)(2,1)} %get-tuple-element.68.refs_0_, bf16[2048,512]{1,0:T(8,128)(2,1)} %all-gather.4.cloned.1.call-done.wg_ref.refs_1_, bf16[2048,512]{1,0:T(8,128)(2,1)} %all-gather.6.cloned.1.call-done.wu_ref.refs_2_, ...), custom_call_target="tpu_custom_call" | custom-call | tf_op jit(solution)/shard_map/hidden_backward/pallas_call | solution.py:521
  389.3 0.0 reduce-scatter.4.cloned.1.call-done.refs_4_
  389.3 63.2 %attend_backward.1 = (bf16[2048,384]{1,0:T(8,128)(2,1)}, bf16[128,2048]{1,0:T(8,128)(2,1)}, f32[8,128]{1,0:T(8,128)}, bf16[64,8192]{1,0:T(8,128)(2,1)}) custom-call(bf16[128,2048]{1,0:T(8,128)(2,1)} %get-tuple-element.70.refs_0_, f32[2,1,2048]{2,1,0:T(1,128)} %get-tuple-element.71.refs_1_, f32[32,8,128]{2,1,0:T(8,128)} %get-tuple-element.52.ga.refs_2_.refs_3_, ...), custom_call_target="tpu_custom_call" | custom-call | tf_op jit(solution)/shard_map/attend_backward/pallas_call | solution.py:1347
  452.5 0.0 reduce-scatter.6.cloned.1.call-done.gu
  452.5 84.3 %finish_backward.1 = (f32[128,2048]{1,0:T(8,128)}, f32[64,8192]{1,0:T(8,128)}, bf16[64,8192]{1,0:T(8,128)(2,1)}, f32[32,8,128]{2,1,0:T(8,128)}) custom-call(bf16[2048,384]{1,0:T(8,128)(2,1)} %get-tuple-element.78.dq_ref, bf16[2048,384]{1,0:T(8,128)(2,1)} %get-tuple-element.51.wq_ref, bf16[2048,2048]{1,0:T(8,128)(2,1)} %get-tuple-element.50.x_ref, ...), custom_call_target="tpu_custom_call" | custom-call | tf_op jit(solution)/shard_map/finish_backward/pallas_call | solution.py:1531
  536.8 0.9 reduce_sum.9
  537.8 0.5 slice_bitcast_fusion
  538.3 3.5 maximum_convert_fusion
  541.8 2.9 convert_element_type.7
  544.7 0.8 copy.24
  545.5 1.0 copy.25
  546.5 1.3 copy.26
  (10 shorter events, 0.0 us)
Async XLA Ops:
  7.2 211.5 %all-gather.4.cloned.1.call-start = ((), (), s32[]{:S(2)}) async-start(), calls=%async_computation.3 | async-start | bytes 3145728 | tf_op jit(solution)/shard_map/all_gather | solution.py:1586
  88.7 130.0 %all-gather.6.cloned.1.call-start = ((), (), s32[]{:S(2)}) async-start(), calls=%async_computation.4 | async-start | bytes 3145728 | tf_op jit(solution)/shard_map/all_gather | solution.py:1586
  133.3 99.9 %all-gather.8.cloned.1.call-start = ((), (), s32[]{:S(2)}) async-start(), calls=%async_computation.5 | async-start | bytes 3145728 | tf_op jit(solution)/shard_map/all_gather | solution.py:1586
  134.0 255.3 %reduce-scatter.4.cloned.1.call-start = ((), (), s32[]{:S(2)}) async-start(), calls=%async_computation.6 | async-start | bytes 3145728 | tf_op jit(solution)/shard_map/reduce_scatter | solution.py:1589
  336.8 115.7 %reduce-scatter.6.cloned.1.call-start = ((), (), s32[]{:S(2)}) async-start(), calls=%async_computation.7 | async-start | bytes 3145728 | tf_op jit(solution)/shard_map/reduce_scatter | solution.py:1589
  337.4 204.4 %reduce-scatter.8.cloned.1.call-start = ((), (), s32[]{:S(2)}) async-start(), calls=%async_computation.8 | async-start | bytes 3145728 | tf_op jit(solution)/shard_map/reduce_scatter | solution.py:1589
  452.5 85.8 %copy-start.2 = (bf16[64,8192]{1,0:T(8,128)(2,1)S(1)}, bf16[64,8192]{1,0:T(8,128)(2,1)}, u32[]{:S(2)}) copy-start(bf16[64,8192]{1,0:T(8,128)(2,1)} %get-tuple-element.87) | copy-start | bytes 3145732
  541.8 2.9 copy-start.3
  541.8 3.7 copy-start.1
  544.7 1.8 copy-start
Sparse Core Ops, SparseCore 0:
  88.8 44.8 all-gather.3
  135.3 51.4 all-gather.5
  188.3 35.4 all-gather.7
  336.9 35.7 reduce-scatter.3
  374.8 46.1 reduce-scatter.5
  423.2 36.6 reduce-scatter.7
